TPU v7x, 128 devices: a whole 4x4x4 slice. The times are simulated.
128 devices in a mesh: dp: 16 (over y, z_hi, core), seq: 8 (over x, z_lo).
Axes of the slice: x: 4, y: 4, z: 4 (z_hi: 2, z_lo: 2; z = z_hi * 2 + z_lo), core: 2. Of those that a mesh axis runs over, the one named last changes fastest.
Arguments:
- inputs: bfloat16 [16, 1024, 1024], P('dp', 'seq'), may hold values from -6 to 6
- cotangent: bfloat16 [16, 1024, 1024], P('dp', 'seq'), may hold values from -6 to 6
- mixer_in: bfloat16 [1, 1024, 3352], P(None, 'seq'), may hold values from -0.1875 to 0.1875
- attn_in: bfloat16 [1, 1024, 768], P(None, 'seq'), may hold values from -0.1875 to 0.1875
- mamba_out: bfloat16 [1, 1536, 1024], P(None, 'seq'), may hold values from -0.15625 to 0.15625
- attn_out: bfloat16 [1, 512, 1024], P(None, 'seq'), may hold values from -1 to 1
- gate_up: bfloat16 [1, 1024, 4096], P(None, 'seq'), may hold values from -0.1875 to 0.1875
- down_proj: bfloat16 [1, 2048, 1024], P(None, 'seq'), may hold values from -0.125 to 0.125
- norm_gains: bfloat16 [1, 2, 1024], P(None, None, 'seq'), may hold values from 0.5 to 1.5
- step_bias: bfloat16 [1, 24], P(None, 'seq'), may hold values from -6 to -3
- decay_log: bfloat16 [1, 24], P(None, 'seq'), may hold values from 0 to 2.5
- skip_gain: bfloat16 [1, 24], P(None, 'seq'), may hold values from 0.5 to 1.5
Outputs:
- outputs: bfloat16 [16, 1024, 1024], P('dp', 'seq')
- input_grad: float32 [16, 1024, 1024], P('dp', 'seq')
- mixer_in_grad: float32 [1, 1024, 3352], P(None, 'seq')
- attn_in_grad: float32 [1, 1024, 768], P(None, 'seq')
- mamba_out_grad: float32 [1, 1536, 1024], P(None, 'seq')
- attn_out_grad: float32 [1, 512, 1024], P(None, 'seq')
- gate_up_grad: float32 [1, 1024, 4096], P(None, 'seq')
- down_proj_grad: float32 [1, 2048, 1024], P(None, 'seq')
- norm_gains_grad: float32 [1, 2, 1024], P(None, None, 'seq')
- step_bias_grad: float32 [1, 24], P(None, 'seq')
- decay_log_grad: float32 [1, 24], P(None, 'seq')
- skip_gain_grad: float32 [1, 24], P(None, 'seq')
All inputs are finite; a program needn't handle non-finite values.
Results may differ from a plain program's by a relative error of at most 0.03.
Values may be sent and summed in bfloat16 or wider, within the bound.
No kernel may reach another device: no remote copies, remote signals or barrier semaphores. Data moves between devices by JAX's collectives and lax.ppermute only.
A program may use at most 192 MiB of HBM per device.

v0:
```python
import jax
import jax.numpy as jnp
from jax import lax
from jax.sharding import PartitionSpec as P

QUERY_HEADS = 8
KEY_VALUE_HEADS = 2
HEAD_SIZE = 64
MH = 24
MP = 64
NS = 128
LAYERS = 1
SPAN = 64


highest = lax.Precision.HIGHEST
norm_epsilon = 1e-05
masked_score = -1e30


def entering_2(part, axis, combine, identity):
    place = lax.axis_index(axis)
    gathered = jax.tree.map(lambda a: lax.all_gather(a, axis), part)
    state = jax.tree.map(lambda a, e: jnp.zeros_like(a) + jnp.asarray(e, a.dtype), part, identity)

    def entering_one(hop, state):
        return combine(
            state, jax.tree.map(lambda a: lax.dynamic_index_in_dim(a, hop, 0, False), gathered)
        )

    return lax.fori_loop(0, place, entering_one, state)


def prefix(shard, axis, join, neutral):
    count = lax.axis_size(axis)
    place = lax.axis_index(axis)
    ahead = count - 1 - place
    gathered = jax.tree.map(
        lambda a, kind: lax.all_gather(a.astype(kind), axis), shard, (jnp.bfloat16, jnp.bfloat16)
    )
    state = jax.tree.map(lambda a, e: jnp.zeros_like(a) + jnp.asarray(e, a.dtype), shard, neutral)

    def prefix_one(hop, state):
        source = count - 1 - hop
        return join(
            state,
            jax.tree.map(
                lambda a, own: lax.dynamic_index_in_dim(a, source, 0, False).astype(own.dtype),
                gathered,
                shard,
            ),
        )

    return lax.fori_loop(0, ahead, prefix_one, state)


def sent_together(arrays, axis, dim, along):
    both = jnp.concatenate(arrays, axis=along)
    out, at, outs = (lax.all_gather(both, axis, axis=dim, tiled=True), 0, [])
    for a in arrays:
        outs.append(lax.slice_in_dim(out, at, at + a.shape[along], axis=along))
        at += a.shape[along]
    return tuple(outs)


def cut_along(shard, dim, peers):
    before, after = (shard.shape[:dim], shard.shape[dim + 1 :])
    return jnp.moveaxis(shard.reshape(*before, peers, -1, *after), dim, 0)


def summed_on_arrival(shard, axis, dim):
    parts = cut_along(shard, dim, lax.axis_size(axis))
    arrived = lax.all_to_all(parts, axis, split_axis=0, concat_axis=0, tiled=True)
    return arrived.sum(axis=0)


def together(arrays, axis):
    ends = [0]
    for a in arrays:
        ends.append(ends[-1] + a.size)
    so_far = lax.psum(jnp.concatenate([a.ravel() for a in arrays]), axis)
    return tuple((so_far[b:e].reshape(a.shape) for a, b, e in zip(arrays, ends, ends[1:])))


def sigmoid_linear(value_rows):
    return value_rows * jax.nn.sigmoid(value_rows)


def norm_rows(value_rows, scales):
    return (
        value_rows
        * lax.rsqrt(jnp.mean(value_rows * value_rows, axis=-1, keepdims=True) + norm_epsilon)
        * scales
    )


def swiglu_rows(gate_rows):
    half_width = gate_rows.shape[1] // 2
    return sigmoid_linear(gate_rows[:, :half_width]) * gate_rows[:, half_width:]


def product(left, right):
    return jnp.dot(left, right, preferred_element_type=jnp.float32)


def product_back(left, right):
    return lax.dot_general(
        left, right, (((1,), (1,)), ((), ())), preferred_element_type=jnp.float32
    )


def token_sum(left, right):
    return lax.dot_general(
        left, right, (((0,), (0,)), ((), ())), preferred_element_type=jnp.float32
    )


def carry_state(earlier, later):
    return (earlier[0] * later[0], later[1] + later[0][:, None, None] * earlier[1])


def span_step(carried, pieces):
    scaled_x, log_decay, in_basis, out_basis = pieces
    cumulated = jnp.cumsum(log_decay, axis=0)
    length = log_decay.shape[0]
    causal = jnp.arange(length)[:, None] >= jnp.arange(length)[None, :]
    spread = jnp.where(
        causal[:, :, None], cumulated[:, None, :] - cumulated[None, :, :], masked_score
    )
    mixing = jnp.exp(spread) * jnp.dot(out_basis, in_basis.T, precision=highest)[:, :, None]
    result = jnp.einsum("tsh,shp->thp", mixing, scaled_x, precision=highest)
    result = result + jnp.exp(cumulated)[:, :, None] * jnp.einsum(
        "tn,hpn->thp", out_basis, carried, precision=highest
    )
    final_cumul = cumulated[-1]
    weight_in = jnp.exp(final_cumul[None, :] - cumulated)
    new_state = jnp.exp(final_cumul)[:, None, None] * carried + jnp.einsum(
        "sh,shp,sn->hpn", weight_in, scaled_x, in_basis, precision=highest
    )
    return (new_state, result)


def split_projection(projected):
    inner = MH * MP
    return (
        projected[:, :inner],
        projected[:, inner : 2 * inner],
        projected[:, 2 * inner : 2 * inner + NS],
        projected[:, 2 * inner + NS : 2 * inner + 2 * NS],
        projected[:, 2 * inner + 2 * NS :],
    )


def mamba_first(inner_x, in_basis, out_basis, step_raw, step_shift, decay_rate, skip_weight):
    count_of_rows = inner_x.shape[0]
    step_size = jnp.log1p(jnp.exp(step_raw + step_shift))
    log_decay = -jnp.exp(decay_rate) * step_size
    per_head = inner_x.reshape(count_of_rows, MH, MP)
    scaled_x = per_head * step_size[:, :, None]
    block_count = count_of_rows // SPAN
    pieces = (
        scaled_x.reshape(block_count, SPAN, MH, MP),
        log_decay.reshape(block_count, SPAN, MH),
        in_basis.reshape(block_count, SPAN, NS),
        out_basis.reshape(block_count, SPAN, NS),
    )
    start_state = jnp.zeros((MH, MP, NS), jnp.float32)
    end_state, results = lax.scan(span_step, start_state, pieces)
    mixed = results.reshape(count_of_rows, MH, MP) + skip_weight[None, :, None] * per_head
    cumulative = jnp.cumsum(log_decay, axis=0)
    return (mixed, end_state, cumulative[-1], cumulative)


def mamba_second(mixed, cumulative, gate_raw, out_basis, entering):
    count_of_rows = mixed.shape[0]
    carried_in = jnp.exp(cumulative)[:, :, None] * jnp.einsum(
        "tn,hpn->thp", out_basis, entering, precision=highest
    )
    return (mixed + carried_in).reshape(count_of_rows, MH * MP) * sigmoid_linear(gate_raw)


def mamba_whole(
    gate_raw, inner_x, in_basis, out_basis, step_raw, step_shift, decay_rate, skip_weight, entering
):
    mixed, end_state, total_decay, cumulative = mamba_first(
        inner_x, in_basis, out_basis, step_raw, step_shift, decay_rate, skip_weight
    )
    return (
        mamba_second(mixed, cumulative, gate_raw, out_basis, entering),
        end_state,
        total_decay,
        cumulative,
    )


def split_keys(key_value_pairs):
    count_of_keys = key_value_pairs.shape[0]
    width_of_keys = KEY_VALUE_HEADS * HEAD_SIZE
    return (
        key_value_pairs[:, :width_of_keys].reshape(count_of_keys, KEY_VALUE_HEADS, HEAD_SIZE),
        key_value_pairs[:, width_of_keys:].reshape(count_of_keys, KEY_VALUE_HEADS, HEAD_SIZE),
    )


def block_scores(query_rows, key_part, start_row, rows_per_block, first_row):
    head_groups = QUERY_HEADS // KEY_VALUE_HEADS
    block_of_queries = query_rows.reshape(rows_per_block, KEY_VALUE_HEADS, head_groups, HEAD_SIZE)
    scores = jnp.einsum(
        "qkgd,tkd->kgqt", block_of_queries, key_part, preferred_element_type=jnp.float32
    ) * HEAD_SIZE ** (-0.5)
    query_place = first_row + start_row + jnp.arange(rows_per_block)
    key_place = jnp.arange(key_part.shape[0])
    scores = jnp.where(key_place[None, :] <= query_place[:, None], scores, masked_score)
    return (block_of_queries, scores)


def attend(query_rows, key_value_pairs, first_row):
    count_of_rows = query_rows.shape[0]
    rows_per_block = min(512, count_of_rows)
    key_part, value_part = split_keys(key_value_pairs)

    def one_block(block_index):
        block_of_queries, scores = block_scores(
            query_rows, key_part, block_index * rows_per_block, rows_per_block, first_row
        )
        peak = jnp.max(scores, axis=-1, keepdims=True)
        weights = jnp.exp(scores - peak)
        totals = jnp.sum(weights, axis=-1, keepdims=True)
        probs = (weights / totals).astype(jnp.bfloat16)
        mixed = jnp.einsum("kgqt,tkd->qkgd", probs, value_part, preferred_element_type=jnp.float32)
        return (
            mixed.reshape(rows_per_block, QUERY_HEADS * HEAD_SIZE),
            (peak + jnp.log(totals))[..., 0],
        )

    mixed, log_totals = lax.map(one_block, jnp.arange(count_of_rows // rows_per_block))
    return (mixed.reshape(count_of_rows, QUERY_HEADS * HEAD_SIZE), log_totals)


def attend_back(query_rows, key_value_pairs, mixed_gradient, log_totals, first_row):
    count_of_rows = query_rows.shape[0]
    count_of_keys = key_value_pairs.shape[0]
    head_groups = QUERY_HEADS // KEY_VALUE_HEADS
    scale = HEAD_SIZE ** (-0.5)
    rows_per_block = min(512, count_of_rows)
    key_part, value_part = split_keys(key_value_pairs)

    def one_block(accum, block_index):
        start_row = block_index * rows_per_block
        block_of_queries, scores = block_scores(
            query_rows, key_part, start_row, rows_per_block, first_row
        )
        block_gradient = mixed_gradient.reshape(
            rows_per_block, KEY_VALUE_HEADS, head_groups, HEAD_SIZE
        )
        probs = jnp.exp(scores - log_totals[block_index][..., None])
        prob_grad = jnp.einsum(
            "qkgd,tkd->kgqt", block_gradient, value_part, preferred_element_type=jnp.float32
        )
        centre = jnp.sum(probs * prob_grad, axis=-1, keepdims=True)
        score_grad = (probs * (prob_grad - centre)).astype(jnp.bfloat16)
        query_grad = (
            jnp.einsum("kgqt,tkd->qkgd", score_grad, key_part, preferred_element_type=jnp.float32)
            * scale
        )
        key_gradient = (
            jnp.einsum(
                "kgqt,qkgd->tkd", score_grad, block_of_queries, preferred_element_type=jnp.float32
            )
            * scale
        )
        value_gradient = jnp.einsum(
            "kgqt,qkgd->tkd",
            probs.astype(jnp.bfloat16),
            block_gradient,
            preferred_element_type=jnp.float32,
        )
        accum = accum + jnp.concatenate(
            [
                key_gradient.reshape(count_of_keys, KEY_VALUE_HEADS * HEAD_SIZE),
                value_gradient.reshape(count_of_keys, KEY_VALUE_HEADS * HEAD_SIZE),
            ],
            axis=1,
        )
        return (accum, query_grad.reshape(rows_per_block, QUERY_HEADS * HEAD_SIZE))

    initial_accumulator = jnp.zeros((count_of_keys, 2 * KEY_VALUE_HEADS * HEAD_SIZE), jnp.float32)
    accum, query_grads = lax.scan(
        one_block, initial_accumulator, jnp.arange(count_of_rows // rows_per_block)
    )
    return (query_grads.reshape(count_of_rows, QUERY_HEADS * HEAD_SIZE), accum)


def layer_forward(hidden, weights, first_row):
    (
        mixer_w,
        attn_w,
        mamba_w,
        attn_out_w,
        gate_up_w,
        down_w,
        scales,
        step_shift,
        decay_rate,
        skip_weight,
    ) = weights
    scales = scales.astype(jnp.float32)
    query_width = QUERY_HEADS * HEAD_SIZE
    normed = norm_rows(hidden, scales[0]).astype(jnp.bfloat16)
    projected = product(normed, mixer_w)
    attn_rows = product(normed, attn_w).astype(jnp.bfloat16)
    key_value_pairs = lax.all_gather(attn_rows[:, query_width:], "seq", axis=0, tiled=True)
    attn_mixed, log_totals = attend(attn_rows[:, :query_width], key_value_pairs, first_row)
    attn_mixed = attn_mixed.astype(jnp.bfloat16)
    gate_raw, inner_x, in_basis, out_basis, step_raw = split_projection(projected)
    mixed, end_state, total_decay, cumulative = mamba_first(
        inner_x,
        in_basis,
        out_basis,
        step_raw,
        step_shift.astype(jnp.float32),
        decay_rate.astype(jnp.float32),
        skip_weight.astype(jnp.float32),
    )
    decay_factor = jnp.exp(total_decay)
    state_ident = (jnp.ones_like(decay_factor), jnp.zeros_like(end_state))
    prefix_decay, entering = entering_2((decay_factor, end_state), "seq", carry_state, state_ident)
    gated = mamba_second(mixed, cumulative, gate_raw, out_basis, entering).astype(jnp.bfloat16)
    after_mixers = hidden + product(attn_mixed, attn_out_w) + product(gated, mamba_w)
    normed_two = norm_rows(after_mixers, scales[1]).astype(jnp.bfloat16)
    activated = swiglu_rows(product(normed_two, gate_up_w)).astype(jnp.bfloat16)
    return (
        after_mixers + product(activated, down_w),
        (key_value_pairs, attn_mixed, log_totals, entering),
    )


def layer_backward(hidden, record, weights, grad_rows, first_row):
    key_value_pairs, attn_mixed, log_totals, entering = record
    (
        mixer_w,
        attn_w,
        mamba_w,
        attn_out_w,
        gate_up_w,
        down_w,
        scales,
        step_shift,
        decay_rate,
        skip_weight,
    ) = weights
    scales = scales.astype(jnp.float32)
    query_width = QUERY_HEADS * HEAD_SIZE
    normed_f, norm_back = jax.vjp(norm_rows, hidden, scales[0])
    normed = normed_f.astype(jnp.bfloat16)
    projected = product(normed, mixer_w)
    query_rows = product(normed, attn_w[:, :query_width]).astype(jnp.bfloat16)
    gate_raw, inner_x, in_basis, out_basis, step_raw = split_projection(projected)
    mamba_outs, mamba_back = jax.vjp(
        mamba_whole,
        gate_raw,
        inner_x,
        in_basis,
        out_basis,
        step_raw,
        step_shift.astype(jnp.float32),
        decay_rate.astype(jnp.float32),
        skip_weight.astype(jnp.float32),
        entering,
    )
    gated_f, end_state, total_decay, cumulative = mamba_outs
    gated = gated_f.astype(jnp.bfloat16)
    after_mixers = hidden + product(attn_mixed, attn_out_w) + product(gated, mamba_w)
    normed_two_f, norm_two_back = jax.vjp(norm_rows, after_mixers, scales[1])
    normed_two = normed_two_f.astype(jnp.bfloat16)
    activated_f, swiglu_back = jax.vjp(swiglu_rows, product(normed_two, gate_up_w))
    activated = activated_f.astype(jnp.bfloat16)
    ffn_grad = grad_rows.astype(jnp.bfloat16)
    down_grad = token_sum(activated, ffn_grad)
    act_grad = product_back(ffn_grad, down_w).astype(jnp.bfloat16)
    (up_grad,) = swiglu_back(act_grad.astype(jnp.float32))
    up_grad = up_grad.astype(jnp.bfloat16)
    gate_up_grad = token_sum(normed_two, up_grad)
    mid_part, scale_two_grad = norm_two_back(product_back(up_grad, gate_up_w))
    mid_grad = mid_part + grad_rows
    branch_grad = mid_grad.astype(jnp.bfloat16)
    attn_out_grad = token_sum(attn_mixed, branch_grad)
    mamba_out_grad = token_sum(gated, branch_grad)
    mixed_gradient = product_back(branch_grad, attn_out_w).astype(jnp.bfloat16)
    gated_grad = product_back(branch_grad, mamba_w).astype(jnp.bfloat16).astype(jnp.float32)
    query_grad, key_value_part = attend_back(
        query_rows, key_value_pairs, mixed_gradient, log_totals, first_row
    )
    key_value_grad = lax.psum_scatter(
        key_value_part.astype(jnp.bfloat16), "seq", scatter_dimension=0, tiled=True
    ).astype(jnp.float32)
    attn_rows_grad = jnp.concatenate([query_grad, key_value_grad], axis=1).astype(jnp.bfloat16)
    count_of_rows = hidden.shape[0]
    mixed_dy = (gated_grad * sigmoid_linear(gate_raw)).reshape(count_of_rows, MH, MP)
    state_grad = jnp.einsum(
        "th,thp,tn->hpn", jnp.exp(cumulative), mixed_dy, out_basis, precision=highest
    )
    decay_factor = jnp.exp(total_decay)
    state_ident = (jnp.ones_like(decay_factor), jnp.zeros_like(state_grad))
    suffix_decay, later_grad = prefix((decay_factor, state_grad), "seq", carry_state, state_ident)
    decay_grad = decay_factor * jnp.sum(later_grad * entering, axis=(1, 2))
    pieces_grad = mamba_back((gated_grad, later_grad, decay_grad, jnp.zeros_like(cumulative)))
    proj_grad = jnp.concatenate(
        [pieces_grad[0], pieces_grad[1], pieces_grad[2], pieces_grad[3], pieces_grad[4]], axis=1
    ).astype(jnp.bfloat16)
    mixer_grad = token_sum(normed, proj_grad)
    attn_in_grad = token_sum(normed, attn_rows_grad)
    input_part, scale_one_grad = norm_back(
        product_back(proj_grad, mixer_w) + product_back(attn_rows_grad, attn_w)
    )
    local_grads = (
        mixer_grad,
        attn_in_grad,
        mamba_out_grad,
        attn_out_grad,
        gate_up_grad,
        down_grad,
        jnp.stack([scale_one_grad, scale_two_grad]),
        pieces_grad[5],
        pieces_grad[6],
        pieces_grad[7],
    )
    row_parts = (
        normed,
        gated,
        attn_mixed,
        normed_two,
        activated,
        proj_grad,
        attn_rows_grad,
        branch_grad,
        up_grad,
        ffn_grad,
    )
    return (input_part + mid_grad, local_grads, row_parts)


def local(
    inputs,
    cotangent,
    mixer_in,
    attn_in,
    mamba_out,
    attn_out,
    gate_up,
    down_proj,
    norm_gains,
    step_bias,
    decay_log,
    skip_gain,
):
    hidden = inputs[0].astype(jnp.float32)
    first_row = lax.axis_index("seq") * hidden.shape[0]
    kept_layers = []
    layer_index = 0
    weights = (
        *sent_together((mixer_in[layer_index], attn_in[layer_index]), "seq", 0, 1),
        lax.all_gather(mamba_out[layer_index], "seq", axis=0, tiled=True),
        lax.all_gather(attn_out[layer_index], "seq", axis=0, tiled=True),
        lax.all_gather(gate_up[layer_index], "seq", axis=0, tiled=True),
        lax.all_gather(down_proj[layer_index], "seq", axis=0, tiled=True),
        lax.all_gather(norm_gains[layer_index], "seq", axis=1, tiled=True),
        lax.all_gather(step_bias[layer_index], "seq", axis=0, tiled=True),
        lax.all_gather(decay_log[layer_index], "seq", axis=0, tiled=True),
        lax.all_gather(skip_gain[layer_index], "seq", axis=0, tiled=True),
    )
    kept_layers.append(weights)
    layer_inputs = [hidden]
    hidden, record = layer_forward(hidden, weights, first_row)
    records = [record]
    grad_rows = cotangent[0].astype(jnp.float32)
    layer_grads = [None] * LAYERS
    for layer_index in reversed(range(LAYERS)):
        weights = (
            *sent_together((mixer_in[layer_index], attn_in[layer_index]), "seq", 0, 1),
            lax.all_gather(mamba_out[layer_index], "seq", axis=0, tiled=True),
            lax.all_gather(attn_out[layer_index], "seq", axis=0, tiled=True),
            lax.all_gather(gate_up[layer_index], "seq", axis=0, tiled=True),
            lax.all_gather(down_proj[layer_index], "seq", axis=0, tiled=True),
            lax.all_gather(norm_gains[layer_index], "seq", axis=1, tiled=True),
            lax.all_gather(step_bias[layer_index], "seq", axis=0, tiled=True),
            lax.all_gather(decay_log[layer_index], "seq", axis=0, tiled=True),
            lax.all_gather(skip_gain[layer_index], "seq", axis=0, tiled=True),
        )
        grad_rows, local_grads, row_parts = layer_backward(
            layer_inputs[layer_index], records[layer_index], weights, grad_rows, first_row
        )
        columns = (
            lax.all_to_all(row_parts[0], "seq", split_axis=1, concat_axis=0, tiled=True),
            lax.all_to_all(row_parts[1], "seq", split_axis=1, concat_axis=0, tiled=True),
            lax.all_to_all(row_parts[2], "seq", split_axis=1, concat_axis=0, tiled=True),
            lax.all_to_all(row_parts[3], "seq", split_axis=1, concat_axis=0, tiled=True),
            lax.all_to_all(row_parts[4], "seq", split_axis=1, concat_axis=0, tiled=True),
        )
        gathered = (
            lax.all_gather(row_parts[5], "seq", axis=0, tiled=True),
            lax.all_gather(row_parts[6], "seq", axis=0, tiled=True),
            lax.all_gather(row_parts[7], "seq", axis=0, tiled=True),
            lax.all_gather(row_parts[8], "seq", axis=0, tiled=True),
            lax.all_gather(row_parts[9], "seq", axis=0, tiled=True),
        )
        small_sums = (
            summed_on_arrival(local_grads[6], "seq", 1),
            summed_on_arrival(local_grads[7], "seq", 0),
            summed_on_arrival(local_grads[8], "seq", 0),
            summed_on_arrival(local_grads[9], "seq", 0),
        )
        owned = (
            token_sum(columns[0], gathered[0]),
            token_sum(columns[0], gathered[1]),
            token_sum(columns[1], gathered[2]),
            token_sum(columns[2], gathered[2]),
            token_sum(columns[3], gathered[3]),
            token_sum(columns[4], gathered[4]),
            small_sums[0],
            small_sums[1],
            small_sums[2],
            small_sums[3],
        )
        layer_grads[layer_index] = tuple(
            (
                part.astype(jnp.float32)
                for part in together(
                    (
                        owned[0].astype(jnp.bfloat16),
                        owned[1].astype(jnp.bfloat16),
                        owned[2].astype(jnp.bfloat16),
                        owned[3].astype(jnp.bfloat16),
                        owned[4].astype(jnp.bfloat16),
                        owned[5].astype(jnp.bfloat16),
                        owned[6].astype(jnp.bfloat16),
                        owned[7].astype(jnp.bfloat16),
                        owned[8].astype(jnp.bfloat16),
                        owned[9].astype(jnp.bfloat16),
                    ),
                    "dp",
                )
            )
        )
    stacked = [jnp.stack([layer_grads[0][member_index]]) for member_index in range(10)]
    return (
        hidden.astype(jnp.bfloat16)[None],
        grad_rows[None],
        stacked[0],
        stacked[1],
        stacked[2],
        stacked[3],
        stacked[4],
        stacked[5],
        stacked[6],
        stacked[7],
        stacked[8],
        stacked[9],
    )


def solution(mesh):
    return jax.shard_map(
        local,
        mesh=mesh,
        in_specs=(
            P("dp", "seq", None),
            P("dp", "seq", None),
            P(None, "seq", None),
            P(None, "seq", None),
            P(None, "seq", None),
            P(None, "seq", None),
            P(None, "seq", None),
            P(None, "seq", None),
            P(None, None, "seq"),
            P(None, "seq"),
            P(None, "seq"),
            P(None, "seq"),
        ),
        out_specs=(
            P("dp", "seq", None),
            P("dp", "seq", None),
            P(None, "seq", None),
            P(None, "seq", None),
            P(None, "seq", None),
            P(None, "seq", None),
            P(None, "seq", None),
            P(None, "seq", None),
            P(None, None, "seq"),
            P(None, "seq"),
            P(None, "seq"),
            P(None, "seq"),
        ),
        check_vma=False,
    )
```

profile of v0, /device:TPU:1, one launch (start us, length us, event | category | flops | bytes accessed | tf_op | source)
XLA Modules:
  0.0 1577.0 jit_solution(10265303507284213974)
XLA Ops:
  11.5 16.6 %all-gather = bf16[1,2,1024]{2,1,0:T(2,128)(2,1)S(1)} all-gather(bf16[1,2,128]{2,1,0:T(2,128)(2,1)S(1)} %copy-done.88), channel_id=2, replica_groups=mesh['dp'=16,'seq'=8] {'seq'}, dimensions={2}, use_global_device_ids=true | all-gather | bytes 4608 | tf_op jit(solution)/shard_map/all_gather | solution.py:467
  30.2 15.2 all-reduce.7
  45.5 138.4 %all-gather.26.cloned.1.call-done = bf16[1024,4120]{0,1:T(8,128)(2,1)} async-done(((bf16[128,4120]{0,1:T(8,128)(2,1)}), bf16[1024,4120]{0,1:T(8,128)(2,1)}) %all-gather.26.cloned.1.call-update) | async-done | bytes 8437776 | tf_op jit(solution)/shard_map/all_gather | solution.py:59
  183.9 5.0 fusion.132
  196.9 52.5 %while.114 = (s32[]{:T(128)}, f32[24,64,128]{2,1,0:T(8,128)S(1)}, f32[2,64,24,64]{1,0,3,2:T(2,128)}, f32[2,64,24]{2,1,0:T(8,128)}, f32[2,64,24,64]{1,3,2,0:T(8,1...) while((s32[]{:T(128)}, f32[24,64,128]{2,1,0:T(8,128)S(1)}, ...), condition=%wide.region_5.6_spmd.clone, body=%wide.region_3.0_spmd.clone.sunk | while | flops 385257472 | bytes 6223467 | solution.py:168
  203.8 19.4 %dynamic_update_slice.187 = f32[2,64,24,64]{1,0,3,2:T(2,128)} dynamic-update-slice(f32[2,64,24,64]{1,0,3,2:T(2,128)} %get-tuple-element.2040, f32[1,64,24,64]{1,0,3,2:T(1,128)S(1)} %bitcast.739, s32[]{:T(128)S(6)} %copy.557, s32[]{:T(128)} %constant.270.clone.1..sunk.3, s32[]{:T(128)} %constant.270.clone.1..sunk.3, s32[]{:T(128)} %constant.270.clone.1..sunk.3) | dynamic-update-slice | bytes 786436 | tf_op jit(solution)/shard_map/while/body/jit(dynamic_update_index_in_dim)/dynamic_update_slice | solution.py:168
  230.0 19.4 %dynamic_update_slice.187 = f32[2,64,24,64]{1,0,3,2:T(2,128)} dynamic-update-slice(f32[2,64,24,64]{1,0,3,2:T(2,128)} %get-tuple-element.2040, f32[1,64,24,64]{1,0,3,2:T(1,128)S(1)} %bitcast.739, s32[]{:T(128)S(6)} %copy.557, s32[]{:T(128)} %constant.270.clone.1..sunk.3, s32[]{:T(128)} %constant.270.clone.1..sunk.3, s32[]{:T(128)} %constant.270.clone.1..sunk.3) | dynamic-update-slice | bytes 786436 | tf_op jit(solution)/shard_map/while/body/jit(dynamic_update_index_in_dim)/dynamic_update_slice | solution.py:168
  256.7 73.2 %while.115 = (s32[]{:T(128)}, f32[24,64,128]{2,1,0:T(8,128)S(1)}, f32[2,64,24,64]{1,0,3,2:T(2,128)}, f32[2,64,64,24]{2,1,3,0:T(8,128)}, f32[2,128,64]{1,2,0:T(8,...) while((s32[]{:T(128)}, f32[24,64,128]{2,1,0:T(8,128)S(1)}, ...), condition=%wide.region_12.13_spmd.clone.clone, body=%wide.region_10.12_spmd.clone.clone.sunk | while | flops 385844736 | bytes 12467759 | solution.py:168
  268.9 19.4 %dynamic_update_slice.197 = f32[2,64,24,64]{1,0,3,2:T(2,128)} dynamic-update-slice(f32[2,64,24,64]{1,0,3,2:T(2,128)} %get-tuple-element.1984, f32[1,64,24,64]{1,0,3,2:T(1,128)S(1)} %bitcast.740, s32[]{:T(128)S(6)} %copy.524, s32[]{:T(128)} %constant.270.clone.1..sunk.4, s32[]{:T(128)} %constant.270.clone.1..sunk.4, s32[]{:T(128)} %constant.270.clone.1..sunk.4) | dynamic-update-slice | bytes 786436 | tf_op jit(solution)/shard_map/jvp()/while/body/jit(dynamic_update_index_in_dim)/dynamic_update_slice | solution.py:168
  305.4 19.4 %dynamic_update_slice.197 = f32[2,64,24,64]{1,0,3,2:T(2,128)} dynamic-update-slice(f32[2,64,24,64]{1,0,3,2:T(2,128)} %get-tuple-element.1984, f32[1,64,24,64]{1,0,3,2:T(1,128)S(1)} %bitcast.740, s32[]{:T(128)S(6)} %copy.524, s32[]{:T(128)} %constant.270.clone.1..sunk.4, s32[]{:T(128)} %constant.270.clone.1..sunk.4, s32[]{:T(128)} %constant.270.clone.1..sunk.4) | dynamic-update-slice | bytes 786436 | tf_op jit(solution)/shard_map/jvp()/while/body/jit(dynamic_update_index_in_dim)/dynamic_update_slice | solution.py:168
  332.1 36.5 %all_gather.76 = bf16[1024,256]{1,0:T(8,128)(2,1)S(1)} all-gather(bf16[128,256]{1,0:T(8,128)(2,1)S(1)} %slice.146), channel_id=1, replica_groups=mesh['dp'=16,'seq'=8] {'seq'}, dimensions={0}, use_global_device_ids=true | all-gather | bytes 589824 | tf_op jit(solution)/shard_map/all_gather | solution.py:312
  378.7 17.6 %all-gather.11 = f32[8,1,24]{2,1,0:T(1,128)S(1)} all-gather(f32[1,1,24]{2,1,0:T(1,128)S(1)} %get-tuple-element.1530), channel_id=1, replica_groups=mesh['dp'=16,'seq'=8] {'seq'}, dimensions={0}, use_global_device_ids=true | all-gather | bytes 864 | tf_op jit(solution)/shard_map/all_gather | solution.py:23
  412.8 52.5 %all-gather.40.cloned.1.call-done = bf16[1,1536,1024]{2,1,0:T(8,128)(2,1)} async-done(((bf16[1,192,1024]{2,1,0:T(8,128)(2,1)}), bf16[1,1536,1024]{2,1,0:T(8,128)(2,1)}) %all-gather.40.cloned.1.call-update) | async-done | bytes 3145744 | tf_op jit(solution)/shard_map/all_gather | solution.py:463
  468.0 168.2 %all-gather.42.cloned.1.call-done = bf16[1,1024,4096]{2,1,0:T(8,128)(2,1)} async-done(((bf16[1,128,4096]{2,1,0:T(8,128)(2,1)}), bf16[1,1024,4096]{2,1,0:T(8,128)(2,1)}) %all-gather.42.cloned.1.call-update) | async-done | bytes 8388624 | tf_op jit(solution)/shard_map/all_gather | solution.py:465
  636.2 6.1 fusion.126
  642.3 90.6 %all-gather.44.cloned.1.call-done = bf16[1,2048,1024]{2,1,0:T(8,128)(2,1)} async-done(((bf16[1,256,1024]{2,1,0:T(8,128)(2,1)}), bf16[1,2048,1024]{2,1,0:T(8,128)(2,1)}) %all-gather.44.cloned.1.call-update) | async-done | bytes 4194320 | tf_op jit(solution)/shard_map/all_gather | solution.py:466
  732.9 5.3 fusion.260
  738.4 7.4 multiply_reduce_fusion.5
  758.1 5.2 multiply_reduce_fusion.1
  769.3 23.9 %reduce-scatter.4.cloned.1.call-done = bf16[128,256]{1,0:T(8,128)(2,1)} async-done(((bf16[1024,256]{1,0:T(8,128)(2,1)}), bf16[128,256]{1,0:T(8,128)(2,1)}) %reduce-scatter.4.cloned.1.call-update) | async-done | bytes 65552
  796.9 12.2 all-gather.12
  813.8 55.7 %all-gather.46.cloned.1.call-done = bf16[192,64,128]{2,1,0:T(8,128)(2,1)} async-done(((bf16[24,64,128]{2,1,0:T(8,128)(2,1)}), bf16[192,64,128]{2,1,0:T(8,128)(2,1)}) %all-gather.46.cloned.1.call-update) | async-done | bytes 3145744 | tf_op jit(solution)/shard_map/all_gather | solution.py:39
  869.6 8.7 while.112
  881.6 117.7 %while.113 = (s32[]{:T(128)}, f32[24,64,128]{2,1,0:T(8,128)S(1)}, f32[2,64,24,64]{1,0,3,2:T(2,128)}, f32[2,64,24]{2,1,0:T(8,128)}, bf16[2,64,128]{2,1,0:T(8,128)...) while((s32[]{:T(128)}, f32[24,64,128]{2,1,0:T(8,128)S(1)}, ...), condition=%wide.region_25.26_spmd.clone, body=%wide.region_17.25_spmd.clone.sunk | while | flops 769936896 | bytes 30608172 | solution.py:168
  905.8 19.5 %dynamic_update_slice.186 = f32[2,64,24,64]{1,0,3,2:T(2,128)} dynamic-update-slice(f32[2,64,24,64]{1,0,3,2:T(2,128)} %get-tuple-element.2137, f32[1,64,24,64]{1,0,3,2:T(1,128)} %copy.475, s32[]{:T(128)S(6)} %sub.292, s32[]{:T(128)} %constant.270.clone.1..sunk.2, s32[]{:T(128)} %constant.270.clone.1..sunk.2, s32[]{:T(128)} %constant.270.clone.1..sunk.2) | dynamic-update-slice | bytes 786436 | tf_op jit(solution)/shard_map/transpose(jvp())/while/body/jit(dynamic_update_index_in_dim)/dynamic_update_slice | solution.py:168
  964.7 19.5 %dynamic_update_slice.186 = f32[2,64,24,64]{1,0,3,2:T(2,128)} dynamic-update-slice(f32[2,64,24,64]{1,0,3,2:T(2,128)} %get-tuple-element.2137, f32[1,64,24,64]{1,0,3,2:T(1,128)} %copy.475, s32[]{:T(128)S(6)} %sub.292, s32[]{:T(128)} %constant.270.clone.1..sunk.2, s32[]{:T(128)} %constant.270.clone.1..sunk.2, s32[]{:T(128)} %constant.270.clone.1..sunk.2) | dynamic-update-slice | bytes 786436 | tf_op jit(solution)/shard_map/transpose(jvp())/while/body/jit(dynamic_update_index_in_dim)/dynamic_update_slice | solution.py:168
  1027.7 7.5 all-to-all-done.4
  1046.6 7.3 all-to-all-start.2
  1109.7 105.9 %all-gather.34.cloned.1.call-done = bf16[1024,4096]{1,0:T(8,128)(2,1)} async-done(((bf16[128,4096]{1,0:T(8,128)(2,1)}), bf16[1024,4096]{1,0:T(8,128)(2,1)}) %all-gather.34.cloned.1.call-update) | async-done | bytes 8388624 | tf_op jit(solution)/shard_map/all_gather | solution.py:504
  1220.5 137.7 %all-gather.28.cloned.1.call-done = bf16[1024,3352]{0,1:T(8,128)(2,1)} async-done(((bf16[128,3352]{0,1:T(8,128)(2,1)}), bf16[1024,3352]{0,1:T(8,128)(2,1)}) %all-gather.28.cloned.1.call-update) | async-done | bytes 6864912 | tf_op jit(solution)/shard_map/all_gather | solution.py:501
  1365.3 37.0 %concatenate.25 = bf16[1576201]{0:T(1024)(128)(2,1)} concatenate(bf16[429056]{0:T(1024)(128)(2,1)S(1)} %reshape.625, bf16[98304]{0:T(1024)(128)(2,1)S(1)} %reshape.626, bf16[196608]{0:T(1024)(128)(2,1)} %bitcast.759, bf16[65536]{0:T(1024)(128)(2,1)} %bitcast.776, bf16[524288]{0:T(1024)(128)(2,1)S(1)} %bitcast.748, bf16[262144]{0:T(1024)(128)(2,1)S(1)} %bitcast.755, ...), dimensions={0} | concatenate | bytes 6304804 | tf_op jit(solution)/shard_map/concatenate | solution.py:81
  1412.6 140.3 %all-reduce.10.cloned.1.call-done = bf16[1576201]{0:T(1024)(128)(2,1)} async-done(((bf16[1576201]{0:T(1024)(128)(2,1)}), bf16[1576201]{0:T(1024)(128)(2,1)}) %all-reduce.10.cloned.1.call-update) | async-done | bytes 3152418 | tf_op jit(solution)/shard_map/psum | solution.py:81
  (584 shorter events, 351.4 us)
Async XLA Ops:
  7.2 176.7 %all-gather.26.cloned.1.call-start = ((), (), s32[]{:S(2)}) async-start(), calls=%async_computation.10 | async-start | bytes 9492480 | tf_op jit(solution)/shard_map/all_gather | solution.py:59
  10.6 389.1 %all-gather.36.cloned.1.call-start = ((), (), s32[]{:S(2)}) async-start(), calls=%async_computation.16 | async-start | bytes 1179648 | tf_op jit(solution)/shard_map/all_gather | solution.py:464
  11.4 393.6 %all-gather.38.cloned.1.call-start = ((), (), s32[]{:S(2)}) async-start(), calls=%async_computation.17 | async-start | bytes 7077888 | tf_op jit(solution)/shard_map/all_gather | solution.py:23
  28.0 160.9 %copy-start.66 = (f32[1,1,1024]{2,1,0:T(1,128)}, f32[1,1,1024]{2,1,0:T(1,128)S(1)}, u32[]{:S(2)}) copy-start(f32[1,1,1024]{2,1,0:T(1,128)S(1)} %get-tuple-element.1533) | copy-start | bytes 12292
  28.2 160.8 %copy-start.85 = (f32[128]{0:T(128)}, f32[128]{0:T(128)S(1)}, u32[]{:S(2)}) copy-start(f32[128]{0:T(128)S(1)} %fusion.242) | copy-start | bytes 1540
  28.2 160.8 %copy-start.78 = (f32[128]{0:T(128)}, f32[128]{0:T(128)S(1)}, u32[]{:S(2)}) copy-start(f32[128]{0:T(128)S(1)} %fusion.271) | copy-start | bytes 1540
  45.5 143.5 %copy-start.96 = (bf16[24]{0:T(256)(128)(2,1)}, bf16[24]{0:T(256)(128)(2,1)S(1)}, u32[]{:S(2)}) copy-start(bf16[24]{0:T(256)(128)(2,1)S(1)} %get-tuple-element.1486) | copy-start | bytes 148
  45.5 207.6 %copy-start.89 = (bf16[24]{0:T(256)(128)(2,1)}, bf16[24]{0:T(256)(128)(2,1)S(1)}, u32[]{:S(2)}) copy-start(bf16[24]{0:T(256)(128)(2,1)S(1)} %get-tuple-element.1487) | copy-start | bytes 148
  45.5 143.6 %copy-start.81 = (f32[24]{0:T(128)}, f32[24]{0:T(128)S(1)}, u32[]{:S(2)}) copy-start(f32[24]{0:T(128)S(1)} %fusion.270) | copy-start | bytes 292
  45.5 143.6 %copy-start.82 = (f32[24]{0:T(128)}, f32[24]{0:T(128)S(1)}, u32[]{:S(2)}) copy-start(f32[24]{0:T(128)S(1)} %convert_element_type.353) | copy-start | bytes 292
  250.3 215.0 %all-gather.40.cloned.1.call-start = ((), (), s32[]{:S(2)}) async-start(), calls=%async_computation.18 | async-start | bytes 3538944 | tf_op jit(solution)/shard_map/all_gather | solution.py:463
  250.9 385.3 %all-gather.42.cloned.1.call-start = ((), (), s32[]{:S(2)}) async-start(), calls=%async_computation.19 | async-start | bytes 9437184 | tf_op jit(solution)/shard_map/all_gather | solution.py:465
  251.5 481.4 %all-gather.44.cloned.1.call-start = ((), (), s32[]{:S(2)}) async-start(), calls=%async_computation.20 | async-start | bytes 4718592 | tf_op jit(solution)/shard_map/all_gather | solution.py:466
  252.1 541.2 %reduce-scatter.4.cloned.1.call-start = ((), (), s32[]{:S(2)}) async-start(), calls=%async_computation.23 | async-start | bytes 589824
  468.0 277.8 %copy-start.11 = (f32[128,1024]{1,0:T(8,128)}, f32[128,1024]{1,0:T(8,128)S(1)}, u32[]{:S(2)}) copy-start(f32[128,1024]{1,0:T(8,128)S(1)} %get-tuple-element.1538) | copy-start | bytes 1572868
  468.0 277.8 %copy-start.72 = (f32[128]{0:T(128)}, f32[128]{0:T(128)S(1)}, u32[]{:S(2)}) copy-start(f32[128]{0:T(128)S(1)} %fusion.272) | copy-start | bytes 1540
  757.9 111.7 %all-gather.46.cloned.1.call-start = ((), (), s32[]{:S(2)}) async-start(), calls=%async_computation.21 | async-start | bytes 3538944 | tf_op jit(solution)/shard_map/all_gather | solution.py:39
  765.8 275.2 %all-gather.48.cloned.1.call-start = ((), (), s32[]{:S(2)}) async-start(), calls=%async_computation.22 | async-start | bytes 2359296 | tf_op jit(solution)/shard_map/all_gather | solution.py:505
  766.6 287.3 %all-gather.32.cloned.1.call-start = ((), (), s32[]{:S(2)}) async-start(), calls=%async_computation.13 | async-start | bytes 2359296 | tf_op jit(solution)/shard_map/all_gather | solution.py:503
  767.2 336.9 %all-gather.30.cloned.1.call-start = ((), (), s32[]{:S(2)}) async-start(), calls=%async_computation.12 | async-start | bytes 1769472 | tf_op jit(solution)/shard_map/all_gather | solution.py:502
  794.9 420.6 %all-gather.34.cloned.1.call-start = ((), (), s32[]{:S(2)}) async-start(), calls=%async_computation.14 | async-start | bytes 9437184 | tf_op jit(solution)/shard_map/all_gather | solution.py:504
  795.5 562.7 %all-gather.28.cloned.1.call-start = ((), (), s32[]{:S(2)}) async-start(), calls=%async_computation.11 | async-start | bytes 7723008 | tf_op jit(solution)/shard_map/all_gather | solution.py:501
  1015.9 8.2 all-to-all-start.8
  1024.0 11.1 all-to-all-start.4
  1035.2 11.4 all-to-all-start.1
  1046.6 15.4 all-to-all-start.2
  1061.9 12.3 all-to-all-start
  1074.2 9.7 all-to-all-start.6
  1083.9 8.2 all-to-all-start.7
  1092.1 8.3 all-to-all-start.5
  1100.4 9.3 all-to-all-start.3
  1103.8 449.1 %all-reduce.10.cloned.1.call-start = ((), (), s32[]{:S(2)}) async-start(), calls=%async_computation.15 | async-start | bytes 6307840 | tf_op jit(solution)/shard_map/psum | solution.py:81
  (103 other events, 1236.6 us)
Sparse Core Ops, SparseCore 0:
  10.8 173.1 all-gather.25
  185.6 37.2 all-gather.35
  250.4 141.5 all-gather.37
  393.6 71.6 all-gather.39
  466.8 169.3 all-gather.41
  637.7 95.1 all-gather.43
  758.0 35.2 reduce-scatter.3
  795.5 73.9 all-gather.45
  871.3 50.3 all-gather.47
  923.8 51.4 all-gather.31
  976.9 48.3 all-gather.29
  1027.5 188.0 all-gather.33
  1217.2 140.9 all-gather.27
  1402.5 150.3 all-reduce.9
where the time goes:
time: 1600 us; the launch traced here: 1580 us
  waiting for transfers between devices  951 us (59%)
  local copies, waits for them, and re-layouts  257 us (16%)
  matrix products  160 us (10%)
  blocking collectives  98.1 us (6%)
  other arithmetic  55.6 us (3%)
  starting transfers between devices  38.3 us (2%)
  between operations  16.3 us (1%)
    all_gather x1, waiting for transfers between devices, local(): lax.all_gather(gate_up[layer_index], 'seq', axis=0, tiled=True)  168 us
    psum x1, waiting for transfers between devices, together(): so_far = lax.psum(jnp.concatenate([a.ravel() for a in arrays]), axis)  140 us
    all_gather x1, waiting for transfers between devices, sent_together(): out, at, outs = (lax.all_gather(both, axis, axis=dim, tiled=True), 0, [])  138 us
    all_gather x1, waiting for transfers between devices, local(): lax.all_gather(row_parts[5], 'seq', axis=0, tiled=True)  138 us
    dynamic_update_slice x20, local copies, waits for them, and re-layouts, mamba_first(): end_state, results = lax.scan(span_step, start_state, pieces)  128 us
    all_gather x1, waiting for transfers between devices, local(): lax.all_gather(row_parts[8], 'seq', axis=0, tiled=True)  106 us
    all_gather x1, waiting for transfers between devices, local(): lax.all_gather(down_proj[layer_index], 'seq', axis=0, tiled=True)  90.6 us
    all_gather x1, waiting for transfers between devices, prefix(): lax.all_gather(a.astype(kind), axis)  55.7 us
  transfers between devices with their start and end apart: 23, of which 18 were waited for; matrix products, arithmetic and copies ran while one was open for 24% of the time, Pallas kernels for 0%

commit v1 on v0

v1 whole, which is shorter than its diff:
```python
import jax
import jax.numpy as jnp
from jax import lax
from jax.experimental import pallas as pl
from jax.experimental.pallas import tpu as pltpu
from jax.sharding import PartitionSpec as P

MH = 24
MP = 64
NS = 128
QH = 8
KVH = 2
HS = 64
FF = 2048
SEQ = 8
DP = 16
HL = MH // SEQ
HW = HL * MP
INNER = MH * MP
FL = FF // SEQ
ROWS = 128
TOK = 1024
D = 1024
CH = 256
NCH = TOK // CH
CB, CC, CZ, CQ, CU, CK, CV, CR, CW = 0, 128, 256, 448, 512, 704, 768, 832, 896
EPS = 1e-05
NEG = -1e30
F32 = jnp.float32
BF = jnp.bfloat16
HIGH = lax.Precision.HIGHEST


def dot(a, b, dims=((1,), (0,)), precision=None):
    return lax.dot_general(a, b, (dims, ((), ())), precision=precision, preferred_element_type=F32)


def x_shift(k):
    return [(i, ((i // 2 + k) % 4) * 2 + i % 2) for i in range(SEQ)]


Z_SWAP = [(i, i ^ 1) for i in range(SEQ)]


def gather_rows(x):
    me = lax.axis_index("seq")
    mx, mz = me // 2, me % 2
    h = x.shape[0] // 2
    send = lambda v, perm: lax.ppermute(v, "seq", perm)
    z, a, b = send(x, Z_SWAP), send(x, x_shift(1)), send(x, x_shift(-1))
    c0, c1 = send(a[:h], x_shift(1)), send(b[h:], x_shift(-1))
    za, zb = send(z, x_shift(1)), send(z, x_shift(-1))
    zc0, zc1 = send(c0, Z_SWAP), send(c1, Z_SWAP)
    out = jnp.zeros((TOK, x.shape[1]), x.dtype)

    def put(out, v, dx, other, off):
        at = ((mx + dx) % 4 * 2 + (1 - mz if other else mz)) * ROWS + off
        return lax.dynamic_update_slice(out, v, (at, 0))

    for v, dx, other, off in (
        (x, 0, 0, 0), (z, 0, 1, 0), (a, 3, 0, 0), (b, 1, 0, 0), (c0, 2, 0, 0), (c1, 2, 0, h),
        (za, 3, 1, 0), (zb, 1, 1, 0), (zc0, 2, 1, 0), (zc1, 2, 1, h),
    ):
        out = put(out, v, dx, other, off)
    return out


def scatter_rows(part):
    got = lax.all_to_all(part.reshape(SEQ, ROWS, D), "seq", split_axis=0, concat_axis=0, tiled=True)
    return got.astype(F32).sum(0)


def per_head(cols, shape):
    lane = lax.broadcasted_iota(jnp.int32, shape, 1)
    return jnp.where(lane < MP, cols[0], jnp.where(lane < 2 * MP, cols[1], cols[2]))


def widen(v8):
    return per_head([v8[:, h : h + 1] for h in range(HL)], (v8.shape[0], HW))


def row_heads(v8):
    row = lax.broadcasted_iota(jnp.int32, (HW, NS), 0)
    return jnp.where(row < MP, v8[:, 0:1], jnp.where(row < 2 * MP, v8[:, 1:2], v8[:, 2:3]))


def head_mask(h, shape):
    lane = lax.broadcasted_iota(jnp.int32, shape, 1)
    return (lane >= h * MP) & (lane < (h + 1) * MP)


def tri_lower():
    t = lax.broadcasted_iota(jnp.int32, (CH, CH), 0)
    s = lax.broadcasted_iota(jnp.int32, (CH, CH), 1)
    return t >= s


def steps(r8, small):
    pre = r8 + small[0:1, :]
    dt = jnp.log1p(jnp.exp(pre))
    return pre, dt, -jnp.exp(small[1:2, :]) * dt


def block_decays(log_decay):
    low = tri_lower()
    ones = low.astype(F32)
    cum = dot(ones, log_decay, precision=HIGH)
    cum_t = dot(log_decay, ones, ((0,), (1,)), precision=HIGH)
    decays = [
        jnp.exp(jnp.where(low, cum[:, h : h + 1] - cum_t[h : h + 1, :], NEG)) for h in range(HL)
    ]
    return cum, decays


def causal(c, scores):
    t = c * CH + lax.broadcasted_iota(jnp.int32, scores.shape, 0)
    s = lax.broadcasted_iota(jnp.int32, scores.shape, 1)
    return jnp.where(s <= t, scores, NEG)


def mixer_forward_kernel(proj, small_ref, mix, y_out, states, log_totals, keys, values):
    small = small_ref[...]
    state = jnp.zeros((HW, NS), F32)
    for c in range(NCH):
        rows = slice(c * CH, (c + 1) * CH)
        b = proj[rows, CB : CB + NS].astype(BF)
        cc = proj[rows, CC : CC + NS].astype(BF)
        z = proj[rows, CZ : CZ + HW]
        u = proj[rows, CU : CU + HW]
        _, dt, log_decay = steps(proj[rows, CR : CR + 8], small)
        cum, decays = block_decays(log_decay)
        g = dot(cc, b, ((1,), (1,)))
        v = u * widen(dt)
        vb = v.astype(BF)
        intra = [dot((m * g).astype(BF), vb) for m in decays]
        last = cum[CH - 1 : CH, :]
        y = per_head(intra, (CH, HW)) + widen(jnp.exp(cum)) * dot(
            cc, state.astype(BF), ((1,), (1,))
        )
        states[c] = state
        state = row_heads(jnp.exp(last)) * state + dot(
            (v * widen(jnp.exp(last - cum))).astype(BF), b, ((0,), (0,))
        )
        y = y + widen(jnp.broadcast_to(small[2:3, :], (CH, 8))) * u
        y_out[rows, :] = y
        mix[rows, 0:HW] = (y * z * jax.nn.sigmoid(z)).astype(BF)

        q = proj[rows, CQ : CQ + HS].astype(BF)
        keys[rows, :] = proj[rows, CK : CK + HS].astype(BF)
        values[rows, :] = proj[rows, CV : CV + HS].astype(BF)
        seen = (c + 1) * CH
        scores = causal(c, dot(q, keys[0:seen, :], ((1,), (1,))) * HS**-0.5)
        peak = jnp.max(scores, axis=1, keepdims=True)
        weights = jnp.exp(scores - peak)
        totals = jnp.sum(weights, axis=1, keepdims=True)
        probs = (weights / totals).astype(BF)
        mix[rows, HW : HW + HS] = dot(probs, values[0:seen, :]).astype(BF)
        log_totals[rows, :] = jnp.broadcast_to(peak + jnp.log(totals), (CH, 8))


def mixer_backward_kernel(
    proj, small_ref, y_in, states, log_totals, mix_grad, out, sums, keys, values, key_grad, value_grad
):
    small = small_ref[...]
    skip_w = widen(jnp.broadcast_to(small[2:3, :], (CH, 8)))
    keys[...] = proj[:, CK : CK + HS].astype(BF)
    values[...] = proj[:, CV : CV + HS].astype(BF)
    key_grad[...] = jnp.zeros_like(key_grad)
    value_grad[...] = jnp.zeros_like(value_grad)
    state_grad = jnp.zeros((HW, NS), F32)
    low = tri_lower()
    ones_low = low.astype(F32)
    lane8 = lax.broadcasted_iota(jnp.int32, (HW, 8), 1)
    row8 = lax.broadcasted_iota(jnp.int32, (HW, 8), 0)
    heads = (row8 // MP == lane8).astype(F32)
    lane_ch = lax.broadcasted_iota(jnp.int32, (CH, 8), 1)
    acc_bias = jnp.zeros((1, 8), F32)
    acc_decay = jnp.zeros((1, 8), F32)
    acc_skip = jnp.zeros((1, 8), F32)
    rate = jnp.exp(small[1:2, :])
    for c in reversed(range(NCH)):
        rows = slice(c * CH, (c + 1) * CH)
        seen = (c + 1) * CH
        q = proj[rows, CQ : CQ + HS].astype(BF)
        grad = mix_grad[rows, HW : HW + HS].astype(BF)
        scores = causal(c, dot(q, keys[0:seen, :], ((1,), (1,))) * HS**-0.5)
        probs = jnp.exp(scores - log_totals[rows, 0:1])
        prob_grad = dot(grad, values[0:seen, :], ((1,), (1,)))
        weighted = probs * prob_grad
        centre = jnp.sum(weighted, axis=1, keepdims=True)
        score_grad = (weighted - probs * centre).astype(BF)
        query_grad = dot(score_grad, keys[0:seen, :]) * HS**-0.5
        key_grad[0:seen, :] += dot(score_grad, q, ((0,), (0,)))
        value_grad[0:seen, :] += dot(probs.astype(BF), grad, ((0,), (0,)))
        out[rows, CQ : CQ + HS] = query_grad.astype(BF)
        out[rows, CK : CK + HS] = (key_grad[rows, :] * HS**-0.5).astype(BF)
        out[rows, CV : CV + HS] = value_grad[rows, :].astype(BF)

        b = proj[rows, CB : CB + NS].astype(BF)
        cc = proj[rows, CC : CC + NS].astype(BF)
        z = proj[rows, CZ : CZ + HW]
        u = proj[rows, CU : CU + HW]
        pre, dt, log_decay = steps(proj[rows, CR : CR + 8], small)
        cum, decays = block_decays(log_decay)
        last = cum[CH - 1 : CH, :]
        g = dot(cc, b, ((1,), (1,)))
        dt_w = widen(dt)
        v = u * dt_w
        vb = v.astype(BF)
        gated_grad = mix_grad[rows, 0:HW].astype(BF).astype(F32)
        gate = jax.nn.sigmoid(z)
        dy = gated_grad * z * gate
        out[rows, CZ : CZ + HW] = (
            gated_grad * y_in[rows, :] * gate * (1.0 + z * (1.0 - gate))
        ).astype(BF)
        dyb = dy.astype(BF)
        state = states[c]
        sb = state.astype(BF)
        qb = state_grad.astype(BF)
        grow = widen(jnp.exp(cum))
        fade = widen(jnp.exp(last - cum))
        v_grad_inter = fade * dot(b, qb, ((1,), (1,)))
        y_inter = grow * dot(cc, sb, ((1,), (1,)))
        g_grad = jnp.zeros((CH, CH), F32)
        v_grads = []
        cum_grad = jnp.zeros((CH, 8), F32)
        for h in range(HL):
            pair = dot(jnp.where(head_mask(h, (CH, HW)), dyb, jnp.zeros_like(dyb)), vb, ((1,), (1,)))
            mixed_pair = decays[h] * pair
            g_grad = g_grad + mixed_pair
            v_grads.append(dot((decays[h] * g).astype(BF), dyb, ((0,), (0,))))
            swing = (mixed_pair * g).astype(BF)
            one = (lane_ch == h).astype(BF)
            cum_grad = cum_grad + dot(swing, one) - dot(swing, one, ((0,), (0,)))
        v_grad = per_head(v_grads, (CH, HW)) + v_grad_inter
        g_gradb = g_grad.astype(BF)
        grown = (grow * dy).astype(BF)
        out[rows, CC : CC + NS] = (dot(g_gradb, b) + dot(grown, sb)).astype(BF)
        out[rows, CB : CB + NS] = (
            dot(g_gradb, cc, ((0,), (0,))) + dot((fade * v).astype(BF), qb)
        ).astype(BF)
        out[rows, CU : CU + HW] = (skip_w * dy + dt_w * v_grad).astype(BF)
        per_state = dot(heads, state * state_grad, ((0,), (0,)), precision=HIGH)
        over = dot(jnp.ones((8, NS), F32), per_state, ((1,), (1,)), precision=HIGH)[0:1, :]
        behind = dot(v * v_grad_inter, heads, precision=HIGH)
        ahead = cum_grad + dot(dy * y_inter, heads, precision=HIGH)
        decay_grad = (
            dot(ones_low, ahead, ((0,), (0,)), precision=HIGH)
            + dot(ones_low, behind, precision=HIGH)
            - behind
            + jnp.exp(last) * over
        )
        step_grad = dot(u * v_grad, heads, precision=HIGH) - rate * decay_grad
        r_grad = step_grad * jax.nn.sigmoid(pre)
        out[rows, CR : CR + HS] = jnp.concatenate(
            [r_grad, jnp.zeros((CH, HS - 8), F32)], axis=1
        ).astype(BF)
        acc_bias = acc_bias + jnp.sum(r_grad, axis=0, keepdims=True)
        acc_decay = acc_decay - rate * jnp.sum(dt * decay_grad, axis=0, keepdims=True)
        acc_skip = acc_skip + dot(
            jnp.broadcast_to(jnp.sum(dy * u, axis=0, keepdims=True), (8, HW)), heads, precision=HIGH
        )[0:1, :]
        state_grad = row_heads(jnp.exp(last)) * state_grad + dot(grown, cc, ((0,), (0,)))
    sums[...] = jnp.concatenate([acc_bias, acc_decay, acc_skip, jnp.zeros((5, 8), F32)], axis=0)


VMEM = pl.BlockSpec(memory_space=pltpu.VMEM)
PARAMS = pltpu.CompilerParams(vmem_limit_bytes=50 * 1024 * 1024)


def mixer_forward(proj, small):
    return pl.pallas_call(
        mixer_forward_kernel,
        out_shape=(
            jax.ShapeDtypeStruct((TOK, HW + HS), BF),
            jax.ShapeDtypeStruct((TOK, HW), F32),
            jax.ShapeDtypeStruct((NCH, HW, NS), F32),
            jax.ShapeDtypeStruct((TOK, 8), F32),
        ),
        in_specs=[VMEM] * 2,
        out_specs=(VMEM,) * 4,
        scratch_shapes=[pltpu.VMEM((TOK, HS), BF), pltpu.VMEM((TOK, HS), BF)],
        compiler_params=PARAMS,
    )(proj, small)


def mixer_backward(proj, small, y, states, log_totals, mix_grad):
    return pl.pallas_call(
        mixer_backward_kernel,
        out_shape=(jax.ShapeDtypeStruct((TOK, CW), BF), jax.ShapeDtypeStruct((8, 8), F32)),
        in_specs=[VMEM] * 6,
        out_specs=(VMEM,) * 2,
        scratch_shapes=[
            pltpu.VMEM((TOK, HS), BF),
            pltpu.VMEM((TOK, HS), BF),
            pltpu.VMEM((TOK, HS), F32),
            pltpu.VMEM((TOK, HS), F32),
        ],
        compiler_params=PARAMS,
    )(proj, small, y, states, log_totals, mix_grad)


def mixer_shares(mixer_w, attn_w):
    z = mixer_w[:, :INNER].reshape(ROWS, SEQ, HW).swapaxes(0, 1)
    u = mixer_w[:, INNER : 2 * INNER].reshape(ROWS, SEQ, HW).swapaxes(0, 1)
    both = jnp.broadcast_to(mixer_w[None, :, 2 * INNER : 2 * INNER + 2 * NS], (SEQ, ROWS, 2 * NS))
    r = mixer_w[:, 2 * INNER + 2 * NS :].reshape(ROWS, SEQ, HL).swapaxes(0, 1)
    q = attn_w[:, : QH * HS].reshape(ROWS, SEQ, HS).swapaxes(0, 1)

    def kv(w):
        w = w.reshape(ROWS, KVH, HS).swapaxes(0, 1)
        return jnp.repeat(w, SEQ // KVH, axis=0)

    k = kv(attn_w[:, QH * HS : QH * HS + KVH * HS])
    v = kv(attn_w[:, QH * HS + KVH * HS :])
    pad = jnp.zeros((SEQ, ROWS, CW - CR - HL), mixer_w.dtype)
    return jnp.concatenate([both, z, q, u, k, v, r, pad], axis=2)


def mixer_rows(shares):
    n = shares.shape[1]
    flat = lambda v: v.swapaxes(0, 1).reshape(n, -1)

    def kv(v):
        return flat(v.reshape(KVH, SEQ // KVH, n, HS).sum(1))

    both = shares[:, :, : 2 * NS].sum(0)
    mixer = [
        flat(shares[:, :, CZ : CZ + HW]),
        flat(shares[:, :, CU : CU + HW]),
        both,
        flat(shares[:, :, CR : CR + HL]),
    ]
    attn = [
        flat(shares[:, :, CQ : CQ + HS]),
        kv(shares[:, :, CK : CK + HS]),
        kv(shares[:, :, CV : CV + HS]),
    ]
    sums = shares[:, :, CR + 8 : CR + 8 + 3 * HL].sum(0)
    return jnp.concatenate(mixer + attn + [sums], axis=1)


def unit_rows(x):
    return x * lax.rsqrt(jnp.mean(x * x, axis=-1, keepdims=True) + EPS)


def unit_back(x, e):
    rho = lax.rsqrt(jnp.mean(x * x, axis=-1, keepdims=True) + EPS)
    return rho * e - x * (rho * rho * rho) * jnp.mean(x * e, axis=-1, keepdims=True)


def local(
    inputs, cotangent, mixer_in, attn_in, mamba_out, attn_out, gate_up, down_proj,
    norm_gains, step_bias, decay_log, skip_gain,
):
    me = lax.axis_index("seq")
    x0 = inputs[0]
    gains = norm_gains[0].astype(F32)
    g1, g2 = gains[0][:, None], gains[1][:, None]
    mixer_f = mixer_in[0].astype(F32)
    attn_f = attn_in[0].astype(F32)
    gate_up_f = gate_up[0].astype(F32)
    down_w = down_proj[0]
    out_w = jnp.concatenate([mamba_out[0], attn_out[0]], axis=0)
    small = jnp.zeros((8, 8), F32)
    small = small.at[0, :HL].set(step_bias[0].astype(F32))
    small = small.at[1, :HL].set(decay_log[0].astype(F32))
    small = small.at[2, :HL].set(skip_gain[0].astype(F32))

    shares = mixer_shares((mixer_f * g1).astype(BF), (attn_f * g1).astype(BF))
    in_w = lax.all_to_all(shares, "seq", split_axis=0, concat_axis=0, tiled=True).reshape(D, CW)
    x_all = gather_rows(x0)
    unit_one = unit_rows(x_all.astype(F32)).astype(BF)
    proj = dot(unit_one, in_w)
    mix, y, states, log_totals = mixer_forward(proj, small)
    mid = scatter_rows(dot(mix, out_w).astype(BF)) + x0.astype(F32)

    gu = (gate_up_f * g2).astype(BF).reshape(ROWS, 2, SEQ, FL).transpose(2, 0, 1, 3)
    gu_w = lax.all_to_all(gu, "seq", split_axis=0, concat_axis=0, tiled=True).reshape(D, 2 * FL)
    ffn_grad = lax.all_gather(cotangent[0], "seq", axis=0, tiled=True)
    unit_two = gather_rows(unit_rows(mid).astype(BF))
    gate_rows = dot(unit_two, gu_w)
    gate, wide = gate_rows[:, :FL], gate_rows[:, FL:]
    s = jax.nn.sigmoid(gate)
    act = (gate * s * wide).astype(BF)
    act_grad = dot(ffn_grad, down_w, ((1,), (1,))).astype(BF).astype(F32)
    up_grad = jnp.concatenate(
        [act_grad * wide * s * (1.0 + gate * (1.0 - s)), act_grad * gate * s], axis=1
    ).astype(BF)
    mid_e = scatter_rows(dot(up_grad, gu_w, ((1,), (1,))).astype(BF))
    mid_grad = cotangent[0].astype(F32) + unit_back(mid, mid_e)
    branch = gather_rows(mid_grad.astype(BF))

    result = lax.psum_scatter(
        dot(act, down_w).astype(BF), "seq", scatter_dimension=0, tiled=True
    ).astype(F32)
    outputs = (mid + result).astype(BF)
    down_grad = dot(act, ffn_grad, ((0,), (0,))).astype(BF)
    gu_grad = dot(unit_two, up_grad, ((0,), (0,))).astype(BF)
    gu_grad = lax.all_to_all(
        gu_grad.reshape(SEQ, ROWS, 2 * FL), "seq", split_axis=0, concat_axis=0, tiled=True
    )
    gu_grad = gu_grad.reshape(SEQ, ROWS, 2, FL).transpose(1, 2, 0, 3).reshape(ROWS * 4, D)
    ffn_sums = lax.psum(jnp.concatenate([gu_grad, down_grad], axis=0), "dp").astype(F32)
    gate_up_grad = ffn_sums[: ROWS * 4].reshape(ROWS, 2 * FF)
    down_sum = ffn_sums[ROWS * 4 :]

    mix_grad = dot(branch, out_w, ((1,), (1,)))
    out_grad = lax.psum(dot(mix, branch, ((0,), (0,))).astype(BF), "dp").astype(F32)
    proj_grad, sums = mixer_backward(proj, small, y, states, log_totals, mix_grad)
    in_grad = dot(unit_one, proj_grad, ((0,), (0,)))
    line = jnp.concatenate([sums[0, :HL], sums[1, :HL], sums[2, :HL]])[None]
    in_grad = lax.dynamic_update_slice(in_grad, line, (me * ROWS, CR + 8)).astype(BF)
    sent = in_grad.reshape(SEQ, DP, ROWS // DP, CW).swapaxes(0, 1).reshape(DP * SEQ, ROWS // DP, CW)
    got = lax.all_to_all(sent, ("dp", "seq"), split_axis=0, concat_axis=0, tiled=True)
    got = got.reshape(DP, SEQ, ROWS // DP, CW).astype(F32).sum(0)
    rows = mixer_rows(got).astype(BF)
    in_e = scatter_rows(dot(proj_grad, in_w, ((1,), (1,))).astype(BF))
    input_grad = mid_grad + unit_back(x0.astype(F32), in_e)
    rows = lax.all_gather(rows, "dp", axis=0, tiled=True).astype(F32)
    wm = 2 * INNER + 2 * NS + MH
    wa = (QH + 2 * KVH) * HS
    mixer_rows_grad = rows[:, :wm]
    attn_rows_grad = rows[:, wm : wm + wa]
    line = rows[0, wm + wa :]
    gain_one = (mixer_rows_grad * mixer_f).sum(1) + (attn_rows_grad * attn_f).sum(1)
    gain_two = (gate_up_grad * gate_up_f).sum(1)
    return (
        outputs[None],
        input_grad[None],
        (mixer_rows_grad * g1)[None],
        (attn_rows_grad * g1)[None],
        out_grad[None, :HW],
        out_grad[None, HW:],
        (gate_up_grad * g2)[None],
        down_sum[None],
        jnp.stack([gain_one, gain_two])[None],
        line[None, :HL],
        line[None, HL : 2 * HL],
        line[None, 2 * HL : 3 * HL],
    )


def solution(mesh):
    rows = P("dp", "seq", None)
    owned = P(None, "seq", None)
    heads = P(None, "seq")
    gains = P(None, None, "seq")
    return jax.shard_map(
        local,
        mesh=mesh,
        in_specs=(rows, rows) + (owned,) * 6 + (gains,) + (heads,) * 3,
        out_specs=(rows, rows) + (owned,) * 6 + (gains,) + (heads,) * 3,
        check_vma=False,
    )
```

time: 1600 us -> 576 us (0.36); the launches traced: 1580 us -> 570 us
  waiting for transfers between devices: 951 us -> 296 us
  local copies, waits for them, and re-layouts: 257 us -> 72 us
  matrix products: 160 us -> 39.8 us
  blocking collectives: 98.1 us -> 0 us
  starting transfers between devices: 38.3 us -> 90.9 us
  Pallas kernels: 0 us -> 26.8 us
  other arithmetic: 55.6 us -> 28.9 us
    all_gather x12 -> x2, waiting for transfers between devices: 749 us -> 32.5 us  [the longest x1 32.5 us: local(): rows = lax.all_gather(rows, 'dp', axis=0, tiled=True).astype(F32)]
    dot_general x63 -> x12, matrix products: 160 us -> 39.8 us  [dot(): lax.dot_general(a, b, (dims, ((), ())), precision=precision, preferred_el...]
    dynamic_update_slice x20 -> x29, local copies, waits for them, and re-layouts: 128 us -> 14.6 us  [the longest x28 14.3 us: put(): return lax.dynamic_update_slice(out, v, (at, 0))]
    all_gather x4 -> x0, blocking collectives: 82.9 us -> none  [the longest x1 36.5 us: layer_forward(): lax.all_gather(attn_rows[:, query_width:], 'seq', axis=0, tiled=True)]
    all_to_all x9 -> x7, waiting for transfers between devices: 33.8 us -> 93.2 us  [the longest x3 79.1 us: scatter_rows(): lax.all_to_all(part.reshape(SEQ, ROWS, D), 'seq', split_axis=0, concat_ax...]
    ppermute x0 -> x27, starting transfers between devices: none -> 46.7 us  [gather_rows(): send = lambda v, perm: lax.ppermute(v, 'seq', perm)]
    concatenate x2, local copies, waits for them, and re-layouts: 37.6 us -> 4.61 us  [the longest x1 3.9 us: mixer_shares(): return jnp.concatenate([both, z, q, u, k, v, r, pad], axis=2)]
    ppermute x0 -> x27, waiting for transfers between devices: none -> 31.3 us  [gather_rows(): send = lambda v, perm: lax.ppermute(v, 'seq', perm)]
  transfers between devices with their start and end apart: 23 -> 38, of which waited for: 18 -> 18; matrix products, arithmetic and copies ran while one was open for 24% -> 19% of each run, Pallas kernels for 0% -> 3%
where the time goes in v1:
time: 576 us; the launch traced here: 570 us
  waiting for transfers between devices  296 us (51%)
  starting transfers between devices  90.9 us (16%)
  local copies, waits for them, and re-layouts  72 us (12%)
  matrix products  39.8 us (7%)
  other arithmetic  28.9 us (5%)
  Pallas kernels  26.8 us (5%)
  between operations  15.2 us (3%)
    psum x1, waiting for transfers between devices, local(): lax.psum(dot(mix, branch, ((0,), (0,))).astype(BF), 'dp').astype(F32)  109 us
    all_to_all x3, waiting for transfers between devices, scatter_rows(): lax.all_to_all(part.reshape(SEQ, ROWS, D), 'seq', split_axis=0, concat_ax...  79.1 us
    ppermute x27, starting transfers between devices, gather_rows(): send = lambda v, perm: lax.ppermute(v, 'seq', perm)  46.7 us
    dot_general x12, matrix products, dot(): lax.dot_general(a, b, (dims, ((), ())), precision=precision, preferred_el...  39.8 us
    all_gather x1, waiting for transfers between devices, local(): rows = lax.all_gather(rows, 'dp', axis=0, tiled=True).astype(F32)  32.5 us
    ppermute x27, waiting for transfers between devices, gather_rows(): send = lambda v, perm: lax.ppermute(v, 'seq', perm)  31.3 us
    reduce_scatter x1, waiting for transfers between devices, local(): lax.psum_scatter(dot(act, down_w).astype(BF), 'seq', scatter_dimension=0,...  29.4 us
    pallas_call x1, Pallas kernels, mixer_backward(): pl.pallas_call(mixer_backward_kernel, out_shape=(jax.ShapeDtypeStruct((TO...  18.9 us
  transfers between devices with their start and end apart: 38, of which 18 were waited for; matrix products, arithmetic and copies ran while one was open for 19% of the time, Pallas kernels for 3%

profile of v1, /device:TPU:1, one launch (start us, length us, event | category | flops | bytes accessed | tf_op | source)
XLA Modules:
  0.0 570.0 jit_solution(3994626756763478805)
XLA Ops:
  16.8 3.9 concatenate.26
  20.7 4.5 all-to-all-start
  36.4 11.3 %collective-permute-done.3 = bf16[64,1024]{1,0:T(8,128)(2,1)S(1)} collective-permute-done((bf16[64,1024]{1,0:T(8,128)(2,1)S(1)}, bf16[64,1024]{1,0:T(8,128)(2,1)S(1)}, u32[]{:S(2)}, u32[]{:S(2)}) %collective-permute-start.3) | collective-permute-done | bytes 131104 | tf_op jit(solution)/shard_map/ppermute | solution.py:49
  47.7 4.8 collective-permute-start.7
  52.7 3.2 collective-permute-done.5
  58.2 5.7 fusion.27.proj
  63.8 7.9 %shard_map.211 = (bf16[1024,256]{1,0:T(8,128)(2,1)S(1)}, f32[1024,192]{1,0:T(8,128)S(1)}, f32[4,192,128]{2,1,0:T(8,128)S(1)}, f32[1024,8]{1,0:T(8,128)S(1)}) custom-call(f32[1024,896]{1,0:T(8,128)} %fusion.27.proj, f32[8,8]{1,0:T(8,128)S(1)} %scatter.20.small_ref), custom_call_target="tpu_custom_call" | custom-call | tf_op jit(solution)/shard_map/pallas_call | solution.py:272
  73.8 4.5 all-to-all-start.1
  83.9 21.3 %all-to-all-done.1 = bf16[8,128,1024]{2,1,0:T(8,128)(2,1)} async-done(((bf16[8,128,1024]{2,1,0:T(8,128)(2,1)}), bf16[8,128,1024]{2,1,0:T(8,128)(2,1)}, u32[]{:S(2)}, u32[]{:S(2)}) %all-to-all-start.1) | async-done | bytes 2097184 | tf_op jit(solution)/shard_map/all_to_all | solution.py:69
  105.2 8.5 %all-to-all-start.2 = ((bf16[8,128,2,256]{1,3,2,0:T(8,128)(2,1)}), bf16[8,128,2,256]{1,3,2,0:T(8,128)(2,1)}, u32[]{:S(2)}, u32[]{:S(2)}) async-start(bf16[8,128,2,256]{1,3,2,0:T(8,128)(2,1)} %copy.145), calls=%async_computation.2 | async-start | bytes 2097152 | tf_op jit(solution)/shard_map/all_to_all | solution.py:379
  123.9 8.6 %all-to-all-done.2 = bf16[8,128,2,256]{1,3,2,0:T(8,128)(2,1)} async-done(((bf16[8,128,2,256]{1,3,2,0:T(8,128)(2,1)}), bf16[8,128,2,256]{1,3,2,0:T(8,128)(2,1)}, u32[]{:S(2)}, u32[]{:S(2)}) %all-to-all-start.2) | async-done | bytes 1048608 | tf_op jit(solution)/shard_map/all_to_all | solution.py:379
  135.7 5.5 collective-permute-start.12
  145.6 3.8 collective-permute-done.9
  157.9 4.4 collective-permute-done.15
  169.1 4.3 fusion.16
  177.3 4.0 convolution_convert_fusion.1
  181.4 5.2 all-to-all-start.3
  186.5 33.6 %all-to-all-done.3 = bf16[8,128,1024]{2,1,0:T(8,128)(2,1)} async-done(((bf16[8,128,1024]{2,1,0:T(8,128)(2,1)}), bf16[8,128,1024]{2,1,0:T(8,128)(2,1)}, u32[]{:S(2)}, u32[]{:S(2)}) %all-to-all-start.3) | async-done | bytes 2097184 | tf_op jit(solution)/shard_map/all_to_all | solution.py:69
  222.9 29.4 %reduce-scatter.2.cloned.1.call-done = bf16[128,1024]{1,0:T(8,128)(2,1)} async-done(((bf16[1024,1024]{1,0:T(8,128)(2,1)}), bf16[128,1024]{1,0:T(8,128)(2,1)}) %reduce-scatter.2.cloned.1.call-update) | async-done | bytes 262160 | tf_op jit(solution)/shard_map/reduce_scatter | solution.py:394
  261.1 4.2 all-to-all-start.6
  278.0 4.8 collective-permute-start.25
  291.8 18.9 %shard_map.212 = (bf16[1024,896]{1,0:T(8,128)(2,1)}, f32[8,8]{1,0:T(8,128)S(1)}) custom-call(f32[1024,896]{1,0:T(8,128)} %fusion.27.proj, f32[8,8]{1,0:T(8,128)S(1)} %scatter.20.small_ref, f32[1024,192]{1,0:T(8,128)S(1)} %get-tuple-element.55.y_in, f32[4,192,128]{2,1,0:T(8,128)S(1)} %get-tuple-element.56.states, f32[1024,8]{1,0:T(8,128)S(1)} %get-tuple-element.57.log_totals, ...), custom_call_target="tpu_custom_call" | custom-call | tf_op jit(solution)/shard_map/pallas_call | solution.py:288
  310.7 4.0 fusion.25
  316.5 12.5 %all-to-all-start.5 = ((bf16[128,8,896]{2,1,0:T(8,128)(2,1)}), bf16[128,8,896]{2,1,0:T(8,128)(2,1)S(1)}, u32[]{:S(2)}, u32[]{:S(2)}) async-start(bf16[128,8,896]{2,1,0:T(8,128)(2,1)} %bitcast.39), calls=%async_computation.6 | async-start | bytes 3670016 | tf_op jit(solution)/shard_map/all_to_all | solution.py:415
  329.0 3.3 fusion.11
  334.4 3.4 copy.172
  344.6 5.7 %convolution_convert_fusion = bf16[1024,1024]{1,0:T(8,128)(2,1)} fusion(bf16[1024,896]{1,0:T(8,128)(2,1)} %get-tuple-element.58, bf16[1024,896]{1,0:T(8,128)(2,1)} %bitcast.17), kind=kOutput, calls=%fused_computation.16 | convolution fusion | flops 1880096768 | bytes 5767168 | tf_op jit(solution)/shard_map/dot_general | solution.py:35
  350.4 5.4 all-to-all-done.5
  357.1 4.5 all-to-all-start.4
  368.8 24.3 %all-to-all-done.4 = bf16[8,128,1024]{2,1,0:T(8,128)(2,1)} async-done(((bf16[8,128,1024]{2,1,0:T(8,128)(2,1)}), bf16[8,128,1024]{2,1,0:T(8,128)(2,1)}, u32[]{:S(2)}, u32[]{:S(2)}) %all-to-all-start.4) | async-done | bytes 2097184 | tf_op jit(solution)/shard_map/all_to_all | solution.py:69
  396.5 109.3 %all-reduce.4.cloned.1.call-done = (bf16[256,1024]{1,0:T(8,128)(2,1)}, bf16[768,1024]{1,0:T(8,128)(2,1)}) async-done(((bf16[256,1024]{1,0:T(8,128)(2,1)}, bf16[768,1024]{1,0:T(8,128)(2,1)}), (bf16[256,1024]{1,0:T(8,128)(2,1)}, bf16[768,1024]{1,0:T(8,128)(2,1)})) %all-reduce.4.cloned.1.call-update) | async-done | bytes 2097168 | tf_op jit(solution)/shard_map/psum | solution.py:409
  522.4 32.5 %all-gather.4.cloned.1.call-done = bf16[128,4129]{1,0:T(8,128)(2,1)} async-done(((bf16[8,4129]{1,0:T(8,128)(2,1)}), bf16[128,4129]{1,0:T(8,128)(2,1)}) %all-gather.4.cloned.1.call-update) | async-done | bytes 1057040 | tf_op jit(solution)/shard_map/all_gather | solution.py:420
  (295 shorter events, 147.9 us)
Async XLA Ops:
  7.2 23.6 %collective-permute-start = (bf16[128,1024]{1,0:T(8,128)(2,1)}, bf16[128,1024]{1,0:T(8,128)(2,1)}, u32[]{:S(2)}, u32[]{:S(2)}) collective-permute-start(bf16[128,1024]{1,0:T(8,128)(2,1)} %bitcast.171), channel_id=1, source_target_pairs={{0,1},{1,0},{2,3},{3,2},{4,5},{5,4},{6,7},{7,6},{8,9},{9,8},{10,11... | collective-permute-start | bytes 786440 | tf_op jit(solution)/shard_map/ppermute | solution.py:49
  9.8 16.4 %collective-permute-start.1 = (bf16[128,1024]{1,0:T(8,128)(2,1)}, bf16[128,1024]{1,0:T(8,128)(2,1)}, u32[]{:S(2)}, u32[]{:S(2)}) collective-permute-start(bf16[128,1024]{1,0:T(8,128)(2,1)} %bitcast.172), channel_id=1, source_target_pairs={{0,2},{1,3},{2,4},{3,5},{4,6},{5,7},{6,0},{7,1},{8,10},{9,11},{10,... | collective-permute-start | bytes 786440 | tf_op jit(solution)/shard_map/ppermute | solution.py:49
  11.0 17.5 %collective-permute-start.2 = (bf16[128,1024]{1,0:T(8,128)(2,1)}, bf16[128,1024]{1,0:T(8,128)(2,1)}, u32[]{:S(2)}, u32[]{:S(2)}) collective-permute-start(bf16[128,1024]{1,0:T(8,128)(2,1)} %bitcast.173), channel_id=1, source_target_pairs={{0,6},{1,7},{2,0},{3,1},{4,2},{5,3},{6,4},{7,5},{8,14},{9,15},{10,... | collective-permute-start | bytes 786440 | tf_op jit(solution)/shard_map/ppermute | solution.py:49
  20.7 36.6 %all-to-all-start = ((bf16[8,128,896]{2,1,0:T(8,128)(2,1)}), bf16[8,128,896]{2,1,0:T(8,128)(2,1)}, u32[]{:S(2)}, u32[]{:S(2)}) async-start(bf16[8,128,896]{2,1,0:T(8,128)(2,1)} %concatenate.26), calls=%async_computation | async-start | bytes 3670016 | tf_op jit(solution)/shard_map/all_to_all | solution.py:371
  27.0 20.6 %collective-permute-start.3 = (bf16[64,1024]{1,0:T(8,128)(2,1)S(1)}, bf16[64,1024]{1,0:T(8,128)(2,1)S(1)}, u32[]{:S(2)}, u32[]{:S(2)}) collective-permute-start(bf16[64,1024]{1,0:T(8,128)(2,1)S(1)} %slice.215), channel_id=1, source_target_pairs={{0,2},{1,3},{2,4},{3,5},{4,6},{5,7},{6,0},{7,1},{8,10},{9,11},{10,... | collective-permute-start | bytes 393224 | tf_op jit(solution)/shard_map/ppermute | solution.py:49
  29.4 23.2 %collective-permute-start.4 = (bf16[64,1024]{1,0:T(8,128)(2,1)S(1)}, bf16[64,1024]{1,0:T(8,128)(2,1)S(1)}, u32[]{:S(2)}, u32[]{:S(2)}) collective-permute-start(bf16[64,1024]{1,0:T(8,128)(2,1)S(1)} %slice.216), channel_id=1, source_target_pairs={{0,6},{1,7},{2,0},{3,1},{4,2},{5,3},{6,4},{7,5},{8,14},{9,15},{10,... | collective-permute-start | bytes 393224 | tf_op jit(solution)/shard_map/ppermute | solution.py:49
  30.8 25.1 %collective-permute-start.5 = (bf16[128,1024]{1,0:T(8,128)(2,1)}, bf16[128,1024]{1,0:T(8,128)(2,1)S(1)}, u32[]{:S(2)}, u32[]{:S(2)}) collective-permute-start(bf16[128,1024]{1,0:T(8,128)(2,1)} %collective-permute-done), channel_id=1, source_target_pairs={{0,2},{1,3},{2,4},{3,5},{4,6},{5,7},{6,0},{7,1},{8,10},{9,11},{10,... | collective-permute-start | bytes 786440 | tf_op jit(solution)/shard_map/ppermute | solution.py:49
  30.9 25.0 %collective-permute-start.6 = (bf16[128,1024]{1,0:T(8,128)(2,1)}, bf16[128,1024]{1,0:T(8,128)(2,1)S(1)}, u32[]{:S(2)}, u32[]{:S(2)}) collective-permute-start(bf16[128,1024]{1,0:T(8,128)(2,1)} %collective-permute-done), channel_id=1, source_target_pairs={{0,6},{1,7},{2,0},{3,1},{4,2},{5,3},{6,4},{7,5},{8,14},{9,15},{10,... | collective-permute-start | bytes 786440 | tf_op jit(solution)/shard_map/ppermute | solution.py:49
  73.8 31.4 %all-to-all-start.1 = ((bf16[8,128,1024]{2,1,0:T(8,128)(2,1)}), bf16[8,128,1024]{2,1,0:T(8,128)(2,1)}, u32[]{:S(2)}, u32[]{:S(2)}) async-start(bf16[8,128,1024]{2,1,0:T(8,128)(2,1)} %bitcast.174), calls=%async_computation.1 | async-start | bytes 4194304 | tf_op jit(solution)/shard_map/all_to_all | solution.py:69
  78.3 90.9 %all-gather.6.cloned.1.call-start = ((), (), s32[]{:S(2)}) async-start(), calls=%async_computation.10 | async-start | bytes 2359296 | tf_op jit(solution)/shard_map/all_gather | solution.py:380
  105.2 27.3 %all-to-all-start.2 = ((bf16[8,128,2,256]{1,3,2,0:T(8,128)(2,1)}), bf16[8,128,2,256]{1,3,2,0:T(8,128)(2,1)}, u32[]{:S(2)}, u32[]{:S(2)}) async-start(bf16[8,128,2,256]{1,3,2,0:T(8,128)(2,1)} %copy.145), calls=%async_computation.2 | async-start | bytes 2097152 | tf_op jit(solution)/shard_map/all_to_all | solution.py:379
  113.7 138.6 %reduce-scatter.2.cloned.1.call-start = ((), (), s32[]{:S(2)}) async-start(), calls=%async_computation.8 | async-start | bytes 2359296 | tf_op jit(solution)/shard_map/reduce_scatter | solution.py:394
  119.8 14.8 %collective-permute-start.10 = (bf16[128,1024]{1,0:T(8,128)(2,1)}, bf16[128,1024]{1,0:T(8,128)(2,1)}, u32[]{:S(2)}, u32[]{:S(2)}) collective-permute-start(bf16[128,1024]{1,0:T(8,128)(2,1)} %get-tuple-element.141), channel_id=1, source_target_pairs={{0,2},{1,3},{2,4},{3,5},{4,6},{5,7},{6,0},{7,1},{8,10},{9,11},{10,... | collective-permute-start | bytes 786440 | tf_op jit(solution)/shard_map/ppermute | solution.py:49
  121.3 20.6 %collective-permute-start.11 = (bf16[128,1024]{1,0:T(8,128)(2,1)}, bf16[128,1024]{1,0:T(8,128)(2,1)}, u32[]{:S(2)}, u32[]{:S(2)}) collective-permute-start(bf16[128,1024]{1,0:T(8,128)(2,1)} %get-tuple-element.141), channel_id=1, source_target_pairs={{0,6},{1,7},{2,0},{3,1},{4,2},{5,3},{6,4},{7,5},{8,14},{9,15},{10,... | collective-permute-start | bytes 786440 | tf_op jit(solution)/shard_map/ppermute | solution.py:49
  122.5 26.9 %collective-permute-start.9 = (bf16[128,1024]{1,0:T(8,128)(2,1)}, bf16[128,1024]{1,0:T(8,128)(2,1)}, u32[]{:S(2)}, u32[]{:S(2)}) collective-permute-start(bf16[128,1024]{1,0:T(8,128)(2,1)} %get-tuple-element.141), channel_id=1, source_target_pairs={{0,1},{1,0},{2,3},{3,2},{4,5},{5,4},{6,7},{7,6},{8,9},{9,8},{10,11... | collective-permute-start | bytes 786440 | tf_op jit(solution)/shard_map/ppermute | solution.py:49
  135.7 19.3 %collective-permute-start.12 = (bf16[64,1024]{1,0:T(8,128)(2,1)S(1)}, bf16[64,1024]{1,0:T(8,128)(2,1)S(1)}, u32[]{:S(2)}, u32[]{:S(2)}) collective-permute-start(bf16[64,1024]{1,0:T(8,128)(2,1)S(1)} %slice.224), channel_id=1, source_target_pairs={{0,2},{1,3},{2,4},{3,5},{4,6},{5,7},{6,0},{7,1},{8,10},{9,11},{10,... | collective-permute-start | bytes 393224 | tf_op jit(solution)/shard_map/ppermute | solution.py:49
  142.8 14.9 %collective-permute-start.13 = (bf16[64,1024]{1,0:T(8,128)(2,1)S(1)}, bf16[64,1024]{1,0:T(8,128)(2,1)S(1)}, u32[]{:S(2)}, u32[]{:S(2)}) collective-permute-start(bf16[64,1024]{1,0:T(8,128)(2,1)S(1)} %slice.225), channel_id=1, source_target_pairs={{0,6},{1,7},{2,0},{3,1},{4,2},{5,3},{6,4},{7,5},{8,14},{9,15},{10,... | collective-permute-start | bytes 393224 | tf_op jit(solution)/shard_map/ppermute | solution.py:49
  149.4 8.4 %collective-permute-start.14 = (bf16[128,1024]{1,0:T(8,128)(2,1)}, bf16[128,1024]{1,0:T(8,128)(2,1)S(1)}, u32[]{:S(2)}, u32[]{:S(2)}) collective-permute-start(bf16[128,1024]{1,0:T(8,128)(2,1)} %collective-permute-done.9), channel_id=1, source_target_pairs={{0,2},{1,3},{2,4},{3,5},{4,6},{5,7},{6,0},{7,1},{8,10},{9,11},{10,... | collective-permute-start | bytes 786440 | tf_op jit(solution)/shard_map/ppermute | solution.py:49
  151.3 10.9 %collective-permute-start.15 = (bf16[128,1024]{1,0:T(8,128)(2,1)}, bf16[128,1024]{1,0:T(8,128)(2,1)S(1)}, u32[]{:S(2)}, u32[]{:S(2)}) collective-permute-start(bf16[128,1024]{1,0:T(8,128)(2,1)} %collective-permute-done.9), channel_id=1, source_target_pairs={{0,6},{1,7},{2,0},{3,1},{4,2},{5,3},{6,4},{7,5},{8,14},{9,15},{10,... | collective-permute-start | bytes 786440 | tf_op jit(solution)/shard_map/ppermute | solution.py:49
  181.4 38.7 %all-to-all-start.3 = ((bf16[8,128,1024]{2,1,0:T(8,128)(2,1)}), bf16[8,128,1024]{2,1,0:T(8,128)(2,1)}, u32[]{:S(2)}, u32[]{:S(2)}) async-start(bf16[8,128,1024]{2,1,0:T(8,128)(2,1)} %bitcast.179), calls=%async_computation.4 | async-start | bytes 4194304 | tf_op jit(solution)/shard_map/all_to_all | solution.py:69
  256.1 13.1 %collective-permute-start.18 = (bf16[128,1024]{1,0:T(8,128)(2,1)}, bf16[128,1024]{1,0:T(8,128)(2,1)}, u32[]{:S(2)}, u32[]{:S(2)}) collective-permute-start(bf16[128,1024]{1,0:T(8,128)(2,1)} %get-tuple-element.139), channel_id=1, source_target_pairs={{0,1},{1,0},{2,3},{3,2},{4,5},{5,4},{6,7},{7,6},{8,9},{9,8},{10,11... | collective-permute-start | bytes 786440 | tf_op jit(solution)/shard_map/ppermute | solution.py:49
  256.1 9.3 %collective-permute-start.19 = (bf16[128,1024]{1,0:T(8,128)(2,1)}, bf16[128,1024]{1,0:T(8,128)(2,1)S(1)}, u32[]{:S(2)}, u32[]{:S(2)}) collective-permute-start(bf16[128,1024]{1,0:T(8,128)(2,1)} %get-tuple-element.139), channel_id=1, source_target_pairs={{0,2},{1,3},{2,4},{3,5},{4,6},{5,7},{6,0},{7,1},{8,10},{9,11},{10,... | collective-permute-start | bytes 786440 | tf_op jit(solution)/shard_map/ppermute | solution.py:49
  261.1 55.4 %all-to-all-start.6 = ((bf16[8,128,512]{2,1,0:T(8,128)(2,1)}), bf16[8,128,512]{2,1,0:T(8,128)(2,1)}, u32[]{:S(2)}, u32[]{:S(2)}) async-start(bf16[8,128,512]{2,1,0:T(8,128)(2,1)} %bitcast.185), calls=%async_computation.7 | async-start | bytes 2097152 | tf_op jit(solution)/shard_map/all_to_all | solution.py:400
  265.4 12.5 %collective-permute-start.21 = (bf16[64,1024]{1,0:T(8,128)(2,1)S(1)}, bf16[64,1024]{1,0:T(8,128)(2,1)S(1)}, u32[]{:S(2)}, u32[]{:S(2)}) collective-permute-start(bf16[64,1024]{1,0:T(8,128)(2,1)S(1)} %slice.228), channel_id=1, source_target_pairs={{0,2},{1,3},{2,4},{3,5},{4,6},{5,7},{6,0},{7,1},{8,10},{9,11},{10,... | collective-permute-start | bytes 393224 | tf_op jit(solution)/shard_map/ppermute | solution.py:49
  267.7 15.7 %collective-permute-start.22 = (bf16[64,1024]{1,0:T(8,128)(2,1)S(1)}, bf16[64,1024]{1,0:T(8,128)(2,1)S(1)}, u32[]{:S(2)}, u32[]{:S(2)}) collective-permute-start(bf16[64,1024]{1,0:T(8,128)(2,1)S(1)} %slice.229), channel_id=1, source_target_pairs={{0,6},{1,7},{2,0},{3,1},{4,2},{5,3},{6,4},{7,5},{8,14},{9,15},{10,... | collective-permute-start | bytes 393224 | tf_op jit(solution)/shard_map/ppermute | solution.py:49
  269.2 17.5 %collective-permute-start.23 = (bf16[128,1024]{1,0:T(8,128)(2,1)}, bf16[128,1024]{1,0:T(8,128)(2,1)S(1)}, u32[]{:S(2)}, u32[]{:S(2)}) collective-permute-start(bf16[128,1024]{1,0:T(8,128)(2,1)} %collective-permute-done.18), channel_id=1, source_target_pairs={{0,2},{1,3},{2,4},{3,5},{4,6},{5,7},{6,0},{7,1},{8,10},{9,11},{10,... | collective-permute-start | bytes 786440 | tf_op jit(solution)/shard_map/ppermute | solution.py:49
  269.3 18.1 %collective-permute-start.24 = (bf16[128,1024]{1,0:T(8,128)(2,1)}, bf16[128,1024]{1,0:T(8,128)(2,1)S(1)}, u32[]{:S(2)}, u32[]{:S(2)}) collective-permute-start(bf16[128,1024]{1,0:T(8,128)(2,1)} %collective-permute-done.18), channel_id=1, source_target_pairs={{0,6},{1,7},{2,0},{3,1},{4,2},{5,3},{6,4},{7,5},{8,14},{9,15},{10,... | collective-permute-start | bytes 786440 | tf_op jit(solution)/shard_map/ppermute | solution.py:49
  278.0 10.1 %collective-permute-start.25 = (bf16[64,1024]{1,0:T(8,128)(2,1)S(1)}, bf16[64,1024]{1,0:T(8,128)(2,1)S(1)}, u32[]{:S(2)}, u32[]{:S(2)}) collective-permute-start(bf16[64,1024]{1,0:T(8,128)(2,1)S(1)} %collective-permute-done.21), channel_id=1, source_target_pairs={{0,1},{1,0},{2,3},{3,2},{4,5},{5,4},{6,7},{7,6},{8,9},{9,8},{10,11... | collective-permute-start | bytes 393224 | tf_op jit(solution)/shard_map/ppermute | solution.py:49
  316.5 39.3 %all-to-all-start.5 = ((bf16[128,8,896]{2,1,0:T(8,128)(2,1)}), bf16[128,8,896]{2,1,0:T(8,128)(2,1)S(1)}, u32[]{:S(2)}, u32[]{:S(2)}) async-start(bf16[128,8,896]{2,1,0:T(8,128)(2,1)} %bitcast.39), calls=%async_computation.6 | async-start | bytes 3670016 | tf_op jit(solution)/shard_map/all_to_all | solution.py:415
  329.0 176.8 %all-reduce.4.cloned.1.call-start = ((), (), s32[]{:S(2)}) async-start(), calls=%async_computation.11 | async-start | bytes 4194304 | tf_op jit(solution)/shard_map/psum | solution.py:409
  357.1 36.0 %all-to-all-start.4 = ((bf16[8,128,1024]{2,1,0:T(8,128)(2,1)}), bf16[8,128,1024]{2,1,0:T(8,128)(2,1)}, u32[]{:S(2)}, u32[]{:S(2)}) async-start(bf16[8,128,1024]{2,1,0:T(8,128)(2,1)} %bitcast.178), calls=%async_computation.5 | async-start | bytes 4194304 | tf_op jit(solution)/shard_map/all_to_all | solution.py:69
  361.6 193.3 %all-gather.4.cloned.1.call-start = ((), (), s32[]{:S(2)}) async-start(), calls=%async_computation.9 | async-start | bytes 1148928 | tf_op jit(solution)/shard_map/all_gather | solution.py:420
  (53 other events, 661.0 us)
Sparse Core Ops, SparseCore 0:
  80.8 81.4 all-gather.5
  176.5 75.8 reduce-scatter.1
  344.8 160.9 all-reduce.3
  508.1 46.7 all-gather.3

commit v2 on v1

--- a/solution.py
+++ b/solution.py
@@ -42,32 +42,54 @@
 Z_SWAP = [(i, i ^ 1) for i in range(SEQ)]
 
 
-def gather_rows(x):
-    me = lax.axis_index("seq")
-    mx, mz = me // 2, me % 2
+PLACES = (
+    (0, 0, 0), (0, 1, 0), (3, 0, 0), (1, 0, 0), (2, 0, 0), (2, 0, 64), (3, 1, 0), (1, 1, 0), (2, 1, 0), (2, 1, 64),
+)
+
+
+def gather_pieces(x):
     h = x.shape[0] // 2
     send = lambda v, perm: lax.ppermute(v, "seq", perm)
     z, a, b = send(x, Z_SWAP), send(x, x_shift(1)), send(x, x_shift(-1))
     c0, c1 = send(a[:h], x_shift(1)), send(b[h:], x_shift(-1))
     za, zb = send(z, x_shift(1)), send(z, x_shift(-1))
     zc0, zc1 = send(c0, Z_SWAP), send(c1, Z_SWAP)
-    out = jnp.zeros((TOK, x.shape[1]), x.dtype)
-
-    def put(out, v, dx, other, off):
-        at = ((mx + dx) % 4 * 2 + (1 - mz if other else mz)) * ROWS + off
-        return lax.dynamic_update_slice(out, v, (at, 0))
-
-    for v, dx, other, off in (
-        (x, 0, 0, 0), (z, 0, 1, 0), (a, 3, 0, 0), (b, 1, 0, 0), (c0, 2, 0, 0), (c1, 2, 0, h),
-        (za, 3, 1, 0), (zb, 1, 1, 0), (zc0, 2, 1, 0), (zc1, 2, 1, h),
-    ):
-        out = put(out, v, dx, other, off)
-    return out
-
-
-def scatter_rows(part):
+    return x, z, a, b, c0, c1, za, zb, zc0, zc1
+
+
+def piece_row(me, place):
+    dx, other, off = place
+    mx, mz = me // 2, me % 2
+    mz = 1 - mz if other else mz
+    return pl.multiple_of(((mx + dx) % 4 * 2 + mz) * ROWS + off, 64)
+
+
+def scatter_rows(part, beside=()):
     got = lax.all_to_all(part.reshape(SEQ, ROWS, D), "seq", split_axis=0, concat_axis=0, tiled=True)
-    return got.astype(F32).sum(0)
+    if not beside:
+        return got.astype(F32).sum(0)
+    got, *beside = lax.optimization_barrier((got, *beside))
+    return got.astype(F32).sum(0), beside
+
+
+def scatter_rows_direct(part, me):
+    part = part.reshape(SEQ, ROWS, D)
+    total = lax.dynamic_index_in_dim(part, me, 0, False).astype(F32)
+    got = []
+    for k in range(1, SEQ):
+        own = lax.dynamic_index_in_dim(part, me ^ k, 0, False)
+        got.append(lax.ppermute(own, "seq", [(i, i ^ k) for i in range(SEQ)]))
+    for v in got:
+        total = total + v.astype(F32)
+    return total
+
+
+def core_swap(v):
+    return lax.ppermute(v, "dp", [(i, i ^ 1) for i in range(DP)])
+
+
+def same_core():
+    return [[d * SEQ + s for d in range(c, DP, 2) for s in range(SEQ)] for c in range(2)]
 
 
 def per_head(cols, shape):
@@ -118,11 +140,31 @@
     return jnp.where(s <= t, scores, NEG)
 
 
-def mixer_forward_kernel(proj, small_ref, mix, y_out, states, log_totals, keys, values):
+def unit_rows(x):
+    return x * lax.rsqrt(jnp.mean(x * x, axis=-1, keepdims=True) + EPS)
+
+
+def mixer_forward_kernel(*refs):
+    (
+        where, w_mine, w_other, small_ref, out_w, *pieces,
+        unit, ffn_grad, in_w, gu_w, proj, mix, y_out, states, log_totals, mid_part, keys, values,
+    ) = refs
+    me, core = where[0], where[1]
+    for piece, place in zip(pieces, PLACES):
+        rows = pl.ds(piece_row(me, place), piece.shape[0])
+        unit[rows, :] = unit_rows(piece[:, :D].astype(F32)).astype(BF)
+        ffn_grad[rows, :] = piece[:, D:]
+    half = ROWS // 2
+    for j in range(SEQ):
+        for source, at in ((w_mine, core * half), (w_other, half - core * half)):
+            rows = pl.ds(pl.multiple_of(at + j * ROWS, half), half)
+            in_w[rows, :] = source[j, :, :CW]
+            gu_w[rows, :] = source[j, :, CW:]
     small = small_ref[...]
     state = jnp.zeros((HW, NS), F32)
     for c in range(NCH):
         rows = slice(c * CH, (c + 1) * CH)
+        proj[rows, :] = dot(unit[rows, :], in_w[...])
         b = proj[rows, CB : CB + NS].astype(BF)
         cc = proj[rows, CC : CC + NS].astype(BF)
         z = proj[rows, CZ : CZ + HW]
@@ -156,6 +198,7 @@
         probs = (weights / totals).astype(BF)
         mix[rows, HW : HW + HS] = dot(probs, values[0:seen, :]).astype(BF)
         log_totals[rows, :] = jnp.broadcast_to(peak + jnp.log(totals), (CH, 8))
+        mid_part[rows, :] = dot(mix[rows, :], out_w[...]).astype(BF)
 
 
 def mixer_backward_kernel(
@@ -182,7 +225,7 @@
         rows = slice(c * CH, (c + 1) * CH)
         seen = (c + 1) * CH
         q = proj[rows, CQ : CQ + HS].astype(BF)
-        grad = mix_grad[rows, HW : HW + HS].astype(BF)
+        grad = mix_grad[rows, HW : HW + HS]
         scores = causal(c, dot(q, keys[0:seen, :], ((1,), (1,))) * HS**-0.5)
         probs = jnp.exp(scores - log_totals[rows, 0:1])
         prob_grad = dot(grad, values[0:seen, :], ((1,), (1,)))
@@ -207,7 +250,7 @@
         dt_w = widen(dt)
         v = u * dt_w
         vb = v.astype(BF)
-        gated_grad = mix_grad[rows, 0:HW].astype(BF).astype(F32)
+        gated_grad = mix_grad[rows, 0:HW].astype(F32)
         gate = jax.nn.sigmoid(z)
         dy = gated_grad * z * gate
         out[rows, CZ : CZ + HW] = (
@@ -268,20 +311,81 @@
 PARAMS = pltpu.CompilerParams(vmem_limit_bytes=50 * 1024 * 1024)
 
 
-def mixer_forward(proj, small):
+SMEM = pl.BlockSpec(memory_space=pltpu.SMEM)
+
+
+def mixer_forward(where, w_mine, w_other, small, out_w, pieces):
+    shape = jax.ShapeDtypeStruct
     return pl.pallas_call(
         mixer_forward_kernel,
         out_shape=(
-            jax.ShapeDtypeStruct((TOK, HW + HS), BF),
-            jax.ShapeDtypeStruct((TOK, HW), F32),
-            jax.ShapeDtypeStruct((NCH, HW, NS), F32),
-            jax.ShapeDtypeStruct((TOK, 8), F32),
+            shape((TOK, D), BF),
+            shape((TOK, D), BF),
+            shape((D, CW), BF),
+            shape((D, 2 * FL), BF),
+            shape((TOK, CW), F32),
+            shape((TOK, HW + HS), BF),
+            shape((TOK, HW), F32),
+            shape((NCH, HW, NS), F32),
+            shape((TOK, 8), F32),
+            shape((TOK, D), BF),
         ),
-        in_specs=[VMEM] * 2,
-        out_specs=(VMEM,) * 4,
+        in_specs=[SMEM] + [VMEM] * 14,
+        out_specs=(VMEM,) * 10,
         scratch_shapes=[pltpu.VMEM((TOK, HS), BF), pltpu.VMEM((TOK, HS), BF)],
         compiler_params=PARAMS,
-    )(proj, small)
+    )(where, w_mine, w_other, small, out_w, *pieces)
+
+
+def feed_forward_kernel(*refs):
+    where, gu_w, act_grad, *pieces, unit, act, up_grad, e_part = refs
+    for piece, place in zip(pieces, PLACES):
+        unit[pl.ds(piece_row(where[0], place), piece.shape[0]), :] = piece[...]
+    for c in range(NCH):
+        rows = slice(c * CH, (c + 1) * CH)
+        gate_rows = dot(unit[rows, :], gu_w[...])
+        gate, wide = gate_rows[:, :FL], gate_rows[:, FL:]
+        s = jax.nn.sigmoid(gate)
+        act[rows, :] = (gate * s * wide).astype(BF)
+        grad = act_grad[rows, :].astype(F32)
+        up_grad[rows, :FL] = (grad * wide * s * (1.0 + gate * (1.0 - s))).astype(BF)
+        up_grad[rows, FL:] = (grad * gate * s).astype(BF)
+        e_part[rows, :] = dot(up_grad[rows, :], gu_w[...], ((1,), (1,))).astype(BF)
+
+
+def feed_forward(where, gu_w, act_grad, pieces):
+    shape = jax.ShapeDtypeStruct
+    return pl.pallas_call(
+        feed_forward_kernel,
+        out_shape=(
+            shape((TOK, D), BF), shape((TOK, FL), BF), shape((TOK, 2 * FL), BF), shape((TOK, D), BF),
+        ),
+        in_specs=[SMEM] + [VMEM] * 12,
+        out_specs=(VMEM,) * 4,
+        compiler_params=PARAMS,
+    )(where, gu_w, act_grad, *pieces)
+
+
+def branch_kernel(*refs):
+    where, out_w, mix, *pieces, mix_grad, out_grad, branch = refs
+    for piece, place in zip(pieces, PLACES):
+        branch[pl.ds(piece_row(where[0], place), piece.shape[0]), :] = piece[...]
+    for c in range(NCH):
+        rows = slice(c * CH, (c + 1) * CH)
+        mix_grad[rows, :] = dot(branch[rows, :], out_w[...], ((1,), (1,))).astype(BF)
+    out_grad[...] = dot(mix[...], branch[...], ((0,), (0,))).astype(BF)
+
+
+def branch_products(where, out_w, mix, pieces):
+    shape = jax.ShapeDtypeStruct
+    return pl.pallas_call(
+        branch_kernel,
+        out_shape=(shape((TOK, HW + HS), BF), shape((HW + HS, D), BF)),
+        in_specs=[SMEM] + [VMEM] * 12,
+        out_specs=(VMEM,) * 2,
+        scratch_shapes=[pltpu.VMEM((TOK, D), BF)],
+        compiler_params=PARAMS,
+    )(where, out_w, mix, *pieces)
 
 
 def mixer_backward(proj, small, y, states, log_totals, mix_grad):
@@ -300,53 +404,167 @@
     )(proj, small, y, states, log_totals, mix_grad)
 
 
-def mixer_shares(mixer_w, attn_w):
-    z = mixer_w[:, :INNER].reshape(ROWS, SEQ, HW).swapaxes(0, 1)
-    u = mixer_w[:, INNER : 2 * INNER].reshape(ROWS, SEQ, HW).swapaxes(0, 1)
-    both = jnp.broadcast_to(mixer_w[None, :, 2 * INNER : 2 * INNER + 2 * NS], (SEQ, ROWS, 2 * NS))
-    r = mixer_w[:, 2 * INNER + 2 * NS :].reshape(ROWS, SEQ, HL).swapaxes(0, 1)
-    q = attn_w[:, : QH * HS].reshape(ROWS, SEQ, HS).swapaxes(0, 1)
-
-    def kv(w):
-        w = w.reshape(ROWS, KVH, HS).swapaxes(0, 1)
-        return jnp.repeat(w, SEQ // KVH, axis=0)
-
-    k = kv(attn_w[:, QH * HS : QH * HS + KVH * HS])
-    v = kv(attn_w[:, QH * HS + KVH * HS :])
-    pad = jnp.zeros((SEQ, ROWS, CW - CR - HL), mixer_w.dtype)
-    return jnp.concatenate([both, z, q, u, k, v, r, pad], axis=2)
-
-
-def mixer_rows(shares):
-    n = shares.shape[1]
-    flat = lambda v: v.swapaxes(0, 1).reshape(n, -1)
-
-    def kv(v):
-        return flat(v.reshape(KVH, SEQ // KVH, n, HS).sum(1))
-
-    both = shares[:, :, : 2 * NS].sum(0)
-    mixer = [
-        flat(shares[:, :, CZ : CZ + HW]),
-        flat(shares[:, :, CU : CU + HW]),
-        both,
-        flat(shares[:, :, CR : CR + HL]),
-    ]
-    attn = [
-        flat(shares[:, :, CQ : CQ + HS]),
-        kv(shares[:, :, CK : CK + HS]),
-        kv(shares[:, :, CV : CV + HS]),
-    ]
-    sums = shares[:, :, CR + 8 : CR + 8 + 3 * HL].sum(0)
-    return jnp.concatenate(mixer + attn + [sums], axis=1)
-
-
-def unit_rows(x):
-    return x * lax.rsqrt(jnp.mean(x * x, axis=-1, keepdims=True) + EPS)
+def pack_weights_kernel(where, mixer_w, attn_w, gate_up, gains, out):
+    half = ROWS // 2
+    rows = pl.ds(pl.multiple_of(where[1] * half, half), half)
+    g1, g2 = gains[rows, 0:1], gains[rows, 1:2]
+    lane = lax.broadcasted_iota(jnp.int32, (MH, HS), 1)
+    sub = lax.broadcasted_iota(jnp.int32, (MH, HS), 0)
+
+    def part(ref, at, width, g):
+        return (ref[rows, at : at + width].astype(F32) * g).astype(BF)
+
+    both = part(mixer_w, 2 * INNER, 2 * NS, g1)
+    steps_w = part(mixer_w, 2 * INNER + 2 * NS, MH, g1)
+    for s in range(SEQ):
+        head = s // (SEQ // KVH) * HS
+        out[s, :, CB : CB + 2 * NS] = both
+        out[s, :, CZ : CZ + HW] = part(mixer_w, s * HW, HW, g1)
+        out[s, :, CQ : CQ + HS] = part(attn_w, s * HS, HS, g1)
+        out[s, :, CU : CU + HW] = part(mixer_w, INNER + s * HW, HW, g1)
+        out[s, :, CK : CK + HS] = part(attn_w, QH * HS + head, HS, g1)
+        out[s, :, CV : CV + HS] = part(attn_w, (QH + KVH) * HS + head, HS, g1)
+        own = ((sub == s * HL + lane) & (lane < HL)).astype(BF)
+        out[s, :, CR:CW] = dot(steps_w, own).astype(BF)
+        out[s, :, CW : CW + FL] = part(gate_up, s * FL, FL, g2)
+        out[s, :, CW + FL :] = part(gate_up, FF + s * FL, FL, g2)
+
+
+def pack_weights(where, mixer_w, attn_w, gate_up, gains):
+    return pl.pallas_call(
+        pack_weights_kernel,
+        out_shape=jax.ShapeDtypeStruct((SEQ, ROWS // 2, CW + 2 * FL), BF),
+        in_specs=[SMEM] + [VMEM] * 4,
+        out_specs=VMEM,
+        compiler_params=PARAMS,
+    )(where, mixer_w, attn_w, gate_up, gains)
+
+
+WM = 2 * INNER + 2 * NS + MH
+WMP = 3456
+WA = (QH + 2 * KVH) * HS
+
+
+WA0 = WMP
+WO0 = WMP + WA
+WALL = WO0 + 2 * FF
+
+
+def mixer_rows_kernel(got, got_gu, out, rows):
+    for s in range(SEQ):
+        rows[:, WO0 + s * 2 * FL : WO0 + (s + 1) * 2 * FL] = sum(
+            got_gu[chip * SEQ + s].astype(F32) for chip in range(8)
+        )
+    share = [sum(got[chip * SEQ + s].astype(F32) for chip in range(8)) for s in range(SEQ)]
+    lane = lax.broadcasted_iota(jnp.int32, (16, 128), 1)
+    sub = lax.broadcasted_iota(jnp.int32, (16, 128), 0)
+    tail = jnp.zeros((8, 128), F32)
+    every = sum(share)
+    for s in range(SEQ):
+        rows[:, s * HW : (s + 1) * HW] = share[s][:, CZ : CZ + HW]
+        rows[:, INNER + s * HW : INNER + (s + 1) * HW] = share[s][:, CU : CU + HW]
+        rows[:, WA0 + s * HS : WA0 + (s + 1) * HS] = share[s][:, CQ : CQ + HS]
+        place = ((lane == s * HL + sub) & (sub < HL)).astype(F32)
+        tail = tail + dot(share[s][:, CR : CR + 16], place, precision=HIGH)
+    rows[:, 2 * INNER : 2 * INNER + 2 * NS] = every[:, : 2 * NS]
+    place = ((lane == MH - 8 + sub) & (sub >= 8)).astype(F32)
+    tail = tail + dot(every[:, CR : CR + 16], place, precision=HIGH)
+    place = ((lane == MH + 8 + sub) & (sub == 0)).astype(F32)
+    tail = tail + dot(every[:, CR + 16 : CR + 32], place, precision=HIGH)
+    rows[:, 2 * INNER + 2 * NS : WMP] = tail
+    each = SEQ // KVH
+    for j in range(KVH):
+        both = sum(share[j * each : (j + 1) * each])
+        at = WA0 + QH * HS + j * HS
+        rows[:, at : at + HS] = both[:, CK : CK + HS]
+        at = at + KVH * HS
+        rows[:, at : at + HS] = both[:, CV : CV + HS]
+    out[...] = rows[...].astype(BF)
+
+
+def mixer_rows(got, got_gu):
+    return pl.pallas_call(
+        mixer_rows_kernel,
+        out_shape=jax.ShapeDtypeStruct((8, WALL), BF),
+        in_specs=[VMEM] * 2,
+        out_specs=VMEM,
+        scratch_shapes=[pltpu.VMEM((8, WALL), F32)],
+        compiler_params=PARAMS,
+    )(got, got_gu)
+
+
+def finish_kernel(
+    where, mine, other, mixer_w, attn_w, gate_up, gains, mixer_out, attn_out, gate_up_out, gain, line, rows
+):
+    half = ROWS // 2
+    core = where[1]
+    for source, at in ((mine, core * half), (other, half - core * half)):
+        for i in range(half // 16):
+            to = pl.ds(pl.multiple_of(at + i * 16, 16), 16)
+            rows[to, :] = source[i * 16 : (i + 1) * 16, :].astype(F32)
+    line[...] = rows[0:8, WM - MH : WMP] + rows[half : half + 8, WM - MH : WMP]
+    for i in range(ROWS // 16):
+        at = slice(i * 16, (i + 1) * 16)
+        mixer, attn, g = rows[at, :WM], rows[at, WA0:WO0], gains[at, :]
+        total = jnp.sum(mixer * mixer_w[at, :].astype(F32), axis=1, keepdims=True) + jnp.sum(
+            attn * attn_w[at, :].astype(F32), axis=1, keepdims=True
+        )
+        mixer_out[at, :] = mixer * g[:, 0:1]
+        attn_out[at, :] = attn * g[:, 0:1]
+        total_two = jnp.zeros((16, 1), F32)
+        for s in range(SEQ):
+            for k in range(2):
+                block = rows[at, WO0 + (s * 2 + k) * FL : WO0 + (s * 2 + k + 1) * FL]
+                to = slice(k * FF + s * FL, k * FF + (s + 1) * FL)
+                total_two = total_two + jnp.sum(
+                    block * gate_up[at, to].astype(F32), axis=1, keepdims=True
+                )
+                gate_up_out[at, to] = block * g[:, 1:2]
+        gain[at, :] = jnp.concatenate([total, total_two], axis=1)
+
+
+def finish(where, mine, other, mixer_w, attn_w, gate_up, gains):
+    shape = lambda *dims: jax.ShapeDtypeStruct(dims, F32)
+    return pl.pallas_call(
+        finish_kernel,
+        out_shape=(
+            shape(ROWS, WM), shape(ROWS, WA), shape(ROWS, 2 * FF), shape(ROWS, 2), shape(8, 128),
+        ),
+        in_specs=[SMEM] + [VMEM] * 6,
+        out_specs=(VMEM,) * 5,
+        scratch_shapes=[pltpu.VMEM((ROWS, WALL), F32)],
+        compiler_params=PARAMS,
+    )(where, mine, other, mixer_w, attn_w, gate_up, gains)
 
 
 def unit_back(x, e):
     rho = lax.rsqrt(jnp.mean(x * x, axis=-1, keepdims=True) + EPS)
     return rho * e - x * (rho * rho * rho) * jnp.mean(x * e, axis=-1, keepdims=True)
+
+
+def chip_groups():
+    return [list(range(c, DP, 2)) for c in range(2)]
+
+
+def core_sum(grad, core, line=None):
+    n = grad.shape[1]
+    parts = grad.reshape(SEQ, 2, ROWS // 2, n)
+    mine = lax.dynamic_index_in_dim(parts, core, 1, False).astype(F32)
+    other = core_swap(lax.dynamic_index_in_dim(parts, 1 - core, 1, False))
+    both = mine + other.astype(F32)
+    if line is not None:
+        me = lax.axis_index("seq")
+        here = (lax.broadcasted_iota(jnp.int32, both.shape, 0) == me) & (
+            lax.broadcasted_iota(jnp.int32, both.shape, 1) == 0
+        )
+        both = both + jnp.where(here, line[None, None], 0.0)
+    return both.astype(BF).reshape(SEQ, 8, 8, n).swapaxes(0, 1).reshape(64, 8, n)
+
+
+def to_owners(sent):
+    return lax.all_to_all(
+        sent, ("dp", "seq"), split_axis=0, concat_axis=0, tiled=True, axis_index_groups=same_core()
+    )
 
 
 def local(
@@ -354,90 +572,75 @@
     norm_gains, step_bias, decay_log, skip_gain,
 ):
     me = lax.axis_index("seq")
+    core = lax.axis_index("dp") % 2
+    where = jnp.stack([me, core]).astype(jnp.int32)
     x0 = inputs[0]
-    gains = norm_gains[0].astype(F32)
-    g1, g2 = gains[0][:, None], gains[1][:, None]
-    mixer_f = mixer_in[0].astype(F32)
-    attn_f = attn_in[0].astype(F32)
-    gate_up_f = gate_up[0].astype(F32)
+    gains = norm_gains[0].astype(F32).T
     down_w = down_proj[0]
     out_w = jnp.concatenate([mamba_out[0], attn_out[0]], axis=0)
-    small = jnp.zeros((8, 8), F32)
-    small = small.at[0, :HL].set(step_bias[0].astype(F32))
-    small = small.at[1, :HL].set(decay_log[0].astype(F32))
-    small = small.at[2, :HL].set(skip_gain[0].astype(F32))
-
-    shares = mixer_shares((mixer_f * g1).astype(BF), (attn_f * g1).astype(BF))
-    in_w = lax.all_to_all(shares, "seq", split_axis=0, concat_axis=0, tiled=True).reshape(D, CW)
-    x_all = gather_rows(x0)
-    unit_one = unit_rows(x_all.astype(F32)).astype(BF)
-    proj = dot(unit_one, in_w)
-    mix, y, states, log_totals = mixer_forward(proj, small)
-    mid = scatter_rows(dot(mix, out_w).astype(BF)) + x0.astype(F32)
-
-    gu = (gate_up_f * g2).astype(BF).reshape(ROWS, 2, SEQ, FL).transpose(2, 0, 1, 3)
-    gu_w = lax.all_to_all(gu, "seq", split_axis=0, concat_axis=0, tiled=True).reshape(D, 2 * FL)
-    ffn_grad = lax.all_gather(cotangent[0], "seq", axis=0, tiled=True)
-    unit_two = gather_rows(unit_rows(mid).astype(BF))
-    gate_rows = dot(unit_two, gu_w)
-    gate, wide = gate_rows[:, :FL], gate_rows[:, FL:]
-    s = jax.nn.sigmoid(gate)
-    act = (gate * s * wide).astype(BF)
-    act_grad = dot(ffn_grad, down_w, ((1,), (1,))).astype(BF).astype(F32)
-    up_grad = jnp.concatenate(
-        [act_grad * wide * s * (1.0 + gate * (1.0 - s)), act_grad * gate * s], axis=1
-    ).astype(BF)
-    mid_e = scatter_rows(dot(up_grad, gu_w, ((1,), (1,))).astype(BF))
+    small = jnp.concatenate([step_bias, decay_log, skip_gain], axis=0).astype(F32)
+    small = jnp.pad(small, ((0, 5), (0, 8 - HL)))
+
+    pieces = gather_pieces(jnp.concatenate([x0, cotangent[0]], axis=1))
+    w_mine = lax.all_to_all(
+        pack_weights(where, mixer_in[0], attn_in[0], gate_up[0], gains),
+        "seq", split_axis=0, concat_axis=0, tiled=True,
+    )
+    unit_one, ffn_grad, in_w, gu_w, proj, mix, y, states, log_totals, mid_part = mixer_forward(
+        where, w_mine, core_swap(w_mine), small, out_w, pieces
+    )
+    mid, (act_grad,) = scatter_rows(
+        mid_part, (dot(ffn_grad, down_w, ((1,), (1,))).astype(BF),)
+    )
+    mid = mid + x0.astype(F32)
+
+    unit_two, act, up_grad, e_part = feed_forward(
+        where, gu_w, act_grad, gather_pieces(unit_rows(mid).astype(BF))
+    )
+    gu_sent = core_sum(dot(unit_two, up_grad, ((0,), (0,))).astype(BF), core)
+    down_grad = dot(act, ffn_grad, ((0,), (0,))).astype(BF)
+    mid_e, (gu_sent, out_part, down_grad) = scatter_rows(
+        e_part, (gu_sent, dot(act, down_w).astype(BF), down_grad)
+    )
     mid_grad = cotangent[0].astype(F32) + unit_back(mid, mid_e)
-    branch = gather_rows(mid_grad.astype(BF))
-
-    result = lax.psum_scatter(
-        dot(act, down_w).astype(BF), "seq", scatter_dimension=0, tiled=True
-    ).astype(F32)
+    pieces = gather_pieces(mid_grad.astype(BF))
+    *pieces, gu_got = lax.optimization_barrier((*pieces, to_owners(gu_sent)))
+
+    mix_grad, out_grad = branch_products(where, out_w, mix, pieces)
+    out_part, mix_grad = lax.optimization_barrier((out_part, mix_grad))
+    proj_grad, sums = mixer_backward(proj, small, y, states, log_totals, mix_grad)
+    row_sums = lax.psum(jnp.concatenate([down_grad, out_grad], axis=0), "dp")
+    in_grad = dot(unit_one, proj_grad, ((0,), (0,))).astype(BF)
+    line = jnp.concatenate([sums[0, :HL], sums[1, :HL], sums[2, :HL]])
+    line = jnp.pad(line, (CR + 8, CW - CR - 8 - 3 * HL))
+    e_part = dot(proj_grad, in_w, ((1,), (1,))).astype(BF)
+    result, (sent, e_part) = scatter_rows(out_part, (core_sum(in_grad, core, line), e_part))
     outputs = (mid + result).astype(BF)
-    down_grad = dot(act, ffn_grad, ((0,), (0,))).astype(BF)
-    gu_grad = dot(unit_two, up_grad, ((0,), (0,))).astype(BF)
-    gu_grad = lax.all_to_all(
-        gu_grad.reshape(SEQ, ROWS, 2 * FL), "seq", split_axis=0, concat_axis=0, tiled=True
-    )
-    gu_grad = gu_grad.reshape(SEQ, ROWS, 2, FL).transpose(1, 2, 0, 3).reshape(ROWS * 4, D)
-    ffn_sums = lax.psum(jnp.concatenate([gu_grad, down_grad], axis=0), "dp").astype(F32)
-    gate_up_grad = ffn_sums[: ROWS * 4].reshape(ROWS, 2 * FF)
-    down_sum = ffn_sums[ROWS * 4 :]
-
-    mix_grad = dot(branch, out_w, ((1,), (1,)))
-    out_grad = lax.psum(dot(mix, branch, ((0,), (0,))).astype(BF), "dp").astype(F32)
-    proj_grad, sums = mixer_backward(proj, small, y, states, log_totals, mix_grad)
-    in_grad = dot(unit_one, proj_grad, ((0,), (0,)))
-    line = jnp.concatenate([sums[0, :HL], sums[1, :HL], sums[2, :HL]])[None]
-    in_grad = lax.dynamic_update_slice(in_grad, line, (me * ROWS, CR + 8)).astype(BF)
-    sent = in_grad.reshape(SEQ, DP, ROWS // DP, CW).swapaxes(0, 1).reshape(DP * SEQ, ROWS // DP, CW)
-    got = lax.all_to_all(sent, ("dp", "seq"), split_axis=0, concat_axis=0, tiled=True)
-    got = got.reshape(DP, SEQ, ROWS // DP, CW).astype(F32).sum(0)
-    rows = mixer_rows(got).astype(BF)
-    in_e = scatter_rows(dot(proj_grad, in_w, ((1,), (1,))).astype(BF))
+    rows = mixer_rows(to_owners(sent), gu_got)
+    mine = lax.all_to_all(
+        jnp.broadcast_to(rows[None], (8, 8, WALL)), "dp", split_axis=0, concat_axis=0, tiled=True,
+        axis_index_groups=chip_groups(),
+    ).reshape(ROWS // 2, WALL)
+    in_e = scatter_rows_direct(e_part, me)
     input_grad = mid_grad + unit_back(x0.astype(F32), in_e)
-    rows = lax.all_gather(rows, "dp", axis=0, tiled=True).astype(F32)
-    wm = 2 * INNER + 2 * NS + MH
-    wa = (QH + 2 * KVH) * HS
-    mixer_rows_grad = rows[:, :wm]
-    attn_rows_grad = rows[:, wm : wm + wa]
-    line = rows[0, wm + wa :]
-    gain_one = (mixer_rows_grad * mixer_f).sum(1) + (attn_rows_grad * attn_f).sum(1)
-    gain_two = (gate_up_grad * gate_up_f).sum(1)
+    mixer_g, attn_g, gate_up_g, gain, line = finish(
+        where, mine, core_swap(mine), mixer_in[0], attn_in[0], gate_up[0], gains
+    )
+    row_sums = row_sums.astype(F32)
+    line = line[0:1, MH : MH + 3 * HL]
     return (
         outputs[None],
         input_grad[None],
-        (mixer_rows_grad * g1)[None],
-        (attn_rows_grad * g1)[None],
-        out_grad[None, :HW],
-        out_grad[None, HW:],
-        (gate_up_grad * g2)[None],
-        down_sum[None],
-        jnp.stack([gain_one, gain_two])[None],
-        line[None, :HL],
-        line[None, HL : 2 * HL],
-        line[None, 2 * HL : 3 * HL],
+        mixer_g[None],
+        attn_g[None],
+        row_sums[None, FL : FL + HW],
+        row_sums[None, FL + HW :],
+        gate_up_g[None],
+        row_sums[None, :FL],
+        gain.T[None],
+        line[:, :HL],
+        line[:, HL : 2 * HL],
+        line[:, 2 * HL :],
     )
 
 

time: 576 us -> 488 us (0.85)
  waiting for transfers between devices: 296 us -> 225 us
  local copies, waits for them, and re-layouts: 72 us -> 31.8 us
  blocking collectives: 0 us -> 24.7 us
  Pallas kernels: 26.8 us -> 51.1 us
  matrix products: 39.8 us -> 19.9 us
  other arithmetic: 28.9 us -> 17.1 us
  starting transfers between devices: 90.9 us -> 97.4 us
    all_to_all x3, waiting for transfers between devices: 79.1 us -> 35.5 us  [scatter_rows(): lax.all_to_all(part.reshape(SEQ, ROWS, D), 'seq', split_axis=0, concat_ax...]
    all_gather x2 -> x0, waiting for transfers between devices: 32.5 us -> none  [the longest x1 32.5 us: local(): rows = lax.all_gather(rows, 'dp', axis=0, tiled=True).astype(F32)]
    reduce_scatter x1 -> x0, waiting for transfers between devices: 29.4 us -> none  [local(): lax.psum_scatter(dot(act, down_w).astype(BF), 'seq', scatter_dimension=0,...]
    ppermute x27 -> x38, waiting for transfers between devices: 31.3 us -> 56.7 us  [the longest x27 36.5 us: gather_pieces(): send = lambda v, perm: lax.ppermute(v, 'seq', perm)]
    all_to_all x0 -> x1, blocking collectives: none -> 24.7 us  [local(): lax.all_to_all(pack_weights(where, mixer_in[0], attn_in[0], gate_up[0], g...]
    pallas_call x1 -> x6, Pallas kernels: 7.89 us -> 32.4 us  [the longest x1 18.2 us: mixer_forward(): pl.pallas_call(mixer_forward_kernel, out_shape=(shape((TOK, D), BF), shap...]
    psum x1, waiting for transfers between devices: 109 us -> 130 us  [local(): row_sums = lax.psum(jnp.concatenate([down_grad, out_grad], axis=0), 'dp')]
    dot_general x12 -> x6, matrix products: 39.8 us -> 19.9 us  [dot(): lax.dot_general(a, b, (dims, ((), ())), precision=precision, preferred_el...]
  transfers between devices with their start and end apart: 38 -> 45, of which waited for: 18 -> 20; matrix products, arithmetic and copies ran while one was open for 19% -> 9% of each run, Pallas kernels for 3% -> 4%
where the time goes in v2:
time: 488 us; the launch traced here: 482 us
  waiting for transfers between devices  225 us (46%)
  starting transfers between devices  97.4 us (20%)
  Pallas kernels  51.1 us (10%)
  local copies, waits for them, and re-layouts  31.8 us (7%)
  blocking collectives  24.7 us (5%)
  matrix products  19.9 us (4%)
  other arithmetic  17.1 us (4%)
  between operations  14.9 us (3%)
    psum x1, waiting for transfers between devices, local(): row_sums = lax.psum(jnp.concatenate([down_grad, out_grad], axis=0), 'dp')  130 us
    ppermute x27, waiting for transfers between devices, gather_pieces(): send = lambda v, perm: lax.ppermute(v, 'seq', perm)  36.5 us
    all_to_all x3, waiting for transfers between devices, scatter_rows(): lax.all_to_all(part.reshape(SEQ, ROWS, D), 'seq', split_axis=0, concat_ax...  35.5 us
    ppermute x27, starting transfers between devices, gather_pieces(): send = lambda v, perm: lax.ppermute(v, 'seq', perm)  30.8 us
    all_to_all x1, blocking collectives, local(): lax.all_to_all(pack_weights(where, mixer_in[0], attn_in[0], gate_up[0], g...  24.7 us
    ppermute x7, waiting for transfers between devices, scatter_rows_direct(): got.append(lax.ppermute(own, 'seq', [(i, i ^ k) for i in range(SEQ)]))  20.2 us
    dot_general x6, matrix products, dot(): lax.dot_general(a, b, (dims, ((), ())), precision=precision, preferred_el...  19.9 us
    all_to_all x2, starting transfers between devices, to_owners(): lax.all_to_all(sent, ('dp', 'seq'), split_axis=0, concat_axis=0, tiled=Tr...  19.5 us
  transfers between devices with their start and end apart: 45, of which 20 were waited for; matrix products, arithmetic and copies ran while one was open for 9% of the time, Pallas kernels for 4%

profile of v2, /device:TPU:1, one launch (start us, length us, event | category | flops | bytes accessed | tf_op | source)
XLA Modules:
  0.0 482.4 jit_solution(15829110841132742954)
XLA Ops:
  11.8 24.7 %all_to_all.35.refs_1_ = bf16[8,64,1408]{2,1,0:T(8,128)(2,1)S(1)} all-to-all(bf16[8,64,1408]{2,1,0:T(8,128)(2,1)S(1)} %shard_map.211), channel_id=1, replica_groups=mesh['dp'=16,'seq'=8] {'seq'}, dimensions={0} | all-to-all | bytes 2883584 | tf_op jit(solution)/shard_map/all_to_all | solution.py:585
  42.3 11.3 %collective-permute-done.2.refs_7_ = bf16[128,2048]{1,0:T(8,128)(2,1)S(1)} collective-permute-done((bf16[128,2048]{1,0:T(8,128)(2,1)S(1)}, bf16[128,2048]{1,0:T(8,128)(2,1)S(1)}, u32[]{:S(2)}, u32[]{:S(2)}) %collective-permute-start.2) | collective-permute-done | bytes 524320 | tf_op jit(solution)/shard_map/ppermute | solution.py:52
  63.6 3.8 collective-permute-done.8.refs_13_
  67.4 4.9 %collective-permute-done.9.refs_14_ = bf16[64,2048]{1,0:T(8,128)(2,1)S(1)} collective-permute-done((bf16[64,2048]{1,0:T(8,128)(2,1)S(1)}, bf16[64,2048]{1,0:T(8,128)(2,1)S(1)}, u32[]{:S(2)}, u32[]{:S(2)}) %collective-permute-start.9) | collective-permute-done | bytes 262176 | tf_op jit(solution)/shard_map/ppermute | solution.py:52
  75.2 18.2 %shard_map.212 = (bf16[1024,1024]{1,0:T(8,128)(2,1)}, bf16[1024,1024]{1,0:T(8,128)(2,1)}, bf16[1024,896]{1,0:T(8,128)(2,1)}, bf16[1024,512]{1,0:T(8,128)(2,1)}, ...) custom-call(s32[2]{0:T(128)S(1)} %pad_add_fusion.where.refs_0_, ...), custom_call_target="tpu_custom_call" | custom-call | tf_op jit(solution)/shard_map/pallas_call | solution.py:319
  95.8 4.4 all-to-all-start.1
  100.2 3.1 convolution_convert_fusion.5.refs_2_
  103.3 25.1 %all-to-all-done.1 = bf16[8,128,1024]{2,1,0:T(8,128)(2,1)} async-done(((bf16[8,128,1024]{2,1,0:T(8,128)(2,1)}), bf16[8,128,1024]{2,1,0:T(8,128)(2,1)}, u32[]{:S(2)}, u32[]{:S(2)}) %all-to-all-start.1) | async-done | bytes 2097184 | tf_op jit(solution)/shard_map/all_to_all | solution.py:68
  130.9 3.1 collective-permute-start.12
  133.9 3.4 collective-permute-done.11.refs_5_
  137.4 3.0 collective-permute-start.14
  148.7 5.6 %shard_map.213 = (bf16[1024,1024]{1,0:T(8,128)(2,1)}, bf16[1024,256]{1,0:T(8,128)(2,1)S(1)}, bf16[1024,512]{1,0:T(8,128)(2,1)}, bf16[1024,1024]{1,0:T(8,128)(2,1)}) custom-call(s32[2]{0:T(128)S(1)} %pad_add_fusion.where.refs_0_, bf16[1024,512]{1,0:T(8,128)(2,1)} %get-tuple-element.60.refs_1_, bf16[1024,256]{1,0:T(8,128)(2,1)S(1)} %copy-done.9, ...), custom_call_target="tpu_custom_call" | custom-call | tf_op jit(solution)/shard_map/pallas_call | solution.py:358
  154.3 4.3 all-to-all-start.2
  158.7 3.3 convolution_convert_fusion.3
  162.0 6.5 %collective-permute-start.19 = (bf16[8,64,512]{2,1,0:T(8,128)(2,1)S(1)}, bf16[8,64,512]{2,1,0:T(8,128)(2,1)S(1)}, u32[]{:S(2)}, u32[]{:S(2)}) collective-permute-start(bf16[8,64,512]{2,1,0:T(8,128)(2,1)S(1)} %dynamic-slice_bitcast_fusion.1), channel_id=1, source_target_pairs={{0,8},{8,0},{16,24},{24,16},{32,40},{40,32},{48,56},{56,48},{64,72... | collective-permute-start | bytes 1572872 | tf_op jit(solution)/shard_map/ppermute | solution.py:88
  173.2 10.4 %all-to-all-done.2 = bf16[8,128,1024]{2,1,0:T(8,128)(2,1)} async-done(((bf16[8,128,1024]{2,1,0:T(8,128)(2,1)}), bf16[8,128,1024]{2,1,0:T(8,128)(2,1)}, u32[]{:S(2)}, u32[]{:S(2)}) %all-to-all-start.2) | async-done | bytes 2097184 | tf_op jit(solution)/shard_map/all_to_all | solution.py:68
  189.5 9.3 %all-to-all-start.3 = ((bf16[64,8,512]{2,1,0:T(8,128)(2,1)}), bf16[64,8,512]{2,1,0:T(8,128)(2,1)S(1)}, u32[]{:S(2)}, u32[]{:S(2)}) async-start(bf16[64,8,512]{2,1,0:T(8,128)(2,1)} %bitcast.130), calls=%async_computation.3 | async-start | bytes 1048576 | tf_op jit(solution)/shard_map/all_to_all | solution.py:565
  211.2 3.2 collective-permute-done.28.refs_12_
  214.4 2.9 shard_map.214
  218.9 4.5 all-to-all-start.4
  226.5 18.8 %shard_map.215 = (bf16[1024,896]{1,0:T(8,128)(2,1)}, f32[8,8]{1,0:T(8,128)S(1)}) custom-call(f32[1024,896]{1,0:T(8,128)} %get-tuple-element.83.proj, f32[8,8]{1,0:T(8,128)S(1)} %fusion.30.refs_3_.small_ref, f32[1024,192]{1,0:T(8,128)S(1)} %copy-done.3, f32[4,192,128]{2,1,0:T(8,128)S(1)} %copy-done.17, f32[1024,8]{1,0:T(8,128)S(1)} %copy-done.13, ...), custom_call_target="tpu_custom_call" | custom-call | tf_op jit(solution)/shard_map/pallas_call | solution.py:392
  245.3 3.9 convolution_convert_fusion.2
  251.5 6.6 %collective-permute-start.29 = (bf16[8,64,896]{2,1,0:T(8,128)(2,1)}, bf16[8,64,896]{2,1,0:T(8,128)(2,1)}, u32[]{:S(2)}, u32[]{:S(2)}) collective-permute-start(bf16[8,64,896]{2,1,0:T(8,128)(2,1)} %dynamic-slice_bitcast_fusion), channel_id=1, source_target_pairs={{0,8},{8,0},{16,24},{24,16},{32,40},{40,32},{48,56},{56,48},{64,72... | collective-permute-start | bytes 2752520 | tf_op jit(solution)/shard_map/ppermute | solution.py:88
  259.3 5.9 %convolution_convert_fusion = bf16[1024,1024]{1,0:T(8,128)(2,1)} fusion(bf16[1024,896]{1,0:T(8,128)(2,1)} %get-tuple-element.88, bf16[1024,896]{1,0:T(8,128)(2,1)} %get-tuple-element.90), kind=kOutput, calls=%fused_computation.3 | convolution fusion | flops 1880096768 | bytes 5767168 | tf_op jit(solution)/shard_map/dot_general | solution.py:35
  267.8 10.2 %all-to-all-start.5 = ((bf16[64,8,896]{2,1,0:T(8,128)(2,1)}), bf16[64,8,896]{2,1,0:T(8,128)(2,1)S(1)}, u32[]{:S(2)}, u32[]{:S(2)}) async-start(bf16[64,8,896]{2,1,0:T(8,128)(2,1)} %bitcast.127), calls=%async_computation.5 | async-start | bytes 1835008 | tf_op jit(solution)/shard_map/all_to_all | solution.py:565
  278.1 129.6 %all-reduce.4.cloned.1.call-done = bf16[512,1024]{1,0:T(8,128)(2,1)} async-done(((bf16[512,1024]{1,0:T(8,128)(2,1)}), bf16[512,1024]{1,0:T(8,128)(2,1)}) %all-reduce.4.cloned.1.call-update) | async-done | bytes 1048592 | tf_op jit(solution)/shard_map/psum | solution.py:612
  411.9 6.9 %all-to-all-start.6 = ((bf16[8,8,8320]{2,1,0:T(8,128)(2,1)}), bf16[8,8,8320]{2,1,0:T(8,128)(2,1)S(1)}, u32[]{:S(2)}, u32[]{:S(2)}) async-start(bf16[8,8,8320]{2,1,0:T(8,128)(2,1)} %broadcast_in_dim.52), calls=%async_computation.6 | async-start | bytes 2129920 | tf_op jit(solution)/shard_map/all_to_all | solution.py:620
  435.4 5.9 %collective-permute-done.30 = bf16[128,1024]{1,0:T(8,128)(2,1)} collective-permute-done((bf16[128,1024]{1,0:T(8,128)(2,1)}, bf16[128,1024]{1,0:T(8,128)(2,1)}, u32[]{:S(2)}, u32[]{:S(2)}) %collective-permute-start.30) | collective-permute-done | bytes 262176 | tf_op jit(solution)/shard_map/ppermute | solution.py:81
  441.3 3.3 collective-permute-start.34
  451.3 5.4 %collective-permute-done.35 = bf16[128,1024]{1,0:T(8,128)(2,1)S(1)} collective-permute-done((bf16[128,1024]{1,0:T(8,128)(2,1)S(1)}, bf16[128,1024]{1,0:T(8,128)(2,1)S(1)}, u32[]{:S(2)}, u32[]{:S(2)}) %collective-permute-start.35) | collective-permute-done | bytes 262176 | tf_op jit(solution)/shard_map/ppermute | solution.py:81
  456.7 6.0 %collective-permute-done.36 = bf16[128,1024]{1,0:T(8,128)(2,1)S(1)} collective-permute-done((bf16[128,1024]{1,0:T(8,128)(2,1)S(1)}, bf16[128,1024]{1,0:T(8,128)(2,1)S(1)}, u32[]{:S(2)}, u32[]{:S(2)}) %collective-permute-start.36) | collective-permute-done | bytes 262176 | tf_op jit(solution)/shard_map/ppermute | solution.py:81
  466.5 4.2 shard_map.217
  (222 shorter events, 105.9 us)
Async XLA Ops:
  36.5 36.6 %collective-permute-start = (bf16[8,64,1408]{2,1,0:T(8,128)(2,1)S(1)}, bf16[8,64,1408]{2,1,0:T(8,128)(2,1)S(1)}, u32[]{:S(2)}, u32[]{:S(2)}) collective-permute-start(bf16[8,64,1408]{2,1,0:T(8,128)(2,1)S(1)} %all_to_all.35.refs_1_), channel_id=1, source_target_pairs={{0,8},{8,0},{16,24},{24,16},{32,40},{40,32},{48,56},{56,48},{64,72... | collective-permute-start | bytes 4325384 | tf_op jit(solution)/shard_map/ppermute | solution.py:88
  38.8 14.8 %collective-permute-start.2 = (bf16[128,2048]{1,0:T(8,128)(2,1)S(1)}, bf16[128,2048]{1,0:T(8,128)(2,1)S(1)}, u32[]{:S(2)}, u32[]{:S(2)}) collective-permute-start(bf16[128,2048]{1,0:T(8,128)(2,1)S(1)} %pad_maximum_fusion.2.refs_5_), channel_id=1, source_target_pairs={{0,2},{1,3},{2,4},{3,5},{4,6},{5,7},{6,0},{7,1},{8,10},{9,11},{10,... | collective-permute-start | bytes 1572872 | tf_op jit(solution)/shard_map/ppermute | solution.py:52
  39.2 14.5 %collective-permute-start.3 = (bf16[128,2048]{1,0:T(8,128)(2,1)S(1)}, bf16[128,2048]{1,0:T(8,128)(2,1)S(1)}, u32[]{:S(2)}, u32[]{:S(2)}) collective-permute-start(bf16[128,2048]{1,0:T(8,128)(2,1)S(1)} %pad_maximum_fusion.2.refs_5_), channel_id=1, source_target_pairs={{0,6},{1,7},{2,0},{3,1},{4,2},{5,3},{6,4},{7,5},{8,14},{9,15},{10,... | collective-permute-start | bytes 1572872 | tf_op jit(solution)/shard_map/ppermute | solution.py:52
  41.5 14.9 %collective-permute-start.1 = (bf16[128,2048]{1,0:T(8,128)(2,1)S(1)}, bf16[128,2048]{1,0:T(8,128)(2,1)S(1)}, u32[]{:S(2)}, u32[]{:S(2)}) collective-permute-start(bf16[128,2048]{1,0:T(8,128)(2,1)S(1)} %pad_maximum_fusion.2.refs_5_), channel_id=1, source_target_pairs={{0,1},{1,0},{2,3},{3,2},{4,5},{5,4},{6,7},{7,6},{8,9},{9,8},{10,11... | collective-permute-start | bytes 1572872 | tf_op jit(solution)/shard_map/ppermute | solution.py:52
  53.6 8.3 %collective-permute-start.4 = (bf16[64,2048]{1,0:T(8,128)(2,1)S(1)}, bf16[64,2048]{1,0:T(8,128)(2,1)S(1)}, u32[]{:S(2)}, u32[]{:S(2)}) collective-permute-start(bf16[64,2048]{1,0:T(8,128)(2,1)S(1)} %slice.64), channel_id=1, source_target_pairs={{0,2},{1,3},{2,4},{3,5},{4,6},{5,7},{6,0},{7,1},{8,10},{9,11},{10,... | collective-permute-start | bytes 786440 | tf_op jit(solution)/shard_map/ppermute | solution.py:52
  53.7 9.0 %collective-permute-start.5 = (bf16[64,2048]{1,0:T(8,128)(2,1)S(1)}, bf16[64,2048]{1,0:T(8,128)(2,1)S(1)}, u32[]{:S(2)}, u32[]{:S(2)}) collective-permute-start(bf16[64,2048]{1,0:T(8,128)(2,1)S(1)} %slice.65), channel_id=1, source_target_pairs={{0,6},{1,7},{2,0},{3,1},{4,2},{5,3},{6,4},{7,5},{8,14},{9,15},{10,... | collective-permute-start | bytes 786440 | tf_op jit(solution)/shard_map/ppermute | solution.py:52
  56.5 16.7 %collective-permute-start.6 = (bf16[128,2048]{1,0:T(8,128)(2,1)S(1)}, bf16[128,2048]{1,0:T(8,128)(2,1)S(1)}, u32[]{:S(2)}, u32[]{:S(2)}) collective-permute-start(bf16[128,2048]{1,0:T(8,128)(2,1)S(1)} %collective-permute-done.1.refs_6_), channel_id=1, source_target_pairs={{0,2},{1,3},{2,4},{3,5},{4,6},{5,7},{6,0},{7,1},{8,10},{9,11},{10,... | collective-permute-start | bytes 1572872 | tf_op jit(solution)/shard_map/ppermute | solution.py:52
  56.5 16.7 %collective-permute-start.7 = (bf16[128,2048]{1,0:T(8,128)(2,1)S(1)}, bf16[128,2048]{1,0:T(8,128)(2,1)S(1)}, u32[]{:S(2)}, u32[]{:S(2)}) collective-permute-start(bf16[128,2048]{1,0:T(8,128)(2,1)S(1)} %collective-permute-done.1.refs_6_), channel_id=1, source_target_pairs={{0,6},{1,7},{2,0},{3,1},{4,2},{5,3},{6,4},{7,5},{8,14},{9,15},{10,... | collective-permute-start | bytes 1572872 | tf_op jit(solution)/shard_map/ppermute | solution.py:52
  62.7 9.6 %collective-permute-start.9 = (bf16[64,2048]{1,0:T(8,128)(2,1)S(1)}, bf16[64,2048]{1,0:T(8,128)(2,1)S(1)}, u32[]{:S(2)}, u32[]{:S(2)}) collective-permute-start(bf16[64,2048]{1,0:T(8,128)(2,1)S(1)} %collective-permute-done.5.refs_10_), channel_id=1, source_target_pairs={{0,1},{1,0},{2,3},{3,2},{4,5},{5,4},{6,7},{7,6},{8,9},{9,8},{10,11... | collective-permute-start | bytes 786440 | tf_op jit(solution)/shard_map/ppermute | solution.py:52
  95.8 32.6 %all-to-all-start.1 = ((bf16[8,128,1024]{2,1,0:T(8,128)(2,1)}), bf16[8,128,1024]{2,1,0:T(8,128)(2,1)}, u32[]{:S(2)}, u32[]{:S(2)}) async-start(bf16[8,128,1024]{2,1,0:T(8,128)(2,1)} %bitcast.129), calls=%async_computation.1 | async-start | bytes 4194304 | tf_op jit(solution)/shard_map/all_to_all | solution.py:68
  140.4 8.2 %collective-permute-start.16 = (bf16[128,1024]{1,0:T(8,128)(2,1)S(1)}, bf16[128,1024]{1,0:T(8,128)(2,1)S(1)}, u32[]{:S(2)}, u32[]{:S(2)}) collective-permute-start(bf16[128,1024]{1,0:T(8,128)(2,1)S(1)} %collective-permute-done.10.refs_4_), channel_id=1, source_target_pairs={{0,6},{1,7},{2,0},{3,1},{4,2},{5,3},{6,4},{7,5},{8,14},{9,15},{10,... | collective-permute-start | bytes 786440 | tf_op jit(solution)/shard_map/ppermute | solution.py:52
  154.3 29.3 %all-to-all-start.2 = ((bf16[8,128,1024]{2,1,0:T(8,128)(2,1)}), bf16[8,128,1024]{2,1,0:T(8,128)(2,1)}, u32[]{:S(2)}, u32[]{:S(2)}) async-start(bf16[8,128,1024]{2,1,0:T(8,128)(2,1)} %bitcast.128), calls=%async_computation.2 | async-start | bytes 4194304 | tf_op jit(solution)/shard_map/all_to_all | solution.py:68
  162.0 10.2 %collective-permute-start.19 = (bf16[8,64,512]{2,1,0:T(8,128)(2,1)S(1)}, bf16[8,64,512]{2,1,0:T(8,128)(2,1)S(1)}, u32[]{:S(2)}, u32[]{:S(2)}) collective-permute-start(bf16[8,64,512]{2,1,0:T(8,128)(2,1)S(1)} %dynamic-slice_bitcast_fusion.1), channel_id=1, source_target_pairs={{0,8},{8,0},{16,24},{24,16},{32,40},{40,32},{48,56},{56,48},{64,72... | collective-permute-start | bytes 1572872 | tf_op jit(solution)/shard_map/ppermute | solution.py:88
  186.9 12.0 %collective-permute-start.21 = (bf16[128,1024]{1,0:T(8,128)(2,1)S(1)}, bf16[128,1024]{1,0:T(8,128)(2,1)S(1)}, u32[]{:S(2)}, u32[]{:S(2)}) collective-permute-start(bf16[128,1024]{1,0:T(8,128)(2,1)S(1)} %get-tuple-element.70.refs_3_), channel_id=1, source_target_pairs={{0,2},{1,3},{2,4},{3,5},{4,6},{5,7},{6,0},{7,1},{8,10},{9,11},{10,... | collective-permute-start | bytes 786440 | tf_op jit(solution)/shard_map/ppermute | solution.py:52
  186.9 13.1 %collective-permute-start.22 = (bf16[128,1024]{1,0:T(8,128)(2,1)S(1)}, bf16[128,1024]{1,0:T(8,128)(2,1)}, u32[]{:S(2)}, u32[]{:S(2)}) collective-permute-start(bf16[128,1024]{1,0:T(8,128)(2,1)S(1)} %get-tuple-element.70.refs_3_), channel_id=1, source_target_pairs={{0,6},{1,7},{2,0},{3,1},{4,2},{5,3},{6,4},{7,5},{8,14},{9,15},{10,... | collective-permute-start | bytes 786440 | tf_op jit(solution)/shard_map/ppermute | solution.py:52
  189.5 13.1 %collective-permute-start.20 = (bf16[128,1024]{1,0:T(8,128)(2,1)S(1)}, bf16[128,1024]{1,0:T(8,128)(2,1)}, u32[]{:S(2)}, u32[]{:S(2)}) collective-permute-start(bf16[128,1024]{1,0:T(8,128)(2,1)S(1)} %get-tuple-element.70.refs_3_), channel_id=1, source_target_pairs={{0,1},{1,0},{2,3},{3,2},{4,5},{5,4},{6,7},{7,6},{8,9},{9,8},{10,11... | collective-permute-start | bytes 786440 | tf_op jit(solution)/shard_map/ppermute | solution.py:52
  189.5 20.1 %all-to-all-start.3 = ((bf16[64,8,512]{2,1,0:T(8,128)(2,1)}), bf16[64,8,512]{2,1,0:T(8,128)(2,1)S(1)}, u32[]{:S(2)}, u32[]{:S(2)}) async-start(bf16[64,8,512]{2,1,0:T(8,128)(2,1)} %bitcast.130), calls=%async_computation.3 | async-start | bytes 1048576 | tf_op jit(solution)/shard_map/all_to_all | solution.py:565
  202.6 11.8 %collective-permute-start.25 = (bf16[128,1024]{1,0:T(8,128)(2,1)}, bf16[128,1024]{1,0:T(8,128)(2,1)}, u32[]{:S(2)}, u32[]{:S(2)}) collective-permute-start(bf16[128,1024]{1,0:T(8,128)(2,1)} %collective-permute-done.20.refs_4_), channel_id=1, source_target_pairs={{0,2},{1,3},{2,4},{3,5},{4,6},{5,7},{6,0},{7,1},{8,10},{9,11},{10,... | collective-permute-start | bytes 786440 | tf_op jit(solution)/shard_map/ppermute | solution.py:52
  202.6 11.8 %collective-permute-start.26 = (bf16[128,1024]{1,0:T(8,128)(2,1)}, bf16[128,1024]{1,0:T(8,128)(2,1)}, u32[]{:S(2)}, u32[]{:S(2)}) collective-permute-start(bf16[128,1024]{1,0:T(8,128)(2,1)} %collective-permute-done.20.refs_4_), channel_id=1, source_target_pairs={{0,6},{1,7},{2,0},{3,1},{4,2},{5,3},{6,4},{7,5},{8,14},{9,15},{10,... | collective-permute-start | bytes 786440 | tf_op jit(solution)/shard_map/ppermute | solution.py:52
  218.9 48.9 %all-to-all-start.4 = ((bf16[8,128,1024]{2,1,0:T(8,128)(2,1)}), bf16[8,128,1024]{2,1,0:T(8,128)(2,1)}, u32[]{:S(2)}, u32[]{:S(2)}) async-start(bf16[8,128,1024]{2,1,0:T(8,128)(2,1)} %bitcast.126), calls=%async_computation.4 | async-start | bytes 4194304 | tf_op jit(solution)/shard_map/all_to_all | solution.py:68
  223.4 184.3 %all-reduce.4.cloned.1.call-start = ((), (), s32[]{:S(2)}) async-start(), calls=%async_computation.7 | async-start | bytes 2097152 | tf_op jit(solution)/shard_map/psum | solution.py:612
  251.5 13.6 %collective-permute-start.29 = (bf16[8,64,896]{2,1,0:T(8,128)(2,1)}, bf16[8,64,896]{2,1,0:T(8,128)(2,1)}, u32[]{:S(2)}, u32[]{:S(2)}) collective-permute-start(bf16[8,64,896]{2,1,0:T(8,128)(2,1)} %dynamic-slice_bitcast_fusion), channel_id=1, source_target_pairs={{0,8},{8,0},{16,24},{24,16},{32,40},{40,32},{48,56},{56,48},{64,72... | collective-permute-start | bytes 2752520 | tf_op jit(solution)/shard_map/ppermute | solution.py:88
  267.8 142.6 %all-to-all-start.5 = ((bf16[64,8,896]{2,1,0:T(8,128)(2,1)}), bf16[64,8,896]{2,1,0:T(8,128)(2,1)S(1)}, u32[]{:S(2)}, u32[]{:S(2)}) async-start(bf16[64,8,896]{2,1,0:T(8,128)(2,1)} %bitcast.127), calls=%async_computation.5 | async-start | bytes 1835008 | tf_op jit(solution)/shard_map/all_to_all | solution.py:565
  411.9 21.3 %all-to-all-start.6 = ((bf16[8,8,8320]{2,1,0:T(8,128)(2,1)}), bf16[8,8,8320]{2,1,0:T(8,128)(2,1)S(1)}, u32[]{:S(2)}, u32[]{:S(2)}) async-start(bf16[8,8,8320]{2,1,0:T(8,128)(2,1)} %broadcast_in_dim.52), calls=%async_computation.6 | async-start | bytes 2129920 | tf_op jit(solution)/shard_map/all_to_all | solution.py:620
  424.6 16.7 %collective-permute-start.30 = (bf16[128,1024]{1,0:T(8,128)(2,1)}, bf16[128,1024]{1,0:T(8,128)(2,1)}, u32[]{:S(2)}, u32[]{:S(2)}) collective-permute-start(bf16[128,1024]{1,0:T(8,128)(2,1)} %get-tuple-element.132), channel_id=1, source_target_pairs={{0,1},{1,0},{2,3},{3,2},{4,5},{5,4},{6,7},{7,6},{8,9},{9,8},{10,11... | collective-permute-start | bytes 786440 | tf_op jit(solution)/shard_map/ppermute | solution.py:81
  424.9 19.7 %collective-permute-start.31 = (bf16[128,1024]{1,0:T(8,128)(2,1)}, bf16[128,1024]{1,0:T(8,128)(2,1)}, u32[]{:S(2)}, u32[]{:S(2)}) collective-permute-start(bf16[128,1024]{1,0:T(8,128)(2,1)} %get-tuple-element.138), channel_id=1, source_target_pairs={{0,2},{1,3},{2,0},{3,1},{4,6},{5,7},{6,4},{7,5},{8,10},{9,11},{10,... | collective-permute-start | bytes 786440 | tf_op jit(solution)/shard_map/ppermute | solution.py:81
  426.0 19.4 %collective-permute-start.32 = (bf16[128,1024]{1,0:T(8,128)(2,1)}, bf16[128,1024]{1,0:T(8,128)(2,1)}, u32[]{:S(2)}, u32[]{:S(2)}) collective-permute-start(bf16[128,1024]{1,0:T(8,128)(2,1)} %get-tuple-element.137), channel_id=1, source_target_pairs={{0,3},{1,2},{2,1},{3,0},{4,7},{5,6},{6,5},{7,4},{8,11},{9,10},{10,... | collective-permute-start | bytes 786440 | tf_op jit(solution)/shard_map/ppermute | solution.py:81
  428.9 19.6 %collective-permute-start.33 = (bf16[128,1024]{1,0:T(8,128)(2,1)}, bf16[128,1024]{1,0:T(8,128)(2,1)}, u32[]{:S(2)}, u32[]{:S(2)}) collective-permute-start(bf16[128,1024]{1,0:T(8,128)(2,1)} %get-tuple-element.136), channel_id=1, source_target_pairs={{0,4},{1,5},{2,6},{3,7},{4,0},{5,1},{6,2},{7,3},{8,12},{9,13},{10,... | collective-permute-start | bytes 786440 | tf_op jit(solution)/shard_map/ppermute | solution.py:81
  433.2 32.3 %collective-permute-start.37 = (bf16[64,8320]{1,0:T(8,128)(2,1)S(1)}, bf16[64,8320]{1,0:T(8,128)(2,1)S(1)}, u32[]{:S(2)}, u32[]{:S(2)}) collective-permute-start(bf16[64,8320]{1,0:T(8,128)(2,1)S(1)} %bitcast.118), channel_id=1, source_target_pairs={{0,8},{8,0},{16,24},{24,16},{32,40},{40,32},{48,56},{56,48},{64,72... | collective-permute-start | bytes 3194888 | tf_op jit(solution)/shard_map/ppermute | solution.py:88
  441.3 10.1 %collective-permute-start.34 = (bf16[128,1024]{1,0:T(8,128)(2,1)S(1)}, bf16[128,1024]{1,0:T(8,128)(2,1)S(1)}, u32[]{:S(2)}, u32[]{:S(2)}) collective-permute-start(bf16[128,1024]{1,0:T(8,128)(2,1)S(1)} %copy-done.45), channel_id=1, source_target_pairs={{0,5},{1,4},{2,7},{3,6},{4,1},{5,0},{6,3},{7,2},{8,13},{9,12},{10,... | collective-permute-start | bytes 786440 | tf_op jit(solution)/shard_map/ppermute | solution.py:81
  444.5 12.2 %collective-permute-start.35 = (bf16[128,1024]{1,0:T(8,128)(2,1)S(1)}, bf16[128,1024]{1,0:T(8,128)(2,1)S(1)}, u32[]{:S(2)}, u32[]{:S(2)}) collective-permute-start(bf16[128,1024]{1,0:T(8,128)(2,1)S(1)} %copy-done.44), channel_id=1, source_target_pairs={{0,6},{1,7},{2,4},{3,5},{4,2},{5,3},{6,0},{7,1},{8,14},{9,15},{10,... | collective-permute-start | bytes 786440 | tf_op jit(solution)/shard_map/ppermute | solution.py:81
  445.4 17.3 %collective-permute-start.36 = (bf16[128,1024]{1,0:T(8,128)(2,1)S(1)}, bf16[128,1024]{1,0:T(8,128)(2,1)S(1)}, u32[]{:S(2)}, u32[]{:S(2)}) collective-permute-start(bf16[128,1024]{1,0:T(8,128)(2,1)S(1)} %copy-done.43), channel_id=1, source_target_pairs={{0,7},{1,6},{2,5},{3,4},{4,3},{5,2},{6,1},{7,0},{8,15},{9,14},{10,... | collective-permute-start | bytes 786440 | tf_op jit(solution)/shard_map/ppermute | solution.py:81
  (64 other events, 872.1 us)
Sparse Core Ops, SparseCore 0:
  259.3 148.3 all-reduce.3

commit v3 on v2

--- a/solution.py
+++ b/solution.py
@@ -57,6 +57,21 @@
     return x, z, a, b, c0, c1, za, zb, zc0, zc1
 
 
+def gather_with_weights(x, packed):
+    h = x.shape[0] // 2
+    send = lambda v, perm: lax.ppermute(v, "seq", perm)
+    z, a, b = send(x, Z_SWAP), send(x, x_shift(1)), send(x, x_shift(-1))
+    z, packed = lax.optimization_barrier((z, packed))
+    share = lax.all_to_all(packed, "seq", split_axis=0, concat_axis=0, tiled=True)
+    shares = round_y(share)
+    c0, c1 = send(a[:h], x_shift(1)), send(b[h:], x_shift(-1))
+    za, zb = send(z, x_shift(1)), send(z, x_shift(-1))
+    c0, c1, second = lax.optimization_barrier((c0, c1, shares[1]))
+    shares = (shares[0], second, *shares[2:])
+    zc = send(jnp.concatenate([c0, c1], axis=0), Z_SWAP)
+    return (x, z, a, b, c0, c1, za, zb, zc), (*shares, *(core_swap(v) for v in shares))
+
+
 def piece_row(me, place):
     dx, other, off = place
     mx, mz = me // 2, me % 2
@@ -66,22 +81,15 @@
 
 def scatter_rows(part, beside=()):
     got = lax.all_to_all(part.reshape(SEQ, ROWS, D), "seq", split_axis=0, concat_axis=0, tiled=True)
-    if not beside:
-        return got.astype(F32).sum(0)
-    got, *beside = lax.optimization_barrier((got, *beside))
-    return got.astype(F32).sum(0), beside
-
-
-def scatter_rows_direct(part, me):
-    part = part.reshape(SEQ, ROWS, D)
-    total = lax.dynamic_index_in_dim(part, me, 0, False).astype(F32)
-    got = []
-    for k in range(1, SEQ):
-        own = lax.dynamic_index_in_dim(part, me ^ k, 0, False)
-        got.append(lax.ppermute(own, "seq", [(i, i ^ k) for i in range(SEQ)]))
-    for v in got:
-        total = total + v.astype(F32)
-    return total
+    return lax.optimization_barrier((got, *beside))
+
+
+def y_shift(v, k):
+    return lax.ppermute(v, "dp", [(i, (i // 4 + k) % 4 * 4 + i % 4) for i in range(DP)])
+
+
+def round_y(v):
+    return v, y_shift(v, 3), y_shift(v, 2), y_shift(v, 1)
 
 
 def core_swap(v):
@@ -146,20 +154,21 @@
 
 def mixer_forward_kernel(*refs):
     (
-        where, w_mine, w_other, small_ref, out_w, *pieces,
-        unit, ffn_grad, in_w, gu_w, proj, mix, y_out, states, log_totals, mid_part, keys, values,
+        where, small_ref, out_w, *pieces,
+        unit, in_w, gu_w, proj, mix, y_out, states, log_totals, mid_part, keys, values,
     ) = refs
-    me, core = where[0], where[1]
+    me, core, y = where[0], where[1], where[2]
+    shares, pieces = pieces[:8], pieces[8:]
     for piece, place in zip(pieces, PLACES):
         rows = pl.ds(piece_row(me, place), piece.shape[0])
         unit[rows, :] = unit_rows(piece[:, :D].astype(F32)).astype(BF)
-        ffn_grad[rows, :] = piece[:, D:]
-    half = ROWS // 2
-    for j in range(SEQ):
-        for source, at in ((w_mine, core * half), (w_other, half - core * half)):
-            rows = pl.ds(pl.multiple_of(at + j * ROWS, half), half)
-            in_w[rows, :] = source[j, :, :CW]
-            gu_w[rows, :] = source[j, :, CW:]
+    for k, share in enumerate(shares):
+        from_core = core if k < 4 else 1 - core
+        first = (y + k) % 4 * 32 + from_core * 16
+        for j in range(SEQ):
+            rows = pl.ds(pl.multiple_of(j * ROWS + first, 16), 16)
+            in_w[rows, :] = share[j, :, :CW]
+            gu_w[rows, :] = share[j, :, CW:]
     small = small_ref[...]
     state = jnp.zeros((HW, NS), F32)
     for c in range(NCH):
@@ -215,11 +224,12 @@
     ones_low = low.astype(F32)
     lane8 = lax.broadcasted_iota(jnp.int32, (HW, 8), 1)
     row8 = lax.broadcasted_iota(jnp.int32, (HW, 8), 0)
-    heads = (row8 // MP == lane8).astype(F32)
+    heads = (row8 // MP == lane8).astype(BF)
     lane_ch = lax.broadcasted_iota(jnp.int32, (CH, 8), 1)
+    lane_one = lax.broadcasted_iota(jnp.int32, (1, 8), 1)
     acc_bias = jnp.zeros((1, 8), F32)
     acc_decay = jnp.zeros((1, 8), F32)
-    acc_skip = jnp.zeros((1, 8), F32)
+    acc_skip = jnp.zeros((1, HW), F32)
     rate = jnp.exp(small[1:2, :])
     for c in reversed(range(NCH)):
         rows = slice(c * CH, (c + 1) * CH)
@@ -267,14 +277,20 @@
         g_grad = jnp.zeros((CH, CH), F32)
         v_grads = []
         cum_grad = jnp.zeros((CH, 8), F32)
+        columns = []
         for h in range(HL):
             pair = dot(jnp.where(head_mask(h, (CH, HW)), dyb, jnp.zeros_like(dyb)), vb, ((1,), (1,)))
             mixed_pair = decays[h] * pair
             g_grad = g_grad + mixed_pair
             v_grads.append(dot((decays[h] * g).astype(BF), dyb, ((0,), (0,))))
-            swing = (mixed_pair * g).astype(BF)
-            one = (lane_ch == h).astype(BF)
-            cum_grad = cum_grad + dot(swing, one) - dot(swing, one, ((0,), (0,)))
+            swing = mixed_pair * g
+            cum_grad = cum_grad + jnp.where(
+                lane_ch == h, jnp.sum(swing, axis=1, keepdims=True), 0.0
+            )
+            columns.append(jnp.sum(swing, axis=0, keepdims=True))
+        cum_grad = cum_grad - jnp.concatenate(
+            columns + [jnp.zeros((8 - HL, CH), F32)], axis=0
+        ).T
         v_grad = per_head(v_grads, (CH, HW)) + v_grad_inter
         g_gradb = g_grad.astype(BF)
         grown = (grow * dy).astype(BF)
@@ -283,43 +299,52 @@
             dot(g_gradb, cc, ((0,), (0,))) + dot((fade * v).astype(BF), qb)
         ).astype(BF)
         out[rows, CU : CU + HW] = (skip_w * dy + dt_w * v_grad).astype(BF)
-        per_state = dot(heads, state * state_grad, ((0,), (0,)), precision=HIGH)
-        over = dot(jnp.ones((8, NS), F32), per_state, ((1,), (1,)), precision=HIGH)[0:1, :]
-        behind = dot(v * v_grad_inter, heads, precision=HIGH)
-        ahead = cum_grad + dot(dy * y_inter, heads, precision=HIGH)
+        both = state * state_grad
+        over = jnp.zeros((1, 8), F32)
+        for h in range(HL):
+            one = jnp.sum(both[h * MP : (h + 1) * MP, :], axis=0, keepdims=True)
+            over = over + jnp.where(lane_one == h, jnp.sum(one, axis=1, keepdims=True), 0.0)
+        behind = dot((v * v_grad_inter).astype(BF), heads)
+        ahead = cum_grad + dot((dy * y_inter).astype(BF), heads)
         decay_grad = (
             dot(ones_low, ahead, ((0,), (0,)), precision=HIGH)
             + dot(ones_low, behind, precision=HIGH)
             - behind
             + jnp.exp(last) * over
         )
-        step_grad = dot(u * v_grad, heads, precision=HIGH) - rate * decay_grad
+        step_grad = dot((u * v_grad).astype(BF), heads) - rate * decay_grad
         r_grad = step_grad * jax.nn.sigmoid(pre)
         out[rows, CR : CR + HS] = jnp.concatenate(
             [r_grad, jnp.zeros((CH, HS - 8), F32)], axis=1
         ).astype(BF)
         acc_bias = acc_bias + jnp.sum(r_grad, axis=0, keepdims=True)
         acc_decay = acc_decay - rate * jnp.sum(dt * decay_grad, axis=0, keepdims=True)
-        acc_skip = acc_skip + dot(
-            jnp.broadcast_to(jnp.sum(dy * u, axis=0, keepdims=True), (8, HW)), heads, precision=HIGH
-        )[0:1, :]
+        acc_skip = acc_skip + jnp.sum(dy * u, axis=0, keepdims=True)
         state_grad = row_heads(jnp.exp(last)) * state_grad + dot(grown, cc, ((0,), (0,)))
-    sums[...] = jnp.concatenate([acc_bias, acc_decay, acc_skip, jnp.zeros((5, 8), F32)], axis=0)
+    skip_sum = jnp.zeros((1, 8), F32)
+    for h in range(HL):
+        one = jnp.sum(jnp.where(head_mask(h, (1, HW)), acc_skip, 0.0), axis=1, keepdims=True)
+        skip_sum = skip_sum + jnp.where(lane_one == h, one, 0.0)
+    sums[...] = jnp.concatenate([acc_bias, acc_decay, skip_sum, jnp.zeros((5, 8), F32)], axis=0)
 
 
 VMEM = pl.BlockSpec(memory_space=pltpu.VMEM)
-PARAMS = pltpu.CompilerParams(vmem_limit_bytes=50 * 1024 * 1024)
+def cost(us):
+    return pl.CostEstimate(flops=int(us * 1e9), bytes_accessed=1 << 20, transcendentals=0)
+
+
+def params(mib):
+    return pltpu.CompilerParams(vmem_limit_bytes=mib * 1024 * 1024)
 
 
 SMEM = pl.BlockSpec(memory_space=pltpu.SMEM)
 
 
-def mixer_forward(where, w_mine, w_other, small, out_w, pieces):
+def mixer_forward(where, small, out_w, shares, pieces):
     shape = jax.ShapeDtypeStruct
     return pl.pallas_call(
         mixer_forward_kernel,
         out_shape=(
-            shape((TOK, D), BF),
             shape((TOK, D), BF),
             shape((D, CW), BF),
             shape((D, 2 * FL), BF),
@@ -330,11 +355,12 @@
             shape((TOK, 8), F32),
             shape((TOK, D), BF),
         ),
-        in_specs=[SMEM] + [VMEM] * 14,
-        out_specs=(VMEM,) * 10,
+        in_specs=[SMEM] + [VMEM] * 19,
+        out_specs=(VMEM,) * 9,
         scratch_shapes=[pltpu.VMEM((TOK, HS), BF), pltpu.VMEM((TOK, HS), BF)],
-        compiler_params=PARAMS,
-    )(where, w_mine, w_other, small, out_w, *pieces)
+        cost_estimate=cost(16),
+        compiler_params=params(50),
+    )(where, small, out_w, *shares, *pieces)
 
 
 def feed_forward_kernel(*refs):
@@ -362,8 +388,30 @@
         ),
         in_specs=[SMEM] + [VMEM] * 12,
         out_specs=(VMEM,) * 4,
-        compiler_params=PARAMS,
+        cost_estimate=cost(6),
+        compiler_params=params(50),
     )(where, gu_w, act_grad, *pieces)
+
+
+def output_gradients_kernel(*refs):
+    where, down_w, *pieces, ffn_grad, act_grad = refs
+    for piece, place in zip(pieces, PLACES):
+        ffn_grad[pl.ds(piece_row(where[0], place), piece.shape[0]), :] = piece[:, D:]
+    for c in range(NCH):
+        rows = slice(c * CH, (c + 1) * CH)
+        act_grad[rows, :] = dot(ffn_grad[rows, :], down_w[...], ((1,), (1,))).astype(BF)
+
+
+def output_gradients(where, down_w, pieces):
+    shape = jax.ShapeDtypeStruct
+    return pl.pallas_call(
+        output_gradients_kernel,
+        out_shape=(shape((TOK, D), BF), shape((TOK, FL), BF)),
+        in_specs=[SMEM] + [VMEM] * 10,
+        out_specs=(VMEM,) * 2,
+        cost_estimate=cost(3),
+        compiler_params=params(50),
+    )(where, down_w, *pieces)
 
 
 def branch_kernel(*refs):
@@ -384,7 +432,8 @@
         in_specs=[SMEM] + [VMEM] * 12,
         out_specs=(VMEM,) * 2,
         scratch_shapes=[pltpu.VMEM((TOK, D), BF)],
-        compiler_params=PARAMS,
+        cost_estimate=cost(3),
+        compiler_params=params(50),
     )(where, out_w, mix, *pieces)
 
 
@@ -400,13 +449,13 @@
             pltpu.VMEM((TOK, HS), F32),
             pltpu.VMEM((TOK, HS), F32),
         ],
-        compiler_params=PARAMS,
+        cost_estimate=cost(19),
+        compiler_params=params(50),
     )(proj, small, y, states, log_totals, mix_grad)
 
 
 def pack_weights_kernel(where, mixer_w, attn_w, gate_up, gains, out):
-    half = ROWS // 2
-    rows = pl.ds(pl.multiple_of(where[1] * half, half), half)
+    rows = pl.ds(pl.multiple_of(where[2] * 32 + where[1] * 16, 16), 16)
     g1, g2 = gains[rows, 0:1], gains[rows, 1:2]
     lane = lax.broadcasted_iota(jnp.int32, (MH, HS), 1)
     sub = lax.broadcasted_iota(jnp.int32, (MH, HS), 0)
@@ -433,10 +482,11 @@
 def pack_weights(where, mixer_w, attn_w, gate_up, gains):
     return pl.pallas_call(
         pack_weights_kernel,
-        out_shape=jax.ShapeDtypeStruct((SEQ, ROWS // 2, CW + 2 * FL), BF),
+        out_shape=jax.ShapeDtypeStruct((SEQ, 16, CW + 2 * FL), BF),
         in_specs=[SMEM] + [VMEM] * 4,
         out_specs=VMEM,
-        compiler_params=PARAMS,
+        cost_estimate=cost(1),
+        compiler_params=params(50),
     )(where, mixer_w, attn_w, gate_up, gains)
 
 
@@ -447,10 +497,14 @@
 
 WA0 = WMP
 WO0 = WMP + WA
-WALL = WO0 + 2 * FF
-
-
-def mixer_rows_kernel(got, got_gu, out, rows):
+WD0 = WO0 + 2 * FF
+WALL = WD0 + 4 * D
+
+
+def mixer_rows_kernel(got, got_gu, thin, out, rows):
+    thin_rows = thin[...].astype(F32)
+    for k in range(4):
+        rows[:, WD0 + k * D : WD0 + (k + 1) * D] = thin_rows[k * 8 : (k + 1) * 8, :]
     for s in range(SEQ):
         rows[:, WO0 + s * 2 * FL : WO0 + (s + 1) * 2 * FL] = sum(
             got_gu[chip * SEQ + s].astype(F32) for chip in range(8)
@@ -482,26 +536,42 @@
     out[...] = rows[...].astype(BF)
 
 
-def mixer_rows(got, got_gu):
+def mixer_rows(got, got_gu, thin):
     return pl.pallas_call(
         mixer_rows_kernel,
         out_shape=jax.ShapeDtypeStruct((8, WALL), BF),
-        in_specs=[VMEM] * 2,
+        in_specs=[VMEM] * 3,
         out_specs=VMEM,
         scratch_shapes=[pltpu.VMEM((8, WALL), F32)],
-        compiler_params=PARAMS,
-    )(got, got_gu)
+        cost_estimate=cost(1),
+        compiler_params=params(50),
+    )(got, got_gu, thin)
 
 
 def finish_kernel(
-    where, mine, other, mixer_w, attn_w, gate_up, gains, mixer_out, attn_out, gate_up_out, gain, line, rows
+    where, mixer_w, attn_w, gate_up, gains, *refs,
 ):
+    blocks = refs[:8]
+    (
+    mixer_out, attn_out, gate_up_out, down_out, mamba_rows, attn_rows, gain, line, rows, thin,
+    ) = refs[8:]
+    core, y, high = where[1], where[2], where[3]
     half = ROWS // 2
-    core = where[1]
-    for source, at in ((mine, core * half), (other, half - core * half)):
-        for i in range(half // 16):
-            to = pl.ds(pl.multiple_of(at + i * 16, 16), 16)
-            rows[to, :] = source[i * 16 : (i + 1) * 16, :].astype(F32)
+    for n, block in enumerate(blocks):
+        block = block[...].astype(F32)
+        from_core, from_y = (core if n < 4 else 1 - core), (y + n) % 4
+        for part in range(2):
+            from_high = high if part == 0 else 1 - high
+            source = block[part * 8 : (part + 1) * 8, :]
+            to = pl.multiple_of(from_core * half + from_y * 16 + from_high * 8, 8)
+            rows[pl.ds(to, 8), :] = source[:, :WD0]
+            first = from_core * FL + from_y * 64 + from_high * 32
+            for k in range(4):
+                to = pl.multiple_of(first + k * 8, 8)
+                thin[pl.ds(to, 8), :] = source[:, WD0 + k * D : WD0 + (k + 1) * D]
+    down_out[...] = thin[:FL, :]
+    mamba_rows[...] = thin[FL : FL + HW, :]
+    attn_rows[...] = thin[FL + HW :, :]
     line[...] = rows[0:8, WM - MH : WMP] + rows[half : half + 8, WM - MH : WMP]
     for i in range(ROWS // 16):
         at = slice(i * 16, (i + 1) * 16)
@@ -509,7 +579,7 @@
         total = jnp.sum(mixer * mixer_w[at, :].astype(F32), axis=1, keepdims=True) + jnp.sum(
             attn * attn_w[at, :].astype(F32), axis=1, keepdims=True
         )
-        mixer_out[at, :] = mixer * g[:, 0:1]
+        rows[at, :WM] = mixer * g[:, 0:1]
         attn_out[at, :] = attn * g[:, 0:1]
         total_two = jnp.zeros((16, 1), F32)
         for s in range(SEQ):
@@ -521,20 +591,25 @@
                 )
                 gate_up_out[at, to] = block * g[:, 1:2]
         gain[at, :] = jnp.concatenate([total, total_two], axis=1)
-
-
-def finish(where, mine, other, mixer_w, attn_w, gate_up, gains):
+    for i in range(WMP // 128):
+        n = min(128, WM - i * 128)
+        mixer_out[i * 128 : i * 128 + n, :] = rows[:, i * 128 : (i + 1) * 128].T[:n, :]
+
+
+def finish(where, mixer_w, attn_w, gate_up, gains, blocks):
     shape = lambda *dims: jax.ShapeDtypeStruct(dims, F32)
     return pl.pallas_call(
         finish_kernel,
         out_shape=(
-            shape(ROWS, WM), shape(ROWS, WA), shape(ROWS, 2 * FF), shape(ROWS, 2), shape(8, 128),
+            shape(WM, ROWS), shape(ROWS, WA), shape(ROWS, 2 * FF), shape(FL, D), shape(HW, D), shape(HS, D),
+            shape(ROWS, 2), shape(8, 128),
         ),
-        in_specs=[SMEM] + [VMEM] * 6,
-        out_specs=(VMEM,) * 5,
-        scratch_shapes=[pltpu.VMEM((ROWS, WALL), F32)],
-        compiler_params=PARAMS,
-    )(where, mine, other, mixer_w, attn_w, gate_up, gains)
+        in_specs=[SMEM] + [VMEM] * 12,
+        out_specs=(VMEM,) * 8,
+        scratch_shapes=[pltpu.VMEM((ROWS, WD0), F32), pltpu.VMEM((2 * FL, D), F32)],
+        cost_estimate=cost(6),
+        compiler_params=params(32),
+    )(where, mixer_w, attn_w, gate_up, gains, *blocks)
 
 
 def unit_back(x, e):
@@ -542,8 +617,47 @@
     return rho * e - x * (rho * rho * rho) * jnp.mean(x * e, axis=-1, keepdims=True)
 
 
-def chip_groups():
-    return [list(range(c, DP, 2)) for c in range(2)]
+def arrived(got, rows):
+    return sum(got[k, rows, :].astype(F32) for k in range(SEQ))
+
+
+def over_rows():
+    return [slice(i * 16, (i + 1) * 16) for i in range(ROWS // 16)]
+
+
+def mid_kernel(got, x, mid, unit):
+    for rows in over_rows():
+        value = x[rows, :].astype(F32) + arrived(got, rows)
+        mid[rows, :] = value
+        unit[rows, :] = unit_rows(value).astype(BF)
+
+
+def mid_grad_kernel(got, cot, mid, grad, low):
+    for rows in over_rows():
+        value = cot[rows, :].astype(F32) + unit_back(mid[rows, :], arrived(got, rows))
+        grad[rows, :] = value
+        low[rows, :] = value.astype(BF)
+
+
+def input_grad_kernel(got, x, mid_grad, grad):
+    for rows in over_rows():
+        grad[rows, :] = mid_grad[rows, :] + unit_back(x[rows, :].astype(F32), arrived(got, rows))
+
+
+def output_kernel(got, mid, out):
+    for rows in over_rows():
+        out[rows, :] = (mid[rows, :] + arrived(got, rows)).astype(BF)
+
+
+def on_rows(kernel, kinds, *arrays):
+    return pl.pallas_call(
+        kernel,
+        out_shape=tuple(jax.ShapeDtypeStruct((ROWS, D), kind) for kind in kinds),
+        in_specs=[VMEM] * len(arrays),
+        out_specs=(VMEM,) * len(kinds),
+        cost_estimate=cost(2),
+        compiler_params=params(16),
+    )(*arrays)
 
 
 def core_sum(grad, core, line=None):
@@ -561,6 +675,14 @@
     return both.astype(BF).reshape(SEQ, 8, 8, n).swapaxes(0, 1).reshape(64, 8, n)
 
 
+def halved(v, mine, bit):
+    v = v.reshape(2, v.shape[0] // 2, v.shape[1])
+    other = lax.dynamic_index_in_dim(v, 1 - mine, 0, False)
+    other = lax.ppermute(other, "dp", [(i, i ^ bit) for i in range(DP)])
+    own = lax.dynamic_index_in_dim(v, mine, 0, False)
+    return (own.astype(F32) + other.astype(F32)).astype(BF)
+
+
 def to_owners(sent):
     return lax.all_to_all(
         sent, ("dp", "seq"), split_axis=0, concat_axis=0, tiled=True, axis_index_groups=same_core()
@@ -572,8 +694,10 @@
     norm_gains, step_bias, decay_log, skip_gain,
 ):
     me = lax.axis_index("seq")
-    core = lax.axis_index("dp") % 2
-    where = jnp.stack([me, core]).astype(jnp.int32)
+    group = lax.axis_index("dp")
+    core = group % 2
+    high = group // 2 % 2
+    where = jnp.stack([me, core, group // 4, high]).astype(jnp.int32)
     x0 = inputs[0]
     gains = norm_gains[0].astype(F32).T
     down_w = down_proj[0]
@@ -581,62 +705,64 @@
     small = jnp.concatenate([step_bias, decay_log, skip_gain], axis=0).astype(F32)
     small = jnp.pad(small, ((0, 5), (0, 8 - HL)))
 
-    pieces = gather_pieces(jnp.concatenate([x0, cotangent[0]], axis=1))
-    w_mine = lax.all_to_all(
-        pack_weights(where, mixer_in[0], attn_in[0], gate_up[0], gains),
-        "seq", split_axis=0, concat_axis=0, tiled=True,
+    packed = pack_weights(where, mixer_in[0], attn_in[0], gate_up[0], gains)
+    pieces, shares = gather_with_weights(jnp.concatenate([x0, cotangent[0]], axis=1), packed)
+    unit_one, in_w, gu_w, proj, mix, y, states, log_totals, mid_part = mixer_forward(
+        where, small, out_w, shares, pieces
     )
-    unit_one, ffn_grad, in_w, gu_w, proj, mix, y, states, log_totals, mid_part = mixer_forward(
-        where, w_mine, core_swap(w_mine), small, out_w, pieces
-    )
-    mid, (act_grad,) = scatter_rows(
-        mid_part, (dot(ffn_grad, down_w, ((1,), (1,))).astype(BF),)
-    )
-    mid = mid + x0.astype(F32)
+    ffn_grad, act_grad = output_gradients(where, down_w, pieces)
+    got, ffn_grad, act_grad = scatter_rows(mid_part, (ffn_grad, act_grad))
+    mid, unit_mid = on_rows(mid_kernel, (F32, BF), got, x0)
 
     unit_two, act, up_grad, e_part = feed_forward(
-        where, gu_w, act_grad, gather_pieces(unit_rows(mid).astype(BF))
+        where, gu_w, act_grad, gather_pieces(unit_mid)
     )
     gu_sent = core_sum(dot(unit_two, up_grad, ((0,), (0,))).astype(BF), core)
     down_grad = dot(act, ffn_grad, ((0,), (0,))).astype(BF)
-    mid_e, (gu_sent, out_part, down_grad) = scatter_rows(
+    got, gu_sent, out_part, down_grad = scatter_rows(
         e_part, (gu_sent, dot(act, down_w).astype(BF), down_grad)
     )
-    mid_grad = cotangent[0].astype(F32) + unit_back(mid, mid_e)
-    pieces = gather_pieces(mid_grad.astype(BF))
+    mid_grad, branch = on_rows(mid_grad_kernel, (F32, BF), got, cotangent[0], mid)
+    pieces = gather_pieces(branch)
     *pieces, gu_got = lax.optimization_barrier((*pieces, to_owners(gu_sent)))
 
     mix_grad, out_grad = branch_products(where, out_w, mix, pieces)
-    out_part, mix_grad = lax.optimization_barrier((out_part, mix_grad))
+    thin = halved(jnp.concatenate([down_grad, out_grad], axis=0), core, 1)
+    mix_grad, out_part = lax.optimization_barrier((mix_grad, out_part))
+    mix_grad, thin = lax.optimization_barrier((mix_grad, thin))
     proj_grad, sums = mixer_backward(proj, small, y, states, log_totals, mix_grad)
-    row_sums = lax.psum(jnp.concatenate([down_grad, out_grad], axis=0), "dp")
+    proj_grad, thin = lax.optimization_barrier((proj_grad, halved(thin, group // 8, 8)))
     in_grad = dot(unit_one, proj_grad, ((0,), (0,))).astype(BF)
+    thin = halved(thin, group // 4 % 2, 4)
     line = jnp.concatenate([sums[0, :HL], sums[1, :HL], sums[2, :HL]])
     line = jnp.pad(line, (CR + 8, CW - CR - 8 - 3 * HL))
+    result, sent = scatter_rows(out_part, (core_sum(in_grad, core, line),))
+    (outputs,) = on_rows(output_kernel, (BF,), result, mid)
+    sent, proj_grad, thin = lax.optimization_barrier((sent, proj_grad, thin))
     e_part = dot(proj_grad, in_w, ((1,), (1,))).astype(BF)
-    result, (sent, e_part) = scatter_rows(out_part, (core_sum(in_grad, core, line), e_part))
-    outputs = (mid + result).astype(BF)
-    rows = mixer_rows(to_owners(sent), gu_got)
-    mine = lax.all_to_all(
-        jnp.broadcast_to(rows[None], (8, 8, WALL)), "dp", split_axis=0, concat_axis=0, tiled=True,
-        axis_index_groups=chip_groups(),
-    ).reshape(ROWS // 2, WALL)
-    in_e = scatter_rows_direct(e_part, me)
-    input_grad = mid_grad + unit_back(x0.astype(F32), in_e)
-    mixer_g, attn_g, gate_up_g, gain, line = finish(
-        where, mine, core_swap(mine), mixer_in[0], attn_in[0], gate_up[0], gains
+    e_part, thin = lax.optimization_barrier((e_part, thin))
+    thin = halved(thin, high, 2)
+    got, outputs = lax.optimization_barrier((to_owners(sent), outputs))
+    rows = mixer_rows(got, gu_got, thin)
+    other_rows = lax.ppermute(rows, "dp", [(i, i ^ 2) for i in range(DP)])
+    other_rows, e_part = lax.optimization_barrier((other_rows, e_part))
+    blocks = round_y(jnp.concatenate([rows, other_rows], axis=0))
+    blocks = (*blocks, *(core_swap(v) for v in blocks))
+    (got,) = scatter_rows(e_part)
+    (input_grad,) = on_rows(input_grad_kernel, (F32,), got, x0, mid_grad)
+    mixer_g, attn_g, gate_up_g, down_g, mamba_out_g, attn_out_g, gain, line = finish(
+        where, mixer_in[0], attn_in[0], gate_up[0], gains, blocks
     )
-    row_sums = row_sums.astype(F32)
     line = line[0:1, MH : MH + 3 * HL]
     return (
         outputs[None],
         input_grad[None],
-        mixer_g[None],
+        mixer_g.T[None],
         attn_g[None],
-        row_sums[None, FL : FL + HW],
-        row_sums[None, FL + HW :],
+        mamba_out_g[None],
+        attn_out_g[None],
         gate_up_g[None],
-        row_sums[None, :FL],
+        down_g[None],
         gain.T[None],
         line[:, :HL],
         line[:, HL : 2 * HL],

time: 488 us -> 326 us (0.67)
  waiting for transfers between devices: 225 us -> 102 us
  blocking collectives: 24.7 us -> 11.3 us
  between operations: 14.9 us -> 1.52 us
  other arithmetic: 17.1 us -> 6.39 us
  starting transfers between devices: 97.4 us -> 106 us
  local copies, waits for them, and re-layouts: 31.8 us -> 23.7 us
    psum x1 -> x0, waiting for transfers between devices: 130 us -> none  [local(): row_sums = lax.psum(jnp.concatenate([down_grad, out_grad], axis=0), 'dp')]
    ppermute x7 -> x19, waiting for transfers between devices: 20.2 us -> 39.5 us  [the longest x8 15.2 us: gather_with_weights(): send = lambda v, perm: lax.ppermute(v, 'seq', perm)]
    ppermute x7 -> x19, starting transfers between devices: 11.6 us -> 27.5 us  [the longest x8 11.4 us: gather_with_weights(): send = lambda v, perm: lax.ppermute(v, 'seq', perm)]
    ppermute x27 -> x18, waiting for transfers between devices: 36.5 us -> 21.1 us  [gather_pieces(): send = lambda v, perm: lax.ppermute(v, 'seq', perm)]
    all_to_all x1, blocking collectives: 24.7 us -> 11.3 us  [gather_with_weights(): lax.all_to_all(packed, 'seq', split_axis=0, concat_axis=0, tiled=True)]
    ppermute x27 -> x18, starting transfers between devices: 30.8 us -> 19.6 us  [gather_pieces(): send = lambda v, perm: lax.ppermute(v, 'seq', perm)]
    reduce_sum x6 -> x0, other arithmetic: 8.31 us -> none  [the longest x3 6.2 us: scatter_rows(): return (got.astype(F32).sum(0), beside)]
    pallas_call x1 -> x6, Pallas kernels: 4.25 us -> 12.2 us  [the longest x1 4.72 us: finish(): pl.pallas_call(finish_kernel, out_shape=(shape(WM, ROWS), shape(ROWS, WA)...]
  transfers between devices with their start and end apart: 45 -> 53, of which waited for: 20 -> 21; matrix products, arithmetic and copies ran while one was open for 9% -> 9% of each run, Pallas kernels for 4% -> 8%
where the time goes in v3:
time: 326 us; the launch traced here: 320 us
  starting transfers between devices  106 us (33%)
  waiting for transfers between devices  102 us (31%)
  Pallas kernels  52 us (16%)
  local copies, waits for them, and re-layouts  23.7 us (7%)
  matrix products  16.7 us (5%)
  blocking collectives  11.3 us (3%)
  other arithmetic  6.39 us (2%)
    all_to_all x4, waiting for transfers between devices, scatter_rows(): lax.all_to_all(part.reshape(SEQ, ROWS, D), 'seq', split_axis=0, concat_ax...  37.2 us
    ppermute x10, starting transfers between devices, core_swap(): return lax.ppermute(v, 'dp', [(i, i ^ 1) for i in range(DP)])  23.3 us
    ppermute x18, waiting for transfers between devices, gather_pieces(): send = lambda v, perm: lax.ppermute(v, 'seq', perm)  21.1 us
    all_to_all x4, starting transfers between devices, scatter_rows(): lax.all_to_all(part.reshape(SEQ, ROWS, D), 'seq', split_axis=0, concat_ax...  20.8 us
    ppermute x18, starting transfers between devices, gather_pieces(): send = lambda v, perm: lax.ppermute(v, 'seq', perm)  19.6 us
    unnamed x103, local copies, waits for them, and re-layouts  18.2 us
    dot_general x5, matrix products, dot(): lax.dot_general(a, b, (dims, ((), ())), precision=precision, preferred_el...  16.7 us
    pallas_call x1, Pallas kernels, mixer_forward(): pl.pallas_call(mixer_forward_kernel, out_shape=(shape((TOK, D), BF), shap...  15.7 us
  transfers between devices with their start and end apart: 53, of which 21 were waited for; matrix products, arithmetic and copies ran while one was open for 9% of the time, Pallas kernels for 8%

profile of v3, /device:TPU:1, one launch (start us, length us, event | category | flops | bytes accessed | tf_op | source)
XLA Modules:
  0.0 320.1 jit_solution(13967940469764156277)
XLA Ops:
  12.0 4.1 %collective-permute-done.refs_12_.refs_3_ = bf16[128,2048]{1,0:T(8,128)(2,1)} collective-permute-done((bf16[128,2048]{1,0:T(8,128)(2,1)S(1)}, bf16[128,2048]{1,0:T(8,128)(2,1)}, u32[]{:S(2)}, u32[]{:S(2)}) %collective-permute-start) | collective-permute-done | bytes 524320 | tf_op jit(solution)/shard_map/ppermute | solution.py:62
  16.1 11.3 %all_to_all.35.refs_3_ = bf16[8,16,1408]{2,1,0:T(8,128)(2,1)S(1)} all-to-all(bf16[8,16,1408]{2,1,0:T(8,128)(2,1)S(1)} %shard_map.211), channel_id=1, replica_groups=mesh['dp'=16,'seq'=8] {'seq'}, dimensions={0} | all-to-all | bytes 720896 | tf_op jit(solution)/shard_map/all_to_all | solution.py:65
  38.4 10.8 %collective-permute-done.12.refs_17_.refs_8_ = bf16[128,2048]{1,0:T(8,128)(2,1)S(1)} collective-permute-done((bf16[128,2048]{1,0:T(8,128)(2,1)}, bf16[128,2048]{1,0:T(8,128)(2,1)S(1)}, u32[]{:S(2)}, u32[]{:S(2)}) %collective-permute-start.12) | collective-permute-done | bytes 524320 | tf_op jit(solution)/shard_map/ppermute | solution.py:62
  53.0 3.9 %collective-permute-start.11 = (bf16[8,16,1408]{2,1,0:T(8,128)(2,1)S(1)}, bf16[8,16,1408]{2,1,0:T(8,128)(2,1)S(1)}, u32[]{:S(2)}, u32[]{:S(2)}) collective-permute-start(bf16[8,16,1408]{2,1,0:T(8,128)(2,1)S(1)} %collective-permute-done.7.refs_6_), channel_id=1, source_target_pairs={{0,8},{8,0},{16,24},{24,16},{32,40},{40,32},{48,56},{56,48},{64,72... | collective-permute-start | bytes 1081352 | tf_op jit(solution)/shard_map/ppermute | solution.py:96
  59.0 15.7 %shard_map.212 = (bf16[1024,1024]{1,0:T(8,128)(2,1)}, bf16[1024,896]{1,0:T(8,128)(2,1)}, bf16[1024,512]{1,0:T(8,128)(2,1)}, f32[1024,896]{1,0:T(8,128)}, bf16[10...) custom-call(s32[4]{0:T(128)S(1)} %pad_add_fusion.where.refs_0_, ...), custom_call_target="tpu_custom_call" | custom-call | flops 16000000000 | bytes 1048576 | tf_op jit(solution)/shard_map/pallas_call | solution.py:345
  75.5 3.7 %all-to-all-start.1 = ((bf16[8,128,1024]{2,1,0:T(8,128)(2,1)}), bf16[8,128,1024]{2,1,0:T(8,128)(2,1)S(1)}, u32[]{:S(2)}, u32[]{:S(2)}) async-start(bf16[8,128,1024]{2,1,0:T(8,128)(2,1)} %bitcast.120), calls=%async_computation.1 | async-start | bytes 4194304 | tf_op jit(solution)/shard_map/all_to_all | solution.py:83
  82.2 3.7 %shard_map.213 = (bf16[1024,1024]{1,0:T(8,128)(2,1)}, bf16[1024,256]{1,0:T(8,128)(2,1)S(1)}) custom-call(s32[4]{0:T(128)S(1)} %pad_add_fusion.where.refs_0_, bf16[256,1024]{1,0:T(8,128)(2,1)S(1)} %bitcast.103, bf16[128,2048]{1,0:T(8,128)(2,1)S(1)} %copy-done.4, bf16[128,2048]{1,0:T(8,128)(2,1)} %collective-permute-done.refs_12_.refs_3_, ...), custom_call_target="tpu_custom_call" | custom-call | flops 3000000000 | bytes 1048576 | tf_op jit(solution)/shard_map/pallas_call | solution.py:407
  86.6 23.7 %all-to-all-done.1.got = bf16[8,128,1024]{2,1,0:T(8,128)(2,1)S(1)} async-done(((bf16[8,128,1024]{2,1,0:T(8,128)(2,1)}), bf16[8,128,1024]{2,1,0:T(8,128)(2,1)S(1)}, u32[]{:S(2)}, u32[]{:S(2)}) %all-to-all-start.1) | async-done | bytes 2097184 | tf_op jit(solution)/shard_map/all_to_all | solution.py:83
  114.6 4.0 %collective-permute-done.16.refs_5_ = bf16[128,1024]{1,0:T(8,128)(2,1)S(1)} collective-permute-done((bf16[128,1024]{1,0:T(8,128)(2,1)S(1)}, bf16[128,1024]{1,0:T(8,128)(2,1)S(1)}, u32[]{:S(2)}, u32[]{:S(2)}) %collective-permute-start.16) | collective-permute-done | bytes 262176 | tf_op jit(solution)/shard_map/ppermute | solution.py:52
  124.5 3.0 collective-permute-done.19.refs_8_
  131.3 5.6 %shard_map.215 = (bf16[1024,1024]{1,0:T(8,128)(2,1)}, bf16[1024,256]{1,0:T(8,128)(2,1)S(1)}, bf16[1024,512]{1,0:T(8,128)(2,1)}, bf16[1024,1024]{1,0:T(8,128)(2,1)}) custom-call(s32[4]{0:T(128)S(1)} %pad_add_fusion.where.refs_0_, bf16[1024,512]{1,0:T(8,128)(2,1)} %get-tuple-element.89.refs_1_, bf16[1024,256]{1,0:T(8,128)(2,1)S(1)} %copy-done.29, ...), custom_call_target="tpu_custom_call" | custom-call | flops 6000000000 | bytes 1048576 | tf_op jit(solution)/shard_map/pallas_call | solution.py:384
  136.9 5.1 %all-to-all-start.2 = ((bf16[8,128,1024]{2,1,0:T(8,128)(2,1)}), bf16[8,128,1024]{2,1,0:T(8,128)(2,1)S(1)}, u32[]{:S(2)}, u32[]{:S(2)}) async-start(bf16[8,128,1024]{2,1,0:T(8,128)(2,1)} %bitcast.119), calls=%async_computation.2 | async-start | bytes 4194304 | tf_op jit(solution)/shard_map/all_to_all | solution.py:83
  142.0 3.1 convolution_convert_fusion.3
  145.2 4.8 %collective-permute-start.24 = (bf16[8,64,512]{2,1,0:T(8,128)(2,1)S(1)}, bf16[8,64,512]{2,1,0:T(8,128)(2,1)S(1)}, u32[]{:S(2)}, u32[]{:S(2)}) collective-permute-start(bf16[8,64,512]{2,1,0:T(8,128)(2,1)S(1)} %dynamic-slice_bitcast_fusion.2), channel_id=1, source_target_pairs={{0,8},{8,0},{16,24},{24,16},{32,40},{40,32},{48,56},{56,48},{64,72... | collective-permute-start | bytes 1572872 | tf_op jit(solution)/shard_map/ppermute | solution.py:96
  154.7 13.5 %all-to-all-done.2.got = bf16[8,128,1024]{2,1,0:T(8,128)(2,1)S(1)} async-done(((bf16[8,128,1024]{2,1,0:T(8,128)(2,1)}), bf16[8,128,1024]{2,1,0:T(8,128)(2,1)S(1)}, u32[]{:S(2)}, u32[]{:S(2)}) %all-to-all-start.2) | async-done | bytes 2097184 | tf_op jit(solution)/shard_map/all_to_all | solution.py:83
  173.9 6.3 %all-to-all-start.3 = ((bf16[64,8,512]{2,1,0:T(8,128)(2,1)}), bf16[64,8,512]{2,1,0:T(8,128)(2,1)S(1)}, u32[]{:S(2)}, u32[]{:S(2)}) async-start(bf16[64,8,512]{2,1,0:T(8,128)(2,1)} %bitcast.121), calls=%async_computation.3 | async-start | bytes 1048576 | tf_op jit(solution)/shard_map/all_to_all | solution.py:687
  188.7 4.7 %collective-permute-done.29.refs_8_ = bf16[64,1024]{1,0:T(8,128)(2,1)S(1)} collective-permute-done((bf16[64,1024]{1,0:T(8,128)(2,1)S(1)}, bf16[64,1024]{1,0:T(8,128)(2,1)S(1)}, u32[]{:S(2)}, u32[]{:S(2)}) %collective-permute-start.29) | collective-permute-done | bytes 131104 | tf_op jit(solution)/shard_map/ppermute | solution.py:52
  202.3 4.1 %collective-permute-start.34 = (bf16[256,1024]{1,0:T(8,128)(2,1)}, bf16[256,1024]{1,0:T(8,128)(2,1)S(1)}, u32[]{:S(2)}, u32[]{:S(2)}) collective-permute-start(bf16[256,1024]{1,0:T(8,128)(2,1)} %dynamic-slice_bitcast_fusion.1), channel_id=1, source_target_pairs={{0,8},{8,0},{16,24},{24,16},{32,40},{40,32},{48,56},{56,48},{64,72... | collective-permute-start | bytes 1572872 | tf_op jit(solution)/shard_map/ppermute | solution.py:681
  206.5 5.6 %all-to-all-start.4 = ((bf16[8,128,1024]{2,1,0:T(8,128)(2,1)}), bf16[8,128,1024]{2,1,0:T(8,128)(2,1)S(1)}, u32[]{:S(2)}, u32[]{:S(2)}) async-start(bf16[8,128,1024]{2,1,0:T(8,128)(2,1)} %bitcast.114), calls=%async_computation.4 | async-start | bytes 4194304 | tf_op jit(solution)/shard_map/all_to_all | solution.py:83
  216.7 14.6 %shard_map.218 = (bf16[1024,896]{1,0:T(8,128)(2,1)}, f32[8,8]{1,0:T(8,128)S(1)}) custom-call(f32[1024,896]{1,0:T(8,128)} %get-tuple-element.119.proj, f32[8,8]{1,0:T(8,128)S(1)} %fusion.19.refs_1_.small_ref, f32[1024,192]{1,0:T(8,128)S(1)} %copy-done.32, f32[4,192,128]{2,1,0:T(8,128)S(1)} %copy-done.35, f32[1024,8]{1,0:T(8,128)S(1)} %copy-done.33, ...), custom_call_target="tpu_custom_call" | custom-call | flops 19000000512 | bytes 1048576 | tf_op jit(solution)/shard_map/pallas_call | solution.py:441
  231.4 4.1 %convolution_convert_fusion.2 = bf16[1024,896]{1,0:T(8,128)(2,1)S(1)} fusion(bf16[1024,1024]{1,0:T(8,128)(2,1)S(1)} %copy-done.49, bf16[1024,896]{1,0:T(8,128)(2,1)} %get-tuple-element.138), kind=kOutput, calls=%fused_computation.5 | convolution fusion | flops 1879965696 | bytes 5767168 | tf_op jit(solution)/shard_map/dot_general | solution.py:35
  238.9 4.7 %collective-permute-done.37 = bf16[64,1024]{1,0:T(8,128)(2,1)S(1)} collective-permute-done((bf16[64,1024]{1,0:T(8,128)(2,1)S(1)}, bf16[64,1024]{1,0:T(8,128)(2,1)S(1)}, u32[]{:S(2)}, u32[]{:S(2)}) %collective-permute-start.37) | collective-permute-done | bytes 131104 | tf_op jit(solution)/shard_map/ppermute | solution.py:681
  247.2 9.0 %all-to-all-start.5 = ((bf16[64,8,896]{2,1,0:T(8,128)(2,1)}), bf16[64,8,896]{2,1,0:T(8,128)(2,1)S(1)}, u32[]{:S(2)}, u32[]{:S(2)}) async-start(bf16[64,8,896]{2,1,0:T(8,128)(2,1)} %bitcast.117), calls=%async_computation.5 | async-start | bytes 1835008 | tf_op jit(solution)/shard_map/all_to_all | solution.py:687
  256.2 5.8 %convolution_convert_fusion = bf16[1024,1024]{1,0:T(8,128)(2,1)} fusion(bf16[1024,896]{1,0:T(8,128)(2,1)} %get-tuple-element.138, bf16[1024,896]{1,0:T(8,128)(2,1)} %get-tuple-element.139), kind=kOutput, calls=%fused_computation | convolution fusion | flops 1880096768 | bytes 5767168 | tf_op jit(solution)/shard_map/dot_general | solution.py:35
  265.6 4.2 %collective-permute-done.38 = bf16[32,1024]{1,0:T(8,128)(2,1)S(1)} collective-permute-done((bf16[32,1024]{1,0:T(8,128)(2,1)S(1)}, bf16[32,1024]{1,0:T(8,128)(2,1)S(1)}, u32[]{:S(2)}, u32[]{:S(2)}) %collective-permute-start.38) | collective-permute-done | bytes 65568 | tf_op jit(solution)/shard_map/ppermute | solution.py:681
  273.7 5.2 %collective-permute-done.39 = bf16[8,12416]{1,0:T(8,128)(2,1)S(1)} collective-permute-done((bf16[8,12416]{1,0:T(8,128)(2,1)S(1)}, bf16[8,12416]{1,0:T(8,128)(2,1)S(1)}, u32[]{:S(2)}, u32[]{:S(2)}) %collective-permute-start.39) | collective-permute-done | bytes 198688 | tf_op jit(solution)/shard_map/ppermute | solution.py:747
  278.9 6.3 %all-to-all-start.6 = ((bf16[8,128,1024]{2,1,0:T(8,128)(2,1)}), bf16[8,128,1024]{2,1,0:T(8,128)(2,1)S(1)}, u32[]{:S(2)}, u32[]{:S(2)}) async-start(bf16[8,128,1024]{2,1,0:T(8,128)(2,1)} %bitcast.118), calls=%async_computation.6 | async-start | bytes 4194304 | tf_op jit(solution)/shard_map/all_to_all | solution.py:83
  289.9 4.6 %collective-permute-done.40.refs_1_ = bf16[16,12416]{1,0:T(8,128)(2,1)S(1)} collective-permute-done((bf16[16,12416]{1,0:T(8,128)(2,1)S(1)}, bf16[16,12416]{1,0:T(8,128)(2,1)S(1)}, u32[]{:S(2)}, u32[]{:S(2)}) %collective-permute-start.40) | collective-permute-done | bytes 397344 | tf_op jit(solution)/shard_map/ppermute | solution.py:88
  294.5 4.5 %collective-permute-start.44 = (bf16[16,12416]{1,0:T(8,128)(2,1)S(1)}, bf16[16,12416]{1,0:T(8,128)(2,1)S(1)}, u32[]{:S(2)}, u32[]{:S(2)}) collective-permute-start(bf16[16,12416]{1,0:T(8,128)(2,1)S(1)} %collective-permute-done.40.refs_1_), channel_id=1, source_target_pairs={{0,8},{8,0},{16,24},{24,16},{32,40},{40,32},{48,56},{56,48},{64,72... | collective-permute-start | bytes 1191944 | tf_op jit(solution)/shard_map/ppermute | solution.py:96
  299.0 3.0 collective-permute-start.45
  302.0 5.6 %collective-permute-done.42.refs_3_ = bf16[16,12416]{1,0:T(8,128)(2,1)S(1)} collective-permute-done((bf16[16,12416]{1,0:T(8,128)(2,1)S(1)}, bf16[16,12416]{1,0:T(8,128)(2,1)S(1)}, u32[]{:S(2)}, u32[]{:S(2)}) %collective-permute-start.42) | collective-permute-done | bytes 397344 | tf_op jit(solution)/shard_map/ppermute | solution.py:88
  311.6 4.7 %shard_map.222 = (f32[3352,128]{1,0:T(8,128)}, f32[128,768]{1,0:T(8,128)}, f32[128,4096]{1,0:T(8,128)}, f32[256,1024]{1,0:T(8,128)}, f32[192,1024]{1,0:T(8,128)}...) custom-call(s32[4]{0:T(128)S(1)} %pad_add_fusion.where.refs_0_, bf16[128,3352]{1,0:T(8,128)(2,1)S(1)} %bitcast.102, ...), custom_call_target="tpu_custom_call" | custom-call | flops 6000000000 | bytes 1048576 | tf_op jit(solution)/shard_map/pallas_call | solution.py:601
  (228 shorter events, 105.4 us)
Async XLA Ops:
  1.8 14.3 %collective-permute-start = (bf16[128,2048]{1,0:T(8,128)(2,1)S(1)}, bf16[128,2048]{1,0:T(8,128)(2,1)}, u32[]{:S(2)}, u32[]{:S(2)}) collective-permute-start(bf16[128,2048]{1,0:T(8,128)(2,1)S(1)} %pad_maximum_fusion.2.refs_11_.refs_2_), channel_id=1, source_target_pairs={{0,1},{1,0},{2,3},{3,2},{4,5},{5,4},{6,7},{7,6},{8,9},{9,8},{10,11... | collective-permute-start | bytes 1572872 | tf_op jit(solution)/shard_map/ppermute | solution.py:62
  4.3 25.8 %collective-permute-start.1 = (bf16[128,2048]{1,0:T(8,128)(2,1)S(1)}, bf16[128,2048]{1,0:T(8,128)(2,1)S(1)}, u32[]{:S(2)}, u32[]{:S(2)}) collective-permute-start(bf16[128,2048]{1,0:T(8,128)(2,1)S(1)} %pad_maximum_fusion.2.refs_11_.refs_2_), channel_id=1, source_target_pairs={{0,2},{1,3},{2,4},{3,5},{4,6},{5,7},{6,0},{7,1},{8,10},{9,11},{10,... | collective-permute-start | bytes 1572872 | tf_op jit(solution)/shard_map/ppermute | solution.py:62
  5.5 24.9 %collective-permute-start.3 = (bf16[128,2048]{1,0:T(8,128)(2,1)S(1)}, bf16[128,2048]{1,0:T(8,128)(2,1)}, u32[]{:S(2)}, u32[]{:S(2)}) collective-permute-start(bf16[128,2048]{1,0:T(8,128)(2,1)S(1)} %pad_maximum_fusion.2.refs_11_.refs_2_), channel_id=1, source_target_pairs={{0,6},{1,7},{2,0},{3,1},{4,2},{5,3},{6,4},{7,5},{8,14},{9,15},{10,... | collective-permute-start | bytes 1572872 | tf_op jit(solution)/shard_map/ppermute | solution.py:62
  27.4 10.3 %collective-permute-start.5 = (bf16[8,16,1408]{2,1,0:T(8,128)(2,1)S(1)}, bf16[8,16,1408]{2,1,0:T(8,128)(2,1)S(1)}, u32[]{:S(2)}, u32[]{:S(2)}) collective-permute-start(bf16[8,16,1408]{2,1,0:T(8,128)(2,1)S(1)} %all_to_all.35.refs_3_), channel_id=1, source_target_pairs={{0,96},{8,104},{16,112},{24,120},{32,0},{40,8},{48,16},{56,24},{64... | collective-permute-start | bytes 1081352 | tf_op jit(solution)/shard_map/ppermute | solution.py:88
  33.9 15.4 %collective-permute-start.12 = (bf16[128,2048]{1,0:T(8,128)(2,1)}, bf16[128,2048]{1,0:T(8,128)(2,1)S(1)}, u32[]{:S(2)}, u32[]{:S(2)}) collective-permute-start(bf16[128,2048]{1,0:T(8,128)(2,1)} %collective-permute-done.refs_12_.refs_3_), channel_id=1, source_target_pairs={{0,2},{1,3},{2,4},{3,5},{4,6},{5,7},{6,0},{7,1},{8,10},{9,11},{10,... | collective-permute-start | bytes 1572872 | tf_op jit(solution)/shard_map/ppermute | solution.py:62
  33.9 18.3 %collective-permute-start.13 = (bf16[128,2048]{1,0:T(8,128)(2,1)}, bf16[128,2048]{1,0:T(8,128)(2,1)S(1)}, u32[]{:S(2)}, u32[]{:S(2)}) collective-permute-start(bf16[128,2048]{1,0:T(8,128)(2,1)} %collective-permute-done.refs_12_.refs_3_), channel_id=1, source_target_pairs={{0,6},{1,7},{2,0},{3,1},{4,2},{5,3},{6,4},{7,5},{8,14},{9,15},{10,... | collective-permute-start | bytes 1572872 | tf_op jit(solution)/shard_map/ppermute | solution.py:62
  36.6 15.7 %collective-permute-start.6 = (bf16[8,16,1408]{2,1,0:T(8,128)(2,1)S(1)}, bf16[8,16,1408]{2,1,0:T(8,128)(2,1)S(1)}, u32[]{:S(2)}, u32[]{:S(2)}) collective-permute-start(bf16[8,16,1408]{2,1,0:T(8,128)(2,1)S(1)} %all_to_all.35.refs_3_), channel_id=1, source_target_pairs={{0,64},{8,72},{16,80},{24,88},{32,96},{40,104},{48,112},{56,120},{... | collective-permute-start | bytes 1081352 | tf_op jit(solution)/shard_map/ppermute | solution.py:88
  37.2 15.7 %collective-permute-start.7 = (bf16[8,16,1408]{2,1,0:T(8,128)(2,1)S(1)}, bf16[8,16,1408]{2,1,0:T(8,128)(2,1)S(1)}, u32[]{:S(2)}, u32[]{:S(2)}) collective-permute-start(bf16[8,16,1408]{2,1,0:T(8,128)(2,1)S(1)} %all_to_all.35.refs_3_), channel_id=1, source_target_pairs={{0,32},{8,40},{16,48},{24,56},{32,64},{40,72},{48,80},{56,88},{64,... | collective-permute-start | bytes 1081352 | tf_op jit(solution)/shard_map/ppermute | solution.py:88
  37.7 20.4 %collective-permute-start.14 = (bf16[128,2048]{1,0:T(8,128)(2,1)S(1)}, bf16[128,2048]{1,0:T(8,128)(2,1)S(1)}, u32[]{:S(2)}, u32[]{:S(2)}) collective-permute-start(bf16[128,2048]{1,0:T(8,128)(2,1)S(1)} %pad_maximum_fusion.3), channel_id=1, source_target_pairs={{0,1},{1,0},{2,3},{3,2},{4,5},{5,4},{6,7},{7,6},{8,9},{9,8},{10,11... | collective-permute-start | bytes 1572872 | tf_op jit(solution)/shard_map/ppermute | solution.py:62
  75.5 34.9 %all-to-all-start.1 = ((bf16[8,128,1024]{2,1,0:T(8,128)(2,1)}), bf16[8,128,1024]{2,1,0:T(8,128)(2,1)S(1)}, u32[]{:S(2)}, u32[]{:S(2)}) async-start(bf16[8,128,1024]{2,1,0:T(8,128)(2,1)} %bitcast.120), calls=%async_computation.1 | async-start | bytes 4194304 | tf_op jit(solution)/shard_map/all_to_all | solution.py:83
  111.6 9.8 %collective-permute-start.17 = (bf16[128,1024]{1,0:T(8,128)(2,1)S(1)}, bf16[128,1024]{1,0:T(8,128)(2,1)S(1)}, u32[]{:S(2)}, u32[]{:S(2)}) collective-permute-start(bf16[128,1024]{1,0:T(8,128)(2,1)S(1)} %get-tuple-element.95.refs_3_), channel_id=1, source_target_pairs={{0,6},{1,7},{2,0},{3,1},{4,2},{5,3},{6,4},{7,5},{8,14},{9,15},{10,... | collective-permute-start | bytes 786440 | tf_op jit(solution)/shard_map/ppermute | solution.py:52
  118.7 9.7 %collective-permute-start.20 = (bf16[128,1024]{1,0:T(8,128)(2,1)S(1)}, bf16[128,1024]{1,0:T(8,128)(2,1)S(1)}, u32[]{:S(2)}, u32[]{:S(2)}) collective-permute-start(bf16[128,1024]{1,0:T(8,128)(2,1)S(1)} %collective-permute-done.15.refs_4_), channel_id=1, source_target_pairs={{0,2},{1,3},{2,4},{3,5},{4,6},{5,7},{6,0},{7,1},{8,10},{9,11},{10,... | collective-permute-start | bytes 786440 | tf_op jit(solution)/shard_map/ppermute | solution.py:52
  118.8 9.6 %collective-permute-start.21 = (bf16[128,1024]{1,0:T(8,128)(2,1)S(1)}, bf16[128,1024]{1,0:T(8,128)(2,1)S(1)}, u32[]{:S(2)}, u32[]{:S(2)}) collective-permute-start(bf16[128,1024]{1,0:T(8,128)(2,1)S(1)} %collective-permute-done.15.refs_4_), channel_id=1, source_target_pairs={{0,6},{1,7},{2,0},{3,1},{4,2},{5,3},{6,4},{7,5},{8,14},{9,15},{10,... | collective-permute-start | bytes 786440 | tf_op jit(solution)/shard_map/ppermute | solution.py:52
  136.9 31.3 %all-to-all-start.2 = ((bf16[8,128,1024]{2,1,0:T(8,128)(2,1)}), bf16[8,128,1024]{2,1,0:T(8,128)(2,1)S(1)}, u32[]{:S(2)}, u32[]{:S(2)}) async-start(bf16[8,128,1024]{2,1,0:T(8,128)(2,1)} %bitcast.119), calls=%async_computation.2 | async-start | bytes 4194304 | tf_op jit(solution)/shard_map/all_to_all | solution.py:83
  171.2 9.0 %collective-permute-start.26 = (bf16[128,1024]{1,0:T(8,128)(2,1)}, bf16[128,1024]{1,0:T(8,128)(2,1)S(1)}, u32[]{:S(2)}, u32[]{:S(2)}) collective-permute-start(bf16[128,1024]{1,0:T(8,128)(2,1)} %get-tuple-element.105.refs_3_), channel_id=1, source_target_pairs={{0,2},{1,3},{2,4},{3,5},{4,6},{5,7},{6,0},{7,1},{8,10},{9,11},{10,... | collective-permute-start | bytes 786440 | tf_op jit(solution)/shard_map/ppermute | solution.py:52
  171.2 10.1 %collective-permute-start.25 = (bf16[128,1024]{1,0:T(8,128)(2,1)}, bf16[128,1024]{1,0:T(8,128)(2,1)S(1)}, u32[]{:S(2)}, u32[]{:S(2)}) collective-permute-start(bf16[128,1024]{1,0:T(8,128)(2,1)} %get-tuple-element.105.refs_3_), channel_id=1, source_target_pairs={{0,1},{1,0},{2,3},{3,2},{4,5},{5,4},{6,7},{7,6},{8,9},{9,8},{10,11... | collective-permute-start | bytes 786440 | tf_op jit(solution)/shard_map/ppermute | solution.py:52
  171.2 12.7 %collective-permute-start.27 = (bf16[128,1024]{1,0:T(8,128)(2,1)}, bf16[128,1024]{1,0:T(8,128)(2,1)S(1)}, u32[]{:S(2)}, u32[]{:S(2)}) collective-permute-start(bf16[128,1024]{1,0:T(8,128)(2,1)} %get-tuple-element.105.refs_3_), channel_id=1, source_target_pairs={{0,6},{1,7},{2,0},{3,1},{4,2},{5,3},{6,4},{7,5},{8,14},{9,15},{10,... | collective-permute-start | bytes 786440 | tf_op jit(solution)/shard_map/ppermute | solution.py:52
  173.9 21.2 %all-to-all-start.3 = ((bf16[64,8,512]{2,1,0:T(8,128)(2,1)}), bf16[64,8,512]{2,1,0:T(8,128)(2,1)S(1)}, u32[]{:S(2)}, u32[]{:S(2)}) async-start(bf16[64,8,512]{2,1,0:T(8,128)(2,1)} %bitcast.121), calls=%async_computation.3 | async-start | bytes 1048576 | tf_op jit(solution)/shard_map/all_to_all | solution.py:687
  181.3 13.9 %collective-permute-start.30 = (bf16[128,1024]{1,0:T(8,128)(2,1)S(1)}, bf16[128,1024]{1,0:T(8,128)(2,1)S(1)}, u32[]{:S(2)}, u32[]{:S(2)}) collective-permute-start(bf16[128,1024]{1,0:T(8,128)(2,1)S(1)} %collective-permute-done.25.refs_4_), channel_id=1, source_target_pairs={{0,2},{1,3},{2,4},{3,5},{4,6},{5,7},{6,0},{7,1},{8,10},{9,11},{10,... | collective-permute-start | bytes 786440 | tf_op jit(solution)/shard_map/ppermute | solution.py:52
  182.5 12.7 %collective-permute-start.31 = (bf16[128,1024]{1,0:T(8,128)(2,1)S(1)}, bf16[128,1024]{1,0:T(8,128)(2,1)S(1)}, u32[]{:S(2)}, u32[]{:S(2)}) collective-permute-start(bf16[128,1024]{1,0:T(8,128)(2,1)S(1)} %collective-permute-done.25.refs_4_), channel_id=1, source_target_pairs={{0,6},{1,7},{2,0},{3,1},{4,2},{5,3},{6,4},{7,5},{8,14},{9,15},{10,... | collective-permute-start | bytes 786440 | tf_op jit(solution)/shard_map/ppermute | solution.py:52
  184.0 9.4 %collective-permute-start.29 = (bf16[64,1024]{1,0:T(8,128)(2,1)S(1)}, bf16[64,1024]{1,0:T(8,128)(2,1)S(1)}, u32[]{:S(2)}, u32[]{:S(2)}) collective-permute-start(bf16[64,1024]{1,0:T(8,128)(2,1)S(1)} %slice.57), channel_id=1, source_target_pairs={{0,6},{1,7},{2,0},{3,1},{4,2},{5,3},{6,4},{7,5},{8,14},{9,15},{10,... | collective-permute-start | bytes 393224 | tf_op jit(solution)/shard_map/ppermute | solution.py:52
  202.3 9.8 %collective-permute-start.34 = (bf16[256,1024]{1,0:T(8,128)(2,1)}, bf16[256,1024]{1,0:T(8,128)(2,1)S(1)}, u32[]{:S(2)}, u32[]{:S(2)}) collective-permute-start(bf16[256,1024]{1,0:T(8,128)(2,1)} %dynamic-slice_bitcast_fusion.1), channel_id=1, source_target_pairs={{0,8},{8,0},{16,24},{24,16},{32,40},{40,32},{48,56},{56,48},{64,72... | collective-permute-start | bytes 1572872 | tf_op jit(solution)/shard_map/ppermute | solution.py:681
  206.5 40.7 %all-to-all-start.4 = ((bf16[8,128,1024]{2,1,0:T(8,128)(2,1)}), bf16[8,128,1024]{2,1,0:T(8,128)(2,1)S(1)}, u32[]{:S(2)}, u32[]{:S(2)}) async-start(bf16[8,128,1024]{2,1,0:T(8,128)(2,1)} %bitcast.114), calls=%async_computation.4 | async-start | bytes 4194304 | tf_op jit(solution)/shard_map/all_to_all | solution.py:83
  213.5 17.8 %collective-permute-start.35 = (bf16[128,1024]{1,0:T(8,128)(2,1)S(1)}, bf16[128,1024]{1,0:T(8,128)(2,1)S(1)}, u32[]{:S(2)}, u32[]{:S(2)}) collective-permute-start(bf16[128,1024]{1,0:T(8,128)(2,1)S(1)} %dynamic-slice_bitcast_fusion.3), channel_id=1, source_target_pairs={{0,64},{8,72},{16,80},{24,88},{32,96},{40,104},{48,112},{56,120},{... | collective-permute-start | bytes 786440 | tf_op jit(solution)/shard_map/ppermute | solution.py:681
  247.2 25.2 %all-to-all-start.5 = ((bf16[64,8,896]{2,1,0:T(8,128)(2,1)}), bf16[64,8,896]{2,1,0:T(8,128)(2,1)S(1)}, u32[]{:S(2)}, u32[]{:S(2)}) async-start(bf16[64,8,896]{2,1,0:T(8,128)(2,1)} %bitcast.117), calls=%async_computation.5 | async-start | bytes 1835008 | tf_op jit(solution)/shard_map/all_to_all | solution.py:687
  278.9 38.6 %all-to-all-start.6 = ((bf16[8,128,1024]{2,1,0:T(8,128)(2,1)}), bf16[8,128,1024]{2,1,0:T(8,128)(2,1)S(1)}, u32[]{:S(2)}, u32[]{:S(2)}) async-start(bf16[8,128,1024]{2,1,0:T(8,128)(2,1)} %bitcast.118), calls=%async_computation.6 | async-start | bytes 4194304 | tf_op jit(solution)/shard_map/all_to_all | solution.py:83
  285.2 9.3 %collective-permute-start.40 = (bf16[16,12416]{1,0:T(8,128)(2,1)S(1)}, bf16[16,12416]{1,0:T(8,128)(2,1)S(1)}, u32[]{:S(2)}, u32[]{:S(2)}) collective-permute-start(bf16[16,12416]{1,0:T(8,128)(2,1)S(1)} %pad_maximum_fusion.4.refs_0_), channel_id=1, source_target_pairs={{0,96},{8,104},{16,112},{24,120},{32,0},{40,8},{48,16},{56,24},{64... | collective-permute-start | bytes 1191944 | tf_op jit(solution)/shard_map/ppermute | solution.py:88
  286.4 12.5 %collective-permute-start.41 = (bf16[16,12416]{1,0:T(8,128)(2,1)S(1)}, bf16[16,12416]{1,0:T(8,128)(2,1)S(1)}, u32[]{:S(2)}, u32[]{:S(2)}) collective-permute-start(bf16[16,12416]{1,0:T(8,128)(2,1)S(1)} %pad_maximum_fusion.4.refs_0_), channel_id=1, source_target_pairs={{0,64},{8,72},{16,80},{24,88},{32,96},{40,104},{48,112},{56,120},{... | collective-permute-start | bytes 1191944 | tf_op jit(solution)/shard_map/ppermute | solution.py:88
  287.5 20.1 %collective-permute-start.42 = (bf16[16,12416]{1,0:T(8,128)(2,1)S(1)}, bf16[16,12416]{1,0:T(8,128)(2,1)S(1)}, u32[]{:S(2)}, u32[]{:S(2)}) collective-permute-start(bf16[16,12416]{1,0:T(8,128)(2,1)S(1)} %pad_maximum_fusion.4.refs_0_), channel_id=1, source_target_pairs={{0,32},{8,40},{16,48},{24,56},{32,64},{40,72},{48,80},{56,88},{64,... | collective-permute-start | bytes 1191944 | tf_op jit(solution)/shard_map/ppermute | solution.py:88
  287.5 20.6 %collective-permute-start.43 = (bf16[16,12416]{1,0:T(8,128)(2,1)S(1)}, bf16[16,12416]{1,0:T(8,128)(2,1)S(1)}, u32[]{:S(2)}, u32[]{:S(2)}) collective-permute-start(bf16[16,12416]{1,0:T(8,128)(2,1)S(1)} %pad_maximum_fusion.4.refs_0_), channel_id=1, source_target_pairs={{0,8},{8,0},{16,24},{24,16},{32,40},{40,32},{48,56},{56,48},{64,72... | collective-permute-start | bytes 1191944 | tf_op jit(solution)/shard_map/ppermute | solution.py:96
  294.5 13.6 %collective-permute-start.44 = (bf16[16,12416]{1,0:T(8,128)(2,1)S(1)}, bf16[16,12416]{1,0:T(8,128)(2,1)S(1)}, u32[]{:S(2)}, u32[]{:S(2)}) collective-permute-start(bf16[16,12416]{1,0:T(8,128)(2,1)S(1)} %collective-permute-done.40.refs_1_), channel_id=1, source_target_pairs={{0,8},{8,0},{16,24},{24,16},{32,40},{40,32},{48,56},{56,48},{64,72... | collective-permute-start | bytes 1191944 | tf_op jit(solution)/shard_map/ppermute | solution.py:96
  299.0 9.1 %collective-permute-start.45 = (bf16[16,12416]{1,0:T(8,128)(2,1)S(1)}, bf16[16,12416]{1,0:T(8,128)(2,1)S(1)}, u32[]{:S(2)}, u32[]{:S(2)}) collective-permute-start(bf16[16,12416]{1,0:T(8,128)(2,1)S(1)} %collective-permute-done.41.refs_2_), channel_id=1, source_target_pairs={{0,8},{8,0},{16,24},{24,16},{32,40},{40,32},{48,56},{56,48},{64,72... | collective-permute-start | bytes 1191944 | tf_op jit(solution)/shard_map/ppermute | solution.py:96
  (71 other events, 807.8 us)

commit v4 on v3

--- a/solution.py
+++ b/solution.py
@@ -155,7 +155,7 @@
 def mixer_forward_kernel(*refs):
     (
         where, small_ref, out_w, *pieces,
-        unit, in_w, gu_w, proj, mix, y_out, states, log_totals, mid_part, keys, values,
+        unit, in_w, gu_w, proj_out, steps_out, mix, y_out, states, log_totals, mid_part, keys, values, part,
     ) = refs
     me, core, y = where[0], where[1], where[2]
     shares, pieces = pieces[:8], pieces[8:]
@@ -173,12 +173,14 @@
     state = jnp.zeros((HW, NS), F32)
     for c in range(NCH):
         rows = slice(c * CH, (c + 1) * CH)
-        proj[rows, :] = dot(unit[rows, :], in_w[...])
-        b = proj[rows, CB : CB + NS].astype(BF)
-        cc = proj[rows, CC : CC + NS].astype(BF)
-        z = proj[rows, CZ : CZ + HW]
-        u = proj[rows, CU : CU + HW]
-        _, dt, log_decay = steps(proj[rows, CR : CR + 8], small)
+        part[...] = dot(unit[rows, :], in_w[...])
+        proj_out[rows, :] = part[...].astype(BF)
+        steps_out[rows, :] = part[:, CR : CR + 8]
+        b = part[:, CB : CB + NS].astype(BF)
+        cc = part[:, CC : CC + NS].astype(BF)
+        z = part[:, CZ : CZ + HW]
+        u = part[:, CU : CU + HW]
+        _, dt, log_decay = steps(part[:, CR : CR + 8], small)
         cum, decays = block_decays(log_decay)
         g = dot(cc, b, ((1,), (1,)))
         v = u * widen(dt)
@@ -196,9 +198,9 @@
         y_out[rows, :] = y
         mix[rows, 0:HW] = (y * z * jax.nn.sigmoid(z)).astype(BF)
 
-        q = proj[rows, CQ : CQ + HS].astype(BF)
-        keys[rows, :] = proj[rows, CK : CK + HS].astype(BF)
-        values[rows, :] = proj[rows, CV : CV + HS].astype(BF)
+        q = part[:, CQ : CQ + HS].astype(BF)
+        keys[rows, :] = part[:, CK : CK + HS].astype(BF)
+        values[rows, :] = part[:, CV : CV + HS].astype(BF)
         seen = (c + 1) * CH
         scores = causal(c, dot(q, keys[0:seen, :], ((1,), (1,))) * HS**-0.5)
         peak = jnp.max(scores, axis=1, keepdims=True)
@@ -211,7 +213,7 @@
 
 
 def mixer_backward_kernel(
-    proj, small_ref, y_in, states, log_totals, mix_grad, out, sums, keys, values, key_grad, value_grad
+    proj, steps_in, small_ref, y_in, states, log_totals, mix_grad, out, sums, keys, values, key_grad, value_grad
 ):
     small = small_ref[...]
     skip_w = widen(jnp.broadcast_to(small[2:3, :], (CH, 8)))
@@ -251,9 +253,9 @@
 
         b = proj[rows, CB : CB + NS].astype(BF)
         cc = proj[rows, CC : CC + NS].astype(BF)
-        z = proj[rows, CZ : CZ + HW]
-        u = proj[rows, CU : CU + HW]
-        pre, dt, log_decay = steps(proj[rows, CR : CR + 8], small)
+        z = proj[rows, CZ : CZ + HW].astype(F32)
+        u = proj[rows, CU : CU + HW].astype(F32)
+        pre, dt, log_decay = steps(steps_in[rows, :], small)
         cum, decays = block_decays(log_decay)
         last = cum[CH - 1 : CH, :]
         g = dot(cc, b, ((1,), (1,)))
@@ -348,7 +350,8 @@
             shape((TOK, D), BF),
             shape((D, CW), BF),
             shape((D, 2 * FL), BF),
-            shape((TOK, CW), F32),
+            shape((TOK, CW), BF),
+            shape((TOK, 8), F32),
             shape((TOK, HW + HS), BF),
             shape((TOK, HW), F32),
             shape((NCH, HW, NS), F32),
@@ -356,8 +359,8 @@
             shape((TOK, D), BF),
         ),
         in_specs=[SMEM] + [VMEM] * 19,
-        out_specs=(VMEM,) * 9,
-        scratch_shapes=[pltpu.VMEM((TOK, HS), BF), pltpu.VMEM((TOK, HS), BF)],
+        out_specs=(VMEM,) * 10,
+        scratch_shapes=[pltpu.VMEM((TOK, HS), BF), pltpu.VMEM((TOK, HS), BF), pltpu.VMEM((CH, CW), F32)],
         cost_estimate=cost(16),
         compiler_params=params(50),
     )(where, small, out_w, *shares, *pieces)
@@ -437,11 +440,11 @@
     )(where, out_w, mix, *pieces)
 
 
-def mixer_backward(proj, small, y, states, log_totals, mix_grad):
+def mixer_backward(proj, step_rows, small, y, states, log_totals, mix_grad):
     return pl.pallas_call(
         mixer_backward_kernel,
         out_shape=(jax.ShapeDtypeStruct((TOK, CW), BF), jax.ShapeDtypeStruct((8, 8), F32)),
-        in_specs=[VMEM] * 6,
+        in_specs=[VMEM] * 7,
         out_specs=(VMEM,) * 2,
         scratch_shapes=[
             pltpu.VMEM((TOK, HS), BF),
@@ -451,7 +454,7 @@
         ],
         cost_estimate=cost(19),
         compiler_params=params(50),
-    )(proj, small, y, states, log_totals, mix_grad)
+    )(proj, step_rows, small, y, states, log_totals, mix_grad)
 
 
 def pack_weights_kernel(where, mixer_w, attn_w, gate_up, gains, out):
@@ -544,7 +547,7 @@
         out_specs=VMEM,
         scratch_shapes=[pltpu.VMEM((8, WALL), F32)],
         cost_estimate=cost(1),
-        compiler_params=params(50),
+        compiler_params=params(16),
     )(got, got_gu, thin)
 
 
@@ -660,19 +663,36 @@
     )(*arrays)
 
 
-def core_sum(grad, core, line=None):
+def core_sum(grad, core):
     n = grad.shape[1]
     parts = grad.reshape(SEQ, 2, ROWS // 2, n)
     mine = lax.dynamic_index_in_dim(parts, core, 1, False).astype(F32)
     other = core_swap(lax.dynamic_index_in_dim(parts, 1 - core, 1, False))
     both = mine + other.astype(F32)
-    if line is not None:
-        me = lax.axis_index("seq")
-        here = (lax.broadcasted_iota(jnp.int32, both.shape, 0) == me) & (
-            lax.broadcasted_iota(jnp.int32, both.shape, 1) == 0
-        )
-        both = both + jnp.where(here, line[None, None], 0.0)
     return both.astype(BF).reshape(SEQ, 8, 8, n).swapaxes(0, 1).reshape(64, 8, n)
+
+
+def core_sum_kernel(where, mine, other, line, out):
+    first = lax.broadcasted_iota(jnp.int32, (ROWS // 2, CW), 0) == 0
+    for j in range(SEQ):
+        value = mine[j].astype(F32) + other[j].astype(F32)
+        value = value + jnp.where(first & (where[0] == j), line[0:1, :], 0.0)
+        for chip in range(8):
+            out[chip * SEQ + j] = value[chip * 8 : (chip + 1) * 8, :].astype(BF)
+
+
+def core_sum_with(where, in_grad, line, core):
+    parts = in_grad.reshape(SEQ, 2, ROWS // 2, CW)
+    other = core_swap(lax.dynamic_index_in_dim(parts, 1 - core, 1, False))
+    mine = lax.dynamic_index_in_dim(parts, core, 1, False)
+    return pl.pallas_call(
+        core_sum_kernel,
+        out_shape=jax.ShapeDtypeStruct((64, 8, CW), BF),
+        in_specs=[SMEM] + [VMEM] * 3,
+        out_specs=VMEM,
+        cost_estimate=cost(1),
+        compiler_params=params(16),
+    )(where, mine, other, line)
 
 
 def halved(v, mine, bit):
@@ -707,7 +727,7 @@
 
     packed = pack_weights(where, mixer_in[0], attn_in[0], gate_up[0], gains)
     pieces, shares = gather_with_weights(jnp.concatenate([x0, cotangent[0]], axis=1), packed)
-    unit_one, in_w, gu_w, proj, mix, y, states, log_totals, mid_part = mixer_forward(
+    unit_one, in_w, gu_w, proj, step_rows, mix, y, states, log_totals, mid_part = mixer_forward(
         where, small, out_w, shares, pieces
     )
     ffn_grad, act_grad = output_gradients(where, down_w, pieces)
@@ -727,20 +747,21 @@
     *pieces, gu_got = lax.optimization_barrier((*pieces, to_owners(gu_sent)))
 
     mix_grad, out_grad = branch_products(where, out_w, mix, pieces)
-    thin = halved(jnp.concatenate([down_grad, out_grad], axis=0), core, 1)
+    kept = core_swap(jnp.where(core == 0, out_grad, down_grad))
     mix_grad, out_part = lax.optimization_barrier((mix_grad, out_part))
-    mix_grad, thin = lax.optimization_barrier((mix_grad, thin))
-    proj_grad, sums = mixer_backward(proj, small, y, states, log_totals, mix_grad)
+    thin = jnp.where(core == 0, down_grad, out_grad).astype(F32) + kept.astype(F32)
+    mix_grad, thin = lax.optimization_barrier((mix_grad, thin.astype(BF)))
+    proj_grad, sums = mixer_backward(proj, step_rows, small, y, states, log_totals, mix_grad)
     proj_grad, thin = lax.optimization_barrier((proj_grad, halved(thin, group // 8, 8)))
     in_grad = dot(unit_one, proj_grad, ((0,), (0,))).astype(BF)
-    thin = halved(thin, group // 4 % 2, 4)
     line = jnp.concatenate([sums[0, :HL], sums[1, :HL], sums[2, :HL]])
     line = jnp.pad(line, (CR + 8, CW - CR - 8 - 3 * HL))
-    result, sent = scatter_rows(out_part, (core_sum(in_grad, core, line),))
+    line = jnp.broadcast_to(line[None], (8, CW))
+    result, sent = scatter_rows(out_part, (core_sum_with(where, in_grad, line, core),))
     (outputs,) = on_rows(output_kernel, (BF,), result, mid)
     sent, proj_grad, thin = lax.optimization_barrier((sent, proj_grad, thin))
     e_part = dot(proj_grad, in_w, ((1,), (1,))).astype(BF)
-    e_part, thin = lax.optimization_barrier((e_part, thin))
+    e_part, thin = lax.optimization_barrier((e_part, halved(thin, group // 4 % 2, 4)))
     thin = halved(thin, high, 2)
     got, outputs = lax.optimization_barrier((to_owners(sent), outputs))
     rows = mixer_rows(got, gu_got, thin)

time: 326 us -> 321 us (0.985)
  starting transfers between devices: 106 us -> 114 us
  waiting for transfers between devices: 102 us -> 94 us
    ppermute x10 -> x11, starting transfers between devices: 23.3 us -> 34.3 us  [core_swap(): return lax.ppermute(v, 'dp', [(i, i ^ 1) for i in range(DP)])]
    ppermute x6, waiting for transfers between devices: 10.2 us -> 3.07 us  [y_shift(): lax.ppermute(v, 'dp', [(i, (i // 4 + k) % 4 * 4 + i % 4) for i in range(D...]
    ppermute x4 -> x3, starting transfers between devices: 9.33 us -> 5.57 us  [halved(): other = lax.ppermute(other, 'dp', [(i, i ^ bit) for i in range(DP)])]
    ppermute x4 -> x3, waiting for transfers between devices: 8.89 us -> 7.89 us  [halved(): other = lax.ppermute(other, 'dp', [(i, i ^ bit) for i in range(DP)])]
    unnamed x103 -> x105, local copies, waits for them, and re-layouts: 18.2 us -> 17.5 us
  transfers between devices with their start and end apart: 53 -> 53, of which waited for: 21 -> 21; matrix products, arithmetic and copies ran while one was open for 9% -> 8% of each run, Pallas kernels for 8% -> 8%
where the time goes in v4:
time: 321 us; the launch traced here: 315 us
  starting transfers between devices  114 us (36%)
  waiting for transfers between devices  94 us (29%)
  Pallas kernels  52.4 us (16%)
  local copies, waits for them, and re-layouts  21.2 us (7%)
  matrix products  16.6 us (5%)
  blocking collectives  11.3 us (4%)
  other arithmetic  4.71 us (1%)
    all_to_all x4, waiting for transfers between devices, scatter_rows(): lax.all_to_all(part.reshape(SEQ, ROWS, D), 'seq', split_axis=0, concat_ax...  38.8 us
    ppermute x11, starting transfers between devices, core_swap(): return lax.ppermute(v, 'dp', [(i, i ^ 1) for i in range(DP)])  34.3 us
    all_to_all x4, starting transfers between devices, scatter_rows(): lax.all_to_all(part.reshape(SEQ, ROWS, D), 'seq', split_axis=0, concat_ax...  20.7 us
    ppermute x18, waiting for transfers between devices, gather_pieces(): send = lambda v, perm: lax.ppermute(v, 'seq', perm)  19.9 us
    ppermute x18, starting transfers between devices, gather_pieces(): send = lambda v, perm: lax.ppermute(v, 'seq', perm)  19.6 us
    unnamed x105, local copies, waits for them, and re-layouts  17.5 us
    dot_general x5, matrix products, dot(): lax.dot_general(a, b, (dims, ((), ())), precision=precision, preferred_el...  16.6 us
    ppermute x8, waiting for transfers between devices, gather_with_weights(): send = lambda v, perm: lax.ppermute(v, 'seq', perm)  15.2 us
  transfers between devices with their start and end apart: 53, of which 21 were waited for; matrix products, arithmetic and copies ran while one was open for 8% of the time, Pallas kernels for 8%

profile of v4, /device:TPU:1, one launch (start us, length us, event | category | flops | bytes accessed | tf_op | source)
XLA Modules:
  0.0 315.3 jit_solution(11562023418488022307)
XLA Ops:
  12.0 4.1 %collective-permute-done.refs_12_.refs_3_ = bf16[128,2048]{1,0:T(8,128)(2,1)} collective-permute-done((bf16[128,2048]{1,0:T(8,128)(2,1)S(1)}, bf16[128,2048]{1,0:T(8,128)(2,1)}, u32[]{:S(2)}, u32[]{:S(2)}) %collective-permute-start) | collective-permute-done | bytes 524320 | tf_op jit(solution)/shard_map/ppermute | solution.py:62
  16.1 11.3 %all_to_all.35.refs_3_ = bf16[8,16,1408]{2,1,0:T(8,128)(2,1)S(1)} all-to-all(bf16[8,16,1408]{2,1,0:T(8,128)(2,1)S(1)} %shard_map.211), channel_id=1, replica_groups=mesh['dp'=16,'seq'=8] {'seq'}, dimensions={0} | all-to-all | bytes 720896 | tf_op jit(solution)/shard_map/all_to_all | solution.py:65
  38.4 10.8 %collective-permute-done.12.refs_17_.refs_8_ = bf16[128,2048]{1,0:T(8,128)(2,1)S(1)} collective-permute-done((bf16[128,2048]{1,0:T(8,128)(2,1)}, bf16[128,2048]{1,0:T(8,128)(2,1)S(1)}, u32[]{:S(2)}, u32[]{:S(2)}) %collective-permute-start.12) | collective-permute-done | bytes 524320 | tf_op jit(solution)/shard_map/ppermute | solution.py:62
  49.3 2.9 collective-permute-start.8
  53.0 3.9 %collective-permute-start.11 = (bf16[8,16,1408]{2,1,0:T(8,128)(2,1)S(1)}, bf16[8,16,1408]{2,1,0:T(8,128)(2,1)S(1)}, u32[]{:S(2)}, u32[]{:S(2)}) collective-permute-start(bf16[8,16,1408]{2,1,0:T(8,128)(2,1)S(1)} %collective-permute-done.7.refs_6_), channel_id=1, source_target_pairs={{0,8},{8,0},{16,24},{24,16},{32,40},{40,32},{48,56},{56,48},{64,72... | collective-permute-start | bytes 1081352 | tf_op jit(solution)/shard_map/ppermute | solution.py:96
  59.0 15.1 %shard_map.212 = (bf16[1024,1024]{1,0:T(8,128)(2,1)}, bf16[1024,896]{1,0:T(8,128)(2,1)}, bf16[1024,512]{1,0:T(8,128)(2,1)}, bf16[1024,896]{1,0:T(8,128)(2,1)}, f...) custom-call(s32[4]{0:T(128)S(1)} %pad_add_fusion.where.refs_0_, ...), custom_call_target="tpu_custom_call" | custom-call | flops 16000000000 | bytes 1048576 | tf_op jit(solution)/shard_map/pallas_call | solution.py:347
  74.8 3.7 %all-to-all-start.1 = ((bf16[8,128,1024]{2,1,0:T(8,128)(2,1)}), bf16[8,128,1024]{2,1,0:T(8,128)(2,1)S(1)}, u32[]{:S(2)}, u32[]{:S(2)}) async-start(bf16[8,128,1024]{2,1,0:T(8,128)(2,1)} %bitcast.109), calls=%async_computation.1 | async-start | bytes 4194304 | tf_op jit(solution)/shard_map/all_to_all | solution.py:83
  81.5 3.7 %shard_map.213 = (bf16[1024,1024]{1,0:T(8,128)(2,1)}, bf16[1024,256]{1,0:T(8,128)(2,1)S(1)}) custom-call(s32[4]{0:T(128)S(1)} %pad_add_fusion.where.refs_0_, bf16[256,1024]{1,0:T(8,128)(2,1)S(1)} %bitcast.93, bf16[128,2048]{1,0:T(8,128)(2,1)S(1)} %copy-done.6, bf16[128,2048]{1,0:T(8,128)(2,1)} %collective-permute-done.refs_12_.refs_3_, ...), custom_call_target="tpu_custom_call" | custom-call | flops 3000000000 | bytes 1048576 | tf_op jit(solution)/shard_map/pallas_call | solution.py:410
  86.0 23.7 %all-to-all-done.1.got = bf16[8,128,1024]{2,1,0:T(8,128)(2,1)S(1)} async-done(((bf16[8,128,1024]{2,1,0:T(8,128)(2,1)}), bf16[8,128,1024]{2,1,0:T(8,128)(2,1)S(1)}, u32[]{:S(2)}, u32[]{:S(2)}) %all-to-all-start.1) | async-done | bytes 2097184 | tf_op jit(solution)/shard_map/all_to_all | solution.py:83
  111.0 3.0 collective-permute-start.17
  113.9 4.0 %collective-permute-done.16.refs_5_ = bf16[128,1024]{1,0:T(8,128)(2,1)S(1)} collective-permute-done((bf16[128,1024]{1,0:T(8,128)(2,1)S(1)}, bf16[128,1024]{1,0:T(8,128)(2,1)S(1)}, u32[]{:S(2)}, u32[]{:S(2)}) %collective-permute-start.16) | collective-permute-done | bytes 262176 | tf_op jit(solution)/shard_map/ppermute | solution.py:52
  123.8 3.0 collective-permute-done.19.refs_8_
  130.6 5.6 %shard_map.215 = (bf16[1024,1024]{1,0:T(8,128)(2,1)}, bf16[1024,256]{1,0:T(8,128)(2,1)S(1)}, bf16[1024,512]{1,0:T(8,128)(2,1)}, bf16[1024,1024]{1,0:T(8,128)(2,1)}) custom-call(s32[4]{0:T(128)S(1)} %pad_add_fusion.where.refs_0_, bf16[1024,512]{1,0:T(8,128)(2,1)} %get-tuple-element.90.refs_1_, bf16[1024,256]{1,0:T(8,128)(2,1)S(1)} %copy-done.31, ...), custom_call_target="tpu_custom_call" | custom-call | flops 6000000000 | bytes 1048576 | tf_op jit(solution)/shard_map/pallas_call | solution.py:387
  136.3 5.1 %all-to-all-start.2 = ((bf16[8,128,1024]{2,1,0:T(8,128)(2,1)}), bf16[8,128,1024]{2,1,0:T(8,128)(2,1)S(1)}, u32[]{:S(2)}, u32[]{:S(2)}) async-start(bf16[8,128,1024]{2,1,0:T(8,128)(2,1)} %bitcast.108), calls=%async_computation.2 | async-start | bytes 4194304 | tf_op jit(solution)/shard_map/all_to_all | solution.py:83
  141.4 3.1 convolution_convert_fusion.3
  144.6 4.8 %collective-permute-start.24 = (bf16[8,64,512]{2,1,0:T(8,128)(2,1)S(1)}, bf16[8,64,512]{2,1,0:T(8,128)(2,1)S(1)}, u32[]{:S(2)}, u32[]{:S(2)}) collective-permute-start(bf16[8,64,512]{2,1,0:T(8,128)(2,1)S(1)} %dynamic-slice_bitcast_fusion.2), channel_id=1, source_target_pairs={{0,8},{8,0},{16,24},{24,16},{32,40},{40,32},{48,56},{56,48},{64,72... | collective-permute-start | bytes 1572872 | tf_op jit(solution)/shard_map/ppermute | solution.py:96
  154.0 13.6 %all-to-all-done.2.got = bf16[8,128,1024]{2,1,0:T(8,128)(2,1)S(1)} async-done(((bf16[8,128,1024]{2,1,0:T(8,128)(2,1)}), bf16[8,128,1024]{2,1,0:T(8,128)(2,1)S(1)}, u32[]{:S(2)}, u32[]{:S(2)}) %all-to-all-start.2) | async-done | bytes 2097184 | tf_op jit(solution)/shard_map/all_to_all | solution.py:83
  172.5 6.3 %all-to-all-start.3 = ((bf16[64,8,512]{2,1,0:T(8,128)(2,1)}), bf16[64,8,512]{2,1,0:T(8,128)(2,1)S(1)}, u32[]{:S(2)}, u32[]{:S(2)}) async-start(bf16[64,8,512]{2,1,0:T(8,128)(2,1)} %bitcast.110), calls=%async_computation.3 | async-start | bytes 1048576 | tf_op jit(solution)/shard_map/all_to_all | solution.py:707
  187.4 4.2 %collective-permute-done.29.refs_8_ = bf16[64,1024]{1,0:T(8,128)(2,1)S(1)} collective-permute-done((bf16[64,1024]{1,0:T(8,128)(2,1)S(1)}, bf16[64,1024]{1,0:T(8,128)(2,1)S(1)}, u32[]{:S(2)}, u32[]{:S(2)}) %collective-permute-start.29) | collective-permute-done | bytes 131104 | tf_op jit(solution)/shard_map/ppermute | solution.py:52
  200.2 4.6 %collective-permute-start.34 = (bf16[256,1024]{1,0:T(8,128)(2,1)}, bf16[256,1024]{1,0:T(8,128)(2,1)}, u32[]{:S(2)}, u32[]{:S(2)}) collective-permute-start(bf16[256,1024]{1,0:T(8,128)(2,1)} %broadcast_select_fusion), channel_id=1, source_target_pairs={{0,8},{8,0},{16,24},{24,16},{32,40},{40,32},{48,56},{56,48},{64,72... | collective-permute-start | bytes 1572872 | tf_op jit(solution)/shard_map/ppermute | solution.py:96
  204.8 5.5 %all-to-all-start.4 = ((bf16[8,128,1024]{2,1,0:T(8,128)(2,1)}), bf16[8,128,1024]{2,1,0:T(8,128)(2,1)S(1)}, u32[]{:S(2)}, u32[]{:S(2)}) async-start(bf16[8,128,1024]{2,1,0:T(8,128)(2,1)} %bitcast.104), calls=%async_computation.4 | async-start | bytes 4194304 | tf_op jit(solution)/shard_map/all_to_all | solution.py:83
  215.2 14.1 %shard_map.218 = (bf16[1024,896]{1,0:T(8,128)(2,1)}, f32[8,8]{1,0:T(8,128)S(1)}) custom-call(bf16[1024,896]{1,0:T(8,128)(2,1)} %get-tuple-element.120.proj, f32[1024,8]{1,0:T(8,128)S(1)} %copy-done.35, f32[8,8]{1,0:T(8,128)S(1)} %fusion.15.refs_1_.small_ref, f32[1024,192]{1,0:T(8,128)S(1)} %copy-done.34, f32[4,192,128]{2,1,0:T(8,128)S(1)} %copy-done.38, ...), custom_call_target="tpu_custom_call" | custom-call | flops 19000000512 | bytes 1048576 | tf_op jit(solution)/shard_map/pallas_call | solution.py:444
  229.4 4.1 %convolution_convert_fusion.2 = bf16[1024,896]{1,0:T(8,128)(2,1)S(1)} fusion(bf16[1024,1024]{1,0:T(8,128)(2,1)S(1)} %copy-done.50, bf16[1024,896]{1,0:T(8,128)(2,1)} %get-tuple-element.140), kind=kOutput, calls=%fused_computation.2 | convolution fusion | flops 1879965696 | bytes 5767168 | tf_op jit(solution)/shard_map/dot_general | solution.py:35
  241.6 7.4 %all-to-all-start.5 = ((bf16[64,8,896]{2,1,0:T(8,128)(2,1)}), bf16[64,8,896]{2,1,0:T(8,128)(2,1)S(1)}, u32[]{:S(2)}, u32[]{:S(2)}) async-start(bf16[64,8,896]{2,1,0:T(8,128)(2,1)} %shard_map.219), calls=%async_computation.5 | async-start | bytes 1835008 | tf_op jit(solution)/shard_map/all_to_all | solution.py:707
  250.1 5.8 %convolution_convert_fusion = bf16[1024,1024]{1,0:T(8,128)(2,1)} fusion(bf16[1024,896]{1,0:T(8,128)(2,1)} %get-tuple-element.140, bf16[1024,896]{1,0:T(8,128)(2,1)} %get-tuple-element.141), kind=kOutput, calls=%fused_computation | convolution fusion | flops 1880096768 | bytes 5767168 | tf_op jit(solution)/shard_map/dot_general | solution.py:35
  255.8 5.4 %collective-permute-done.37 = bf16[64,1024]{1,0:T(8,128)(2,1)S(1)} collective-permute-done((bf16[64,1024]{1,0:T(8,128)(2,1)S(1)}, bf16[64,1024]{1,0:T(8,128)(2,1)S(1)}, u32[]{:S(2)}, u32[]{:S(2)}) %collective-permute-start.37) | collective-permute-done | bytes 131104 | tf_op jit(solution)/shard_map/ppermute | solution.py:701
  268.6 4.9 %collective-permute-done.39 = bf16[8,12416]{1,0:T(8,128)(2,1)S(1)} collective-permute-done((bf16[8,12416]{1,0:T(8,128)(2,1)S(1)}, bf16[8,12416]{1,0:T(8,128)(2,1)S(1)}, u32[]{:S(2)}, u32[]{:S(2)}) %collective-permute-start.39) | collective-permute-done | bytes 198688 | tf_op jit(solution)/shard_map/ppermute | solution.py:768
  273.5 6.3 %all-to-all-start.6 = ((bf16[8,128,1024]{2,1,0:T(8,128)(2,1)}), bf16[8,128,1024]{2,1,0:T(8,128)(2,1)S(1)}, u32[]{:S(2)}, u32[]{:S(2)}) async-start(bf16[8,128,1024]{2,1,0:T(8,128)(2,1)} %bitcast.107), calls=%async_computation.6 | async-start | bytes 4194304 | tf_op jit(solution)/shard_map/all_to_all | solution.py:83
  283.4 4.0 %collective-permute-start.43 = (bf16[16,12416]{1,0:T(8,128)(2,1)S(1)}, bf16[16,12416]{1,0:T(8,128)(2,1)S(1)}, u32[]{:S(2)}, u32[]{:S(2)}) collective-permute-start(bf16[16,12416]{1,0:T(8,128)(2,1)S(1)} %pad_maximum_fusion.3.refs_0_), channel_id=1, source_target_pairs={{0,8},{8,0},{16,24},{24,16},{32,40},{40,32},{48,56},{56,48},{64,72... | collective-permute-start | bytes 1191944 | tf_op jit(solution)/shard_map/ppermute | solution.py:96
  287.5 12.1 %collective-permute-start.44 = (bf16[16,12416]{1,0:T(8,128)(2,1)S(1)}, bf16[16,12416]{1,0:T(8,128)(2,1)S(1)}, u32[]{:S(2)}, u32[]{:S(2)}) collective-permute-start(bf16[16,12416]{1,0:T(8,128)(2,1)S(1)} %collective-permute-done.40.refs_1_), channel_id=1, source_target_pairs={{0,8},{8,0},{16,24},{24,16},{32,40},{40,32},{48,56},{56,48},{64,72... | collective-permute-start | bytes 1191944 | tf_op jit(solution)/shard_map/ppermute | solution.py:96
  299.6 3.1 collective-permute-done.42.refs_3_
  306.8 4.7 %shard_map.223 = (f32[3352,128]{1,0:T(8,128)}, f32[128,768]{1,0:T(8,128)}, f32[128,4096]{1,0:T(8,128)}, f32[256,1024]{1,0:T(8,128)}, f32[192,1024]{1,0:T(8,128)}...) custom-call(s32[4]{0:T(128)S(1)} %pad_add_fusion.where.refs_0_, bf16[128,3352]{1,0:T(8,128)(2,1)S(1)} %bitcast.92, ...), custom_call_target="tpu_custom_call" | custom-call | flops 6000000000 | bytes 1048576 | tf_op jit(solution)/shard_map/pallas_call | solution.py:604
  (227 shorter events, 99.6 us)
Async XLA Ops:
  1.8 14.3 %collective-permute-start = (bf16[128,2048]{1,0:T(8,128)(2,1)S(1)}, bf16[128,2048]{1,0:T(8,128)(2,1)}, u32[]{:S(2)}, u32[]{:S(2)}) collective-permute-start(bf16[128,2048]{1,0:T(8,128)(2,1)S(1)} %pad_maximum_fusion.1.refs_11_.refs_2_), channel_id=1, source_target_pairs={{0,1},{1,0},{2,3},{3,2},{4,5},{5,4},{6,7},{7,6},{8,9},{9,8},{10,11... | collective-permute-start | bytes 1572872 | tf_op jit(solution)/shard_map/ppermute | solution.py:62
  4.3 25.8 %collective-permute-start.1 = (bf16[128,2048]{1,0:T(8,128)(2,1)S(1)}, bf16[128,2048]{1,0:T(8,128)(2,1)S(1)}, u32[]{:S(2)}, u32[]{:S(2)}) collective-permute-start(bf16[128,2048]{1,0:T(8,128)(2,1)S(1)} %pad_maximum_fusion.1.refs_11_.refs_2_), channel_id=1, source_target_pairs={{0,2},{1,3},{2,4},{3,5},{4,6},{5,7},{6,0},{7,1},{8,10},{9,11},{10,... | collective-permute-start | bytes 1572872 | tf_op jit(solution)/shard_map/ppermute | solution.py:62
  5.5 24.9 %collective-permute-start.3 = (bf16[128,2048]{1,0:T(8,128)(2,1)S(1)}, bf16[128,2048]{1,0:T(8,128)(2,1)}, u32[]{:S(2)}, u32[]{:S(2)}) collective-permute-start(bf16[128,2048]{1,0:T(8,128)(2,1)S(1)} %pad_maximum_fusion.1.refs_11_.refs_2_), channel_id=1, source_target_pairs={{0,6},{1,7},{2,0},{3,1},{4,2},{5,3},{6,4},{7,5},{8,14},{9,15},{10,... | collective-permute-start | bytes 1572872 | tf_op jit(solution)/shard_map/ppermute | solution.py:62
  27.4 10.3 %collective-permute-start.5 = (bf16[8,16,1408]{2,1,0:T(8,128)(2,1)S(1)}, bf16[8,16,1408]{2,1,0:T(8,128)(2,1)S(1)}, u32[]{:S(2)}, u32[]{:S(2)}) collective-permute-start(bf16[8,16,1408]{2,1,0:T(8,128)(2,1)S(1)} %all_to_all.35.refs_3_), channel_id=1, source_target_pairs={{0,96},{8,104},{16,112},{24,120},{32,0},{40,8},{48,16},{56,24},{64... | collective-permute-start | bytes 1081352 | tf_op jit(solution)/shard_map/ppermute | solution.py:88
  33.9 15.4 %collective-permute-start.12 = (bf16[128,2048]{1,0:T(8,128)(2,1)}, bf16[128,2048]{1,0:T(8,128)(2,1)S(1)}, u32[]{:S(2)}, u32[]{:S(2)}) collective-permute-start(bf16[128,2048]{1,0:T(8,128)(2,1)} %collective-permute-done.refs_12_.refs_3_), channel_id=1, source_target_pairs={{0,2},{1,3},{2,4},{3,5},{4,6},{5,7},{6,0},{7,1},{8,10},{9,11},{10,... | collective-permute-start | bytes 1572872 | tf_op jit(solution)/shard_map/ppermute | solution.py:62
  33.9 18.3 %collective-permute-start.13 = (bf16[128,2048]{1,0:T(8,128)(2,1)}, bf16[128,2048]{1,0:T(8,128)(2,1)S(1)}, u32[]{:S(2)}, u32[]{:S(2)}) collective-permute-start(bf16[128,2048]{1,0:T(8,128)(2,1)} %collective-permute-done.refs_12_.refs_3_), channel_id=1, source_target_pairs={{0,6},{1,7},{2,0},{3,1},{4,2},{5,3},{6,4},{7,5},{8,14},{9,15},{10,... | collective-permute-start | bytes 1572872 | tf_op jit(solution)/shard_map/ppermute | solution.py:62
  36.6 15.7 %collective-permute-start.6 = (bf16[8,16,1408]{2,1,0:T(8,128)(2,1)S(1)}, bf16[8,16,1408]{2,1,0:T(8,128)(2,1)S(1)}, u32[]{:S(2)}, u32[]{:S(2)}) collective-permute-start(bf16[8,16,1408]{2,1,0:T(8,128)(2,1)S(1)} %all_to_all.35.refs_3_), channel_id=1, source_target_pairs={{0,64},{8,72},{16,80},{24,88},{32,96},{40,104},{48,112},{56,120},{... | collective-permute-start | bytes 1081352 | tf_op jit(solution)/shard_map/ppermute | solution.py:88
  37.2 15.7 %collective-permute-start.7 = (bf16[8,16,1408]{2,1,0:T(8,128)(2,1)S(1)}, bf16[8,16,1408]{2,1,0:T(8,128)(2,1)S(1)}, u32[]{:S(2)}, u32[]{:S(2)}) collective-permute-start(bf16[8,16,1408]{2,1,0:T(8,128)(2,1)S(1)} %all_to_all.35.refs_3_), channel_id=1, source_target_pairs={{0,32},{8,40},{16,48},{24,56},{32,64},{40,72},{48,80},{56,88},{64,... | collective-permute-start | bytes 1081352 | tf_op jit(solution)/shard_map/ppermute | solution.py:88
  37.7 20.4 %collective-permute-start.14 = (bf16[128,2048]{1,0:T(8,128)(2,1)S(1)}, bf16[128,2048]{1,0:T(8,128)(2,1)S(1)}, u32[]{:S(2)}, u32[]{:S(2)}) collective-permute-start(bf16[128,2048]{1,0:T(8,128)(2,1)S(1)} %pad_maximum_fusion.2), channel_id=1, source_target_pairs={{0,1},{1,0},{2,3},{3,2},{4,5},{5,4},{6,7},{7,6},{8,9},{9,8},{10,11... | collective-permute-start | bytes 1572872 | tf_op jit(solution)/shard_map/ppermute | solution.py:62
  49.3 8.4 %collective-permute-start.8 = (bf16[8,16,1408]{2,1,0:T(8,128)(2,1)S(1)}, bf16[8,16,1408]{2,1,0:T(8,128)(2,1)S(1)}, u32[]{:S(2)}, u32[]{:S(2)}) collective-permute-start(bf16[8,16,1408]{2,1,0:T(8,128)(2,1)S(1)} %all_to_all.35.refs_3_), channel_id=1, source_target_pairs={{0,8},{8,0},{16,24},{24,16},{32,40},{40,32},{48,56},{56,48},{64,72... | collective-permute-start | bytes 1081352 | tf_op jit(solution)/shard_map/ppermute | solution.py:96
  74.8 34.9 %all-to-all-start.1 = ((bf16[8,128,1024]{2,1,0:T(8,128)(2,1)}), bf16[8,128,1024]{2,1,0:T(8,128)(2,1)S(1)}, u32[]{:S(2)}, u32[]{:S(2)}) async-start(bf16[8,128,1024]{2,1,0:T(8,128)(2,1)} %bitcast.109), calls=%async_computation.1 | async-start | bytes 4194304 | tf_op jit(solution)/shard_map/all_to_all | solution.py:83
  111.0 9.8 %collective-permute-start.17 = (bf16[128,1024]{1,0:T(8,128)(2,1)S(1)}, bf16[128,1024]{1,0:T(8,128)(2,1)S(1)}, u32[]{:S(2)}, u32[]{:S(2)}) collective-permute-start(bf16[128,1024]{1,0:T(8,128)(2,1)S(1)} %get-tuple-element.96.refs_3_), channel_id=1, source_target_pairs={{0,6},{1,7},{2,0},{3,1},{4,2},{5,3},{6,4},{7,5},{8,14},{9,15},{10,... | collective-permute-start | bytes 786440 | tf_op jit(solution)/shard_map/ppermute | solution.py:52
  118.1 9.7 %collective-permute-start.20 = (bf16[128,1024]{1,0:T(8,128)(2,1)S(1)}, bf16[128,1024]{1,0:T(8,128)(2,1)S(1)}, u32[]{:S(2)}, u32[]{:S(2)}) collective-permute-start(bf16[128,1024]{1,0:T(8,128)(2,1)S(1)} %collective-permute-done.15.refs_4_), channel_id=1, source_target_pairs={{0,2},{1,3},{2,4},{3,5},{4,6},{5,7},{6,0},{7,1},{8,10},{9,11},{10,... | collective-permute-start | bytes 786440 | tf_op jit(solution)/shard_map/ppermute | solution.py:52
  118.1 9.6 %collective-permute-start.21 = (bf16[128,1024]{1,0:T(8,128)(2,1)S(1)}, bf16[128,1024]{1,0:T(8,128)(2,1)S(1)}, u32[]{:S(2)}, u32[]{:S(2)}) collective-permute-start(bf16[128,1024]{1,0:T(8,128)(2,1)S(1)} %collective-permute-done.15.refs_4_), channel_id=1, source_target_pairs={{0,6},{1,7},{2,0},{3,1},{4,2},{5,3},{6,4},{7,5},{8,14},{9,15},{10,... | collective-permute-start | bytes 786440 | tf_op jit(solution)/shard_map/ppermute | solution.py:52
  136.3 31.3 %all-to-all-start.2 = ((bf16[8,128,1024]{2,1,0:T(8,128)(2,1)}), bf16[8,128,1024]{2,1,0:T(8,128)(2,1)S(1)}, u32[]{:S(2)}, u32[]{:S(2)}) async-start(bf16[8,128,1024]{2,1,0:T(8,128)(2,1)} %bitcast.108), calls=%async_computation.2 | async-start | bytes 4194304 | tf_op jit(solution)/shard_map/all_to_all | solution.py:83
  169.9 9.0 %collective-permute-start.26 = (bf16[128,1024]{1,0:T(8,128)(2,1)S(1)}, bf16[128,1024]{1,0:T(8,128)(2,1)S(1)}, u32[]{:S(2)}, u32[]{:S(2)}) collective-permute-start(bf16[128,1024]{1,0:T(8,128)(2,1)S(1)} %get-tuple-element.106.refs_3_), channel_id=1, source_target_pairs={{0,2},{1,3},{2,4},{3,5},{4,6},{5,7},{6,0},{7,1},{8,10},{9,11},{10,... | collective-permute-start | bytes 786440 | tf_op jit(solution)/shard_map/ppermute | solution.py:52
  169.9 10.1 %collective-permute-start.25 = (bf16[128,1024]{1,0:T(8,128)(2,1)S(1)}, bf16[128,1024]{1,0:T(8,128)(2,1)S(1)}, u32[]{:S(2)}, u32[]{:S(2)}) collective-permute-start(bf16[128,1024]{1,0:T(8,128)(2,1)S(1)} %get-tuple-element.106.refs_3_), channel_id=1, source_target_pairs={{0,1},{1,0},{2,3},{3,2},{4,5},{5,4},{6,7},{7,6},{8,9},{9,8},{10,11... | collective-permute-start | bytes 786440 | tf_op jit(solution)/shard_map/ppermute | solution.py:52
  169.9 12.8 %collective-permute-start.27 = (bf16[128,1024]{1,0:T(8,128)(2,1)S(1)}, bf16[128,1024]{1,0:T(8,128)(2,1)S(1)}, u32[]{:S(2)}, u32[]{:S(2)}) collective-permute-start(bf16[128,1024]{1,0:T(8,128)(2,1)S(1)} %get-tuple-element.106.refs_3_), channel_id=1, source_target_pairs={{0,6},{1,7},{2,0},{3,1},{4,2},{5,3},{6,4},{7,5},{8,14},{9,15},{10,... | collective-permute-start | bytes 786440 | tf_op jit(solution)/shard_map/ppermute | solution.py:52
  172.5 20.8 %all-to-all-start.3 = ((bf16[64,8,512]{2,1,0:T(8,128)(2,1)}), bf16[64,8,512]{2,1,0:T(8,128)(2,1)S(1)}, u32[]{:S(2)}, u32[]{:S(2)}) async-start(bf16[64,8,512]{2,1,0:T(8,128)(2,1)} %bitcast.110), calls=%async_computation.3 | async-start | bytes 1048576 | tf_op jit(solution)/shard_map/all_to_all | solution.py:707
  179.9 14.2 %collective-permute-start.30 = (bf16[128,1024]{1,0:T(8,128)(2,1)S(1)}, bf16[128,1024]{1,0:T(8,128)(2,1)S(1)}, u32[]{:S(2)}, u32[]{:S(2)}) collective-permute-start(bf16[128,1024]{1,0:T(8,128)(2,1)S(1)} %collective-permute-done.25.refs_4_), channel_id=1, source_target_pairs={{0,2},{1,3},{2,4},{3,5},{4,6},{5,7},{6,0},{7,1},{8,10},{9,11},{10,... | collective-permute-start | bytes 786440 | tf_op jit(solution)/shard_map/ppermute | solution.py:52
  181.1 13.0 %collective-permute-start.31 = (bf16[128,1024]{1,0:T(8,128)(2,1)S(1)}, bf16[128,1024]{1,0:T(8,128)(2,1)S(1)}, u32[]{:S(2)}, u32[]{:S(2)}) collective-permute-start(bf16[128,1024]{1,0:T(8,128)(2,1)S(1)} %collective-permute-done.25.refs_4_), channel_id=1, source_target_pairs={{0,6},{1,7},{2,0},{3,1},{4,2},{5,3},{6,4},{7,5},{8,14},{9,15},{10,... | collective-permute-start | bytes 786440 | tf_op jit(solution)/shard_map/ppermute | solution.py:52
  182.6 9.0 %collective-permute-start.29 = (bf16[64,1024]{1,0:T(8,128)(2,1)S(1)}, bf16[64,1024]{1,0:T(8,128)(2,1)S(1)}, u32[]{:S(2)}, u32[]{:S(2)}) collective-permute-start(bf16[64,1024]{1,0:T(8,128)(2,1)S(1)} %slice.57), channel_id=1, source_target_pairs={{0,6},{1,7},{2,0},{3,1},{4,2},{5,3},{6,4},{7,5},{8,14},{9,15},{10,... | collective-permute-start | bytes 393224 | tf_op jit(solution)/shard_map/ppermute | solution.py:52
  200.2 10.2 %collective-permute-start.34 = (bf16[256,1024]{1,0:T(8,128)(2,1)}, bf16[256,1024]{1,0:T(8,128)(2,1)}, u32[]{:S(2)}, u32[]{:S(2)}) collective-permute-start(bf16[256,1024]{1,0:T(8,128)(2,1)} %broadcast_select_fusion), channel_id=1, source_target_pairs={{0,8},{8,0},{16,24},{24,16},{32,40},{40,32},{48,56},{56,48},{64,72... | collective-permute-start | bytes 1572872 | tf_op jit(solution)/shard_map/ppermute | solution.py:96
  204.8 36.8 %all-to-all-start.4 = ((bf16[8,128,1024]{2,1,0:T(8,128)(2,1)}), bf16[8,128,1024]{2,1,0:T(8,128)(2,1)S(1)}, u32[]{:S(2)}, u32[]{:S(2)}) async-start(bf16[8,128,1024]{2,1,0:T(8,128)(2,1)} %bitcast.104), calls=%async_computation.4 | async-start | bytes 4194304 | tf_op jit(solution)/shard_map/all_to_all | solution.py:83
  211.8 17.5 %collective-permute-start.35 = (bf16[128,1024]{1,0:T(8,128)(2,1)S(1)}, bf16[128,1024]{1,0:T(8,128)(2,1)S(1)}, u32[]{:S(2)}, u32[]{:S(2)}) collective-permute-start(bf16[128,1024]{1,0:T(8,128)(2,1)S(1)} %dynamic-slice_bitcast_fusion.3), channel_id=1, source_target_pairs={{0,64},{8,72},{16,80},{24,88},{32,96},{40,104},{48,112},{56,120},{... | collective-permute-start | bytes 786440 | tf_op jit(solution)/shard_map/ppermute | solution.py:701
  241.6 25.4 %all-to-all-start.5 = ((bf16[64,8,896]{2,1,0:T(8,128)(2,1)}), bf16[64,8,896]{2,1,0:T(8,128)(2,1)S(1)}, u32[]{:S(2)}, u32[]{:S(2)}) async-start(bf16[64,8,896]{2,1,0:T(8,128)(2,1)} %shard_map.219), calls=%async_computation.5 | async-start | bytes 1835008 | tf_op jit(solution)/shard_map/all_to_all | solution.py:707
  249.0 12.3 %collective-permute-start.37 = (bf16[64,1024]{1,0:T(8,128)(2,1)S(1)}, bf16[64,1024]{1,0:T(8,128)(2,1)S(1)}, u32[]{:S(2)}, u32[]{:S(2)}) collective-permute-start(bf16[64,1024]{1,0:T(8,128)(2,1)S(1)} %dynamic-slice_bitcast_fusion.4), channel_id=1, source_target_pairs={{0,32},{8,40},{16,48},{24,56},{32,0},{40,8},{48,16},{56,24},{64,96... | collective-permute-start | bytes 393224 | tf_op jit(solution)/shard_map/ppermute | solution.py:701
  273.5 39.2 %all-to-all-start.6 = ((bf16[8,128,1024]{2,1,0:T(8,128)(2,1)}), bf16[8,128,1024]{2,1,0:T(8,128)(2,1)S(1)}, u32[]{:S(2)}, u32[]{:S(2)}) async-start(bf16[8,128,1024]{2,1,0:T(8,128)(2,1)} %bitcast.107), calls=%async_computation.6 | async-start | bytes 4194304 | tf_op jit(solution)/shard_map/all_to_all | solution.py:83
  281.6 18.0 %collective-permute-start.41 = (bf16[16,12416]{1,0:T(8,128)(2,1)S(1)}, bf16[16,12416]{1,0:T(8,128)(2,1)S(1)}, u32[]{:S(2)}, u32[]{:S(2)}) collective-permute-start(bf16[16,12416]{1,0:T(8,128)(2,1)S(1)} %pad_maximum_fusion.3.refs_0_), channel_id=1, source_target_pairs={{0,64},{8,72},{16,80},{24,88},{32,96},{40,104},{48,112},{56,120},{... | collective-permute-start | bytes 1191944 | tf_op jit(solution)/shard_map/ppermute | solution.py:88
  282.7 20.0 %collective-permute-start.42 = (bf16[16,12416]{1,0:T(8,128)(2,1)S(1)}, bf16[16,12416]{1,0:T(8,128)(2,1)S(1)}, u32[]{:S(2)}, u32[]{:S(2)}) collective-permute-start(bf16[16,12416]{1,0:T(8,128)(2,1)S(1)} %pad_maximum_fusion.3.refs_0_), channel_id=1, source_target_pairs={{0,32},{8,40},{16,48},{24,56},{32,64},{40,72},{48,80},{56,88},{64,... | collective-permute-start | bytes 1191944 | tf_op jit(solution)/shard_map/ppermute | solution.py:88
  283.4 19.8 %collective-permute-start.43 = (bf16[16,12416]{1,0:T(8,128)(2,1)S(1)}, bf16[16,12416]{1,0:T(8,128)(2,1)S(1)}, u32[]{:S(2)}, u32[]{:S(2)}) collective-permute-start(bf16[16,12416]{1,0:T(8,128)(2,1)S(1)} %pad_maximum_fusion.3.refs_0_), channel_id=1, source_target_pairs={{0,8},{8,0},{16,24},{24,16},{32,40},{40,32},{48,56},{56,48},{64,72... | collective-permute-start | bytes 1191944 | tf_op jit(solution)/shard_map/ppermute | solution.py:96
  287.5 15.8 %collective-permute-start.44 = (bf16[16,12416]{1,0:T(8,128)(2,1)S(1)}, bf16[16,12416]{1,0:T(8,128)(2,1)S(1)}, u32[]{:S(2)}, u32[]{:S(2)}) collective-permute-start(bf16[16,12416]{1,0:T(8,128)(2,1)S(1)} %collective-permute-done.40.refs_1_), channel_id=1, source_target_pairs={{0,8},{8,0},{16,24},{24,16},{32,40},{40,32},{48,56},{56,48},{64,72... | collective-permute-start | bytes 1191944 | tf_op jit(solution)/shard_map/ppermute | solution.py:96
  (72 other events, 807.9 us)

commit v5 on v4

--- a/solution.py
+++ b/solution.py
@@ -765,8 +765,8 @@
     thin = halved(thin, high, 2)
     got, outputs = lax.optimization_barrier((to_owners(sent), outputs))
     rows = mixer_rows(got, gu_got, thin)
+    rows, e_part = lax.optimization_barrier((rows, e_part))
     other_rows = lax.ppermute(rows, "dp", [(i, i ^ 2) for i in range(DP)])
-    other_rows, e_part = lax.optimization_barrier((other_rows, e_part))
     blocks = round_y(jnp.concatenate([rows, other_rows], axis=0))
     blocks = (*blocks, *(core_swap(v) for v in blocks))
     (got,) = scatter_rows(e_part)

time: 321 us -> 320 us (level)
  waiting for transfers between devices: 94 us -> 90.4 us
    ppermute x1, waiting for transfers between devices: 4.87 us -> 0.01 us  [local(): other_rows = lax.ppermute(rows, 'dp', [(i, i ^ 2) for i in range(DP)])]
    unnamed x105 -> x102, local copies, waits for them, and re-layouts: 17.5 us -> 19.2 us
  transfers between devices with their start and end apart: 53 -> 53, of which waited for: 21 -> 21; matrix products, arithmetic and copies ran while one was open for 8% -> 9% of each run, Pallas kernels for 8% -> 9%
where the time goes in v5:
time: 320 us; the launch traced here: 315 us
  starting transfers between devices  113 us (35%)
  waiting for transfers between devices  90.4 us (28%)
  Pallas kernels  53.6 us (17%)
  local copies, waits for them, and re-layouts  23.5 us (7%)
  matrix products  16.6 us (5%)
  blocking collectives  11.3 us (4%)
  other arithmetic  4.7 us (1%)
    all_to_all x4, waiting for transfers between devices, scatter_rows(): lax.all_to_all(part.reshape(SEQ, ROWS, D), 'seq', split_axis=0, concat_ax...  38.7 us
    ppermute x11, starting transfers between devices, core_swap(): return lax.ppermute(v, 'dp', [(i, i ^ 1) for i in range(DP)])  33.4 us
    all_to_all x4, starting transfers between devices, scatter_rows(): lax.all_to_all(part.reshape(SEQ, ROWS, D), 'seq', split_axis=0, concat_ax...  21.1 us
    ppermute x18, waiting for transfers between devices, gather_pieces(): send = lambda v, perm: lax.ppermute(v, 'seq', perm)  19.9 us
    ppermute x18, starting transfers between devices, gather_pieces(): send = lambda v, perm: lax.ppermute(v, 'seq', perm)  19.4 us
    unnamed x102, local copies, waits for them, and re-layouts  19.2 us
    dot_general x5, matrix products, dot(): lax.dot_general(a, b, (dims, ((), ())), precision=precision, preferred_el...  16.6 us
    ppermute x8, waiting for transfers between devices, gather_with_weights(): send = lambda v, perm: lax.ppermute(v, 'seq', perm)  15.2 us
  transfers between devices with their start and end apart: 53, of which 21 were waited for; matrix products, arithmetic and copies ran while one was open for 9% of the time, Pallas kernels for 9%

profile of v5, /device:TPU:1, one launch (start us, length us, event | category | flops | bytes accessed | tf_op | source)
XLA Modules:
  0.0 314.5 jit_solution(11731462410810559593)
XLA Ops:
  12.0 4.1 %collective-permute-done.refs_12_.refs_3_ = bf16[128,2048]{1,0:T(8,128)(2,1)} collective-permute-done((bf16[128,2048]{1,0:T(8,128)(2,1)S(1)}, bf16[128,2048]{1,0:T(8,128)(2,1)}, u32[]{:S(2)}, u32[]{:S(2)}) %collective-permute-start) | collective-permute-done | bytes 524320 | tf_op jit(solution)/shard_map/ppermute | solution.py:62
  16.1 11.3 %all_to_all.35.refs_3_ = bf16[8,16,1408]{2,1,0:T(8,128)(2,1)S(1)} all-to-all(bf16[8,16,1408]{2,1,0:T(8,128)(2,1)S(1)} %shard_map.211), channel_id=1, replica_groups=mesh['dp'=16,'seq'=8] {'seq'}, dimensions={0} | all-to-all | bytes 720896 | tf_op jit(solution)/shard_map/all_to_all | solution.py:65
  38.4 10.8 %collective-permute-done.12.refs_17_.refs_8_ = bf16[128,2048]{1,0:T(8,128)(2,1)S(1)} collective-permute-done((bf16[128,2048]{1,0:T(8,128)(2,1)}, bf16[128,2048]{1,0:T(8,128)(2,1)S(1)}, u32[]{:S(2)}, u32[]{:S(2)}) %collective-permute-start.12) | collective-permute-done | bytes 524320 | tf_op jit(solution)/shard_map/ppermute | solution.py:62
  49.3 2.9 collective-permute-start.8
  53.0 3.9 %collective-permute-start.11 = (bf16[8,16,1408]{2,1,0:T(8,128)(2,1)S(1)}, bf16[8,16,1408]{2,1,0:T(8,128)(2,1)S(1)}, u32[]{:S(2)}, u32[]{:S(2)}) collective-permute-start(bf16[8,16,1408]{2,1,0:T(8,128)(2,1)S(1)} %collective-permute-done.7.refs_6_), channel_id=1, source_target_pairs={{0,8},{8,0},{16,24},{24,16},{32,40},{40,32},{48,56},{56,48},{64,72... | collective-permute-start | bytes 1081352 | tf_op jit(solution)/shard_map/ppermute | solution.py:96
  58.9 15.1 %shard_map.212 = (bf16[1024,1024]{1,0:T(8,128)(2,1)}, bf16[1024,896]{1,0:T(8,128)(2,1)}, bf16[1024,512]{1,0:T(8,128)(2,1)}, bf16[1024,896]{1,0:T(8,128)(2,1)}, f...) custom-call(s32[4]{0:T(128)S(1)} %pad_add_fusion.where.refs_0_, ...), custom_call_target="tpu_custom_call" | custom-call | flops 16000000000 | bytes 1048576 | tf_op jit(solution)/shard_map/pallas_call | solution.py:347
  74.8 3.7 %all-to-all-start.1 = ((bf16[8,128,1024]{2,1,0:T(8,128)(2,1)}), bf16[8,128,1024]{2,1,0:T(8,128)(2,1)S(1)}, u32[]{:S(2)}, u32[]{:S(2)}) async-start(bf16[8,128,1024]{2,1,0:T(8,128)(2,1)} %bitcast.109), calls=%async_computation.1 | async-start | bytes 4194304 | tf_op jit(solution)/shard_map/all_to_all | solution.py:83
  81.5 3.7 %shard_map.213 = (bf16[1024,1024]{1,0:T(8,128)(2,1)}, bf16[1024,256]{1,0:T(8,128)(2,1)S(1)}) custom-call(s32[4]{0:T(128)S(1)} %pad_add_fusion.where.refs_0_, bf16[256,1024]{1,0:T(8,128)(2,1)S(1)} %bitcast.93, bf16[128,2048]{1,0:T(8,128)(2,1)S(1)} %copy-done.6, bf16[128,2048]{1,0:T(8,128)(2,1)} %collective-permute-done.refs_12_.refs_3_, ...), custom_call_target="tpu_custom_call" | custom-call | flops 3000000000 | bytes 1048576 | tf_op jit(solution)/shard_map/pallas_call | solution.py:410
  86.0 23.7 %all-to-all-done.1.got = bf16[8,128,1024]{2,1,0:T(8,128)(2,1)S(1)} async-done(((bf16[8,128,1024]{2,1,0:T(8,128)(2,1)}), bf16[8,128,1024]{2,1,0:T(8,128)(2,1)S(1)}, u32[]{:S(2)}, u32[]{:S(2)}) %all-to-all-start.1) | async-done | bytes 2097184 | tf_op jit(solution)/shard_map/all_to_all | solution.py:83
  110.9 3.0 collective-permute-start.17
  113.9 4.0 %collective-permute-done.16.refs_5_ = bf16[128,1024]{1,0:T(8,128)(2,1)S(1)} collective-permute-done((bf16[128,1024]{1,0:T(8,128)(2,1)S(1)}, bf16[128,1024]{1,0:T(8,128)(2,1)S(1)}, u32[]{:S(2)}, u32[]{:S(2)}) %collective-permute-start.16) | collective-permute-done | bytes 262176 | tf_op jit(solution)/shard_map/ppermute | solution.py:52
  123.7 3.0 collective-permute-done.19.refs_8_
  130.6 5.6 %shard_map.215 = (bf16[1024,1024]{1,0:T(8,128)(2,1)}, bf16[1024,256]{1,0:T(8,128)(2,1)S(1)}, bf16[1024,512]{1,0:T(8,128)(2,1)}, bf16[1024,1024]{1,0:T(8,128)(2,1)}) custom-call(s32[4]{0:T(128)S(1)} %pad_add_fusion.where.refs_0_, bf16[1024,512]{1,0:T(8,128)(2,1)} %get-tuple-element.90.refs_1_, bf16[1024,256]{1,0:T(8,128)(2,1)S(1)} %copy-done.29, ...), custom_call_target="tpu_custom_call" | custom-call | flops 6000000000 | bytes 1048576 | tf_op jit(solution)/shard_map/pallas_call | solution.py:387
  136.2 5.1 %all-to-all-start.2 = ((bf16[8,128,1024]{2,1,0:T(8,128)(2,1)}), bf16[8,128,1024]{2,1,0:T(8,128)(2,1)S(1)}, u32[]{:S(2)}, u32[]{:S(2)}) async-start(bf16[8,128,1024]{2,1,0:T(8,128)(2,1)} %bitcast.108), calls=%async_computation.2 | async-start | bytes 4194304 | tf_op jit(solution)/shard_map/all_to_all | solution.py:83
  141.3 3.1 convolution_convert_fusion.3
  144.5 4.9 %collective-permute-start.24 = (bf16[8,64,512]{2,1,0:T(8,128)(2,1)S(1)}, bf16[8,64,512]{2,1,0:T(8,128)(2,1)S(1)}, u32[]{:S(2)}, u32[]{:S(2)}) collective-permute-start(bf16[8,64,512]{2,1,0:T(8,128)(2,1)S(1)} %dynamic-slice_bitcast_fusion.2), channel_id=1, source_target_pairs={{0,8},{8,0},{16,24},{24,16},{32,40},{40,32},{48,56},{56,48},{64,72... | collective-permute-start | bytes 1572872 | tf_op jit(solution)/shard_map/ppermute | solution.py:96
  153.9 13.5 %all-to-all-done.2.got = bf16[8,128,1024]{2,1,0:T(8,128)(2,1)S(1)} async-done(((bf16[8,128,1024]{2,1,0:T(8,128)(2,1)}), bf16[8,128,1024]{2,1,0:T(8,128)(2,1)S(1)}, u32[]{:S(2)}, u32[]{:S(2)}) %all-to-all-start.2) | async-done | bytes 2097184 | tf_op jit(solution)/shard_map/all_to_all | solution.py:83
  172.5 6.4 %all-to-all-start.3 = ((bf16[64,8,512]{2,1,0:T(8,128)(2,1)}), bf16[64,8,512]{2,1,0:T(8,128)(2,1)S(1)}, u32[]{:S(2)}, u32[]{:S(2)}) async-start(bf16[64,8,512]{2,1,0:T(8,128)(2,1)} %bitcast.110), calls=%async_computation.3 | async-start | bytes 1048576 | tf_op jit(solution)/shard_map/all_to_all | solution.py:707
  183.2 2.9 collective-permute-done.28.refs_7_
  187.4 4.1 %collective-permute-done.29.refs_8_ = bf16[64,1024]{1,0:T(8,128)(2,1)S(1)} collective-permute-done((bf16[64,1024]{1,0:T(8,128)(2,1)S(1)}, bf16[64,1024]{1,0:T(8,128)(2,1)S(1)}, u32[]{:S(2)}, u32[]{:S(2)}) %collective-permute-start.29) | collective-permute-done | bytes 131104 | tf_op jit(solution)/shard_map/ppermute | solution.py:52
  200.0 4.8 %collective-permute-start.34 = (bf16[256,1024]{1,0:T(8,128)(2,1)}, bf16[256,1024]{1,0:T(8,128)(2,1)}, u32[]{:S(2)}, u32[]{:S(2)}) collective-permute-start(bf16[256,1024]{1,0:T(8,128)(2,1)} %broadcast_select_fusion), channel_id=1, source_target_pairs={{0,8},{8,0},{16,24},{24,16},{32,40},{40,32},{48,56},{56,48},{64,72... | collective-permute-start | bytes 1572872 | tf_op jit(solution)/shard_map/ppermute | solution.py:96
  204.8 5.5 %all-to-all-start.4 = ((bf16[8,128,1024]{2,1,0:T(8,128)(2,1)}), bf16[8,128,1024]{2,1,0:T(8,128)(2,1)S(1)}, u32[]{:S(2)}, u32[]{:S(2)}) async-start(bf16[8,128,1024]{2,1,0:T(8,128)(2,1)} %bitcast.104), calls=%async_computation.4 | async-start | bytes 4194304 | tf_op jit(solution)/shard_map/all_to_all | solution.py:83
  215.2 14.1 %shard_map.218 = (bf16[1024,896]{1,0:T(8,128)(2,1)}, f32[8,8]{1,0:T(8,128)S(1)}) custom-call(bf16[1024,896]{1,0:T(8,128)(2,1)} %get-tuple-element.120.proj, f32[1024,8]{1,0:T(8,128)S(1)} %copy-done.33, f32[8,8]{1,0:T(8,128)S(1)} %fusion.15.refs_1_.small_ref, f32[1024,192]{1,0:T(8,128)S(1)} %copy-done.32, f32[4,192,128]{2,1,0:T(8,128)S(1)} %copy-done.36, ...), custom_call_target="tpu_custom_call" | custom-call | flops 19000000512 | bytes 1048576 | tf_op jit(solution)/shard_map/pallas_call | solution.py:444
  229.4 4.1 %convolution_convert_fusion.2 = bf16[1024,896]{1,0:T(8,128)(2,1)S(1)} fusion(bf16[1024,1024]{1,0:T(8,128)(2,1)S(1)} %copy-done.48, bf16[1024,896]{1,0:T(8,128)(2,1)} %get-tuple-element.140), kind=kOutput, calls=%fused_computation.2 | convolution fusion | flops 1879965696 | bytes 5767168 | tf_op jit(solution)/shard_map/dot_general | solution.py:35
  241.5 7.4 %all-to-all-start.5 = ((bf16[64,8,896]{2,1,0:T(8,128)(2,1)}), bf16[64,8,896]{2,1,0:T(8,128)(2,1)S(1)}, u32[]{:S(2)}, u32[]{:S(2)}) async-start(bf16[64,8,896]{2,1,0:T(8,128)(2,1)} %shard_map.219), calls=%async_computation.5 | async-start | bytes 1835008 | tf_op jit(solution)/shard_map/all_to_all | solution.py:707
  250.1 5.8 %convolution_convert_fusion = bf16[1024,1024]{1,0:T(8,128)(2,1)} fusion(bf16[1024,896]{1,0:T(8,128)(2,1)} %get-tuple-element.140, bf16[1024,896]{1,0:T(8,128)(2,1)} %get-tuple-element.141), kind=kOutput, calls=%fused_computation | convolution fusion | flops 1880096768 | bytes 5767168 | tf_op jit(solution)/shard_map/dot_general | solution.py:35
  255.9 5.3 %collective-permute-done.37 = bf16[64,1024]{1,0:T(8,128)(2,1)S(1)} collective-permute-done((bf16[64,1024]{1,0:T(8,128)(2,1)S(1)}, bf16[64,1024]{1,0:T(8,128)(2,1)S(1)}, u32[]{:S(2)}, u32[]{:S(2)}) %collective-permute-start.37) | collective-permute-done | bytes 131104 | tf_op jit(solution)/shard_map/ppermute | solution.py:701
  270.9 6.8 %all-to-all-start.6 = ((bf16[8,128,1024]{2,1,0:T(8,128)(2,1)}), bf16[8,128,1024]{2,1,0:T(8,128)(2,1)S(1)}, u32[]{:S(2)}, u32[]{:S(2)}) async-start(bf16[8,128,1024]{2,1,0:T(8,128)(2,1)} %bitcast.107), calls=%async_computation.6 | async-start | bytes 4194304 | tf_op jit(solution)/shard_map/all_to_all | solution.py:83
  281.8 3.4 %collective-permute-start.43 = (bf16[16,12416]{1,0:T(8,128)(2,1)}, bf16[16,12416]{1,0:T(8,128)(2,1)S(1)}, u32[]{:S(2)}, u32[]{:S(2)}) collective-permute-start(bf16[16,12416]{1,0:T(8,128)(2,1)} %constant_dynamic-update-slice_fusion.refs_0_), channel_id=1, source_target_pairs={{0,8},{8,0},{16,24},{24,16},{32,40},{40,32},{48,56},{56,48},{64,72... | collective-permute-start | bytes 1191944 | tf_op jit(solution)/shard_map/ppermute | solution.py:96
  286.8 11.8 %collective-permute-start.44 = (bf16[16,12416]{1,0:T(8,128)(2,1)S(1)}, bf16[16,12416]{1,0:T(8,128)(2,1)S(1)}, u32[]{:S(2)}, u32[]{:S(2)}) collective-permute-start(bf16[16,12416]{1,0:T(8,128)(2,1)S(1)} %collective-permute-done.40.refs_1_), channel_id=1, source_target_pairs={{0,8},{8,0},{16,24},{24,16},{32,40},{40,32},{48,56},{56,48},{64,72... | collective-permute-start | bytes 1191944 | tf_op jit(solution)/shard_map/ppermute | solution.py:96
  298.6 3.1 collective-permute-done.42.refs_3_
  305.6 5.2 %shard_map.223 = (f32[3352,128]{1,0:T(8,128)}, f32[128,768]{1,0:T(8,128)}, f32[128,4096]{1,0:T(8,128)}, f32[256,1024]{1,0:T(8,128)}, f32[192,1024]{1,0:T(8,128)}...) custom-call(s32[4]{0:T(128)S(1)} %pad_add_fusion.where.refs_0_, bf16[128,3352]{1,0:T(8,128)(2,1)S(1)} %bitcast.92, ...), custom_call_target="tpu_custom_call" | custom-call | flops 6000000000 | bytes 1048576 | tf_op jit(solution)/shard_map/pallas_call | solution.py:604
  (224 shorter events, 100.9 us)
Async XLA Ops:
  1.8 14.3 %collective-permute-start = (bf16[128,2048]{1,0:T(8,128)(2,1)S(1)}, bf16[128,2048]{1,0:T(8,128)(2,1)}, u32[]{:S(2)}, u32[]{:S(2)}) collective-permute-start(bf16[128,2048]{1,0:T(8,128)(2,1)S(1)} %pad_maximum_fusion.1.refs_11_.refs_2_), channel_id=1, source_target_pairs={{0,1},{1,0},{2,3},{3,2},{4,5},{5,4},{6,7},{7,6},{8,9},{9,8},{10,11... | collective-permute-start | bytes 1572872 | tf_op jit(solution)/shard_map/ppermute | solution.py:62
  4.3 25.8 %collective-permute-start.1 = (bf16[128,2048]{1,0:T(8,128)(2,1)S(1)}, bf16[128,2048]{1,0:T(8,128)(2,1)S(1)}, u32[]{:S(2)}, u32[]{:S(2)}) collective-permute-start(bf16[128,2048]{1,0:T(8,128)(2,1)S(1)} %pad_maximum_fusion.1.refs_11_.refs_2_), channel_id=1, source_target_pairs={{0,2},{1,3},{2,4},{3,5},{4,6},{5,7},{6,0},{7,1},{8,10},{9,11},{10,... | collective-permute-start | bytes 1572872 | tf_op jit(solution)/shard_map/ppermute | solution.py:62
  5.5 24.9 %collective-permute-start.3 = (bf16[128,2048]{1,0:T(8,128)(2,1)S(1)}, bf16[128,2048]{1,0:T(8,128)(2,1)}, u32[]{:S(2)}, u32[]{:S(2)}) collective-permute-start(bf16[128,2048]{1,0:T(8,128)(2,1)S(1)} %pad_maximum_fusion.1.refs_11_.refs_2_), channel_id=1, source_target_pairs={{0,6},{1,7},{2,0},{3,1},{4,2},{5,3},{6,4},{7,5},{8,14},{9,15},{10,... | collective-permute-start | bytes 1572872 | tf_op jit(solution)/shard_map/ppermute | solution.py:62
  27.4 10.3 %collective-permute-start.5 = (bf16[8,16,1408]{2,1,0:T(8,128)(2,1)S(1)}, bf16[8,16,1408]{2,1,0:T(8,128)(2,1)S(1)}, u32[]{:S(2)}, u32[]{:S(2)}) collective-permute-start(bf16[8,16,1408]{2,1,0:T(8,128)(2,1)S(1)} %all_to_all.35.refs_3_), channel_id=1, source_target_pairs={{0,96},{8,104},{16,112},{24,120},{32,0},{40,8},{48,16},{56,24},{64... | collective-permute-start | bytes 1081352 | tf_op jit(solution)/shard_map/ppermute | solution.py:88
  33.9 15.4 %collective-permute-start.12 = (bf16[128,2048]{1,0:T(8,128)(2,1)}, bf16[128,2048]{1,0:T(8,128)(2,1)S(1)}, u32[]{:S(2)}, u32[]{:S(2)}) collective-permute-start(bf16[128,2048]{1,0:T(8,128)(2,1)} %collective-permute-done.refs_12_.refs_3_), channel_id=1, source_target_pairs={{0,2},{1,3},{2,4},{3,5},{4,6},{5,7},{6,0},{7,1},{8,10},{9,11},{10,... | collective-permute-start | bytes 1572872 | tf_op jit(solution)/shard_map/ppermute | solution.py:62
  33.9 18.3 %collective-permute-start.13 = (bf16[128,2048]{1,0:T(8,128)(2,1)}, bf16[128,2048]{1,0:T(8,128)(2,1)S(1)}, u32[]{:S(2)}, u32[]{:S(2)}) collective-permute-start(bf16[128,2048]{1,0:T(8,128)(2,1)} %collective-permute-done.refs_12_.refs_3_), channel_id=1, source_target_pairs={{0,6},{1,7},{2,0},{3,1},{4,2},{5,3},{6,4},{7,5},{8,14},{9,15},{10,... | collective-permute-start | bytes 1572872 | tf_op jit(solution)/shard_map/ppermute | solution.py:62
  36.6 15.7 %collective-permute-start.6 = (bf16[8,16,1408]{2,1,0:T(8,128)(2,1)S(1)}, bf16[8,16,1408]{2,1,0:T(8,128)(2,1)S(1)}, u32[]{:S(2)}, u32[]{:S(2)}) collective-permute-start(bf16[8,16,1408]{2,1,0:T(8,128)(2,1)S(1)} %all_to_all.35.refs_3_), channel_id=1, source_target_pairs={{0,64},{8,72},{16,80},{24,88},{32,96},{40,104},{48,112},{56,120},{... | collective-permute-start | bytes 1081352 | tf_op jit(solution)/shard_map/ppermute | solution.py:88
  37.2 15.7 %collective-permute-start.7 = (bf16[8,16,1408]{2,1,0:T(8,128)(2,1)S(1)}, bf16[8,16,1408]{2,1,0:T(8,128)(2,1)S(1)}, u32[]{:S(2)}, u32[]{:S(2)}) collective-permute-start(bf16[8,16,1408]{2,1,0:T(8,128)(2,1)S(1)} %all_to_all.35.refs_3_), channel_id=1, source_target_pairs={{0,32},{8,40},{16,48},{24,56},{32,64},{40,72},{48,80},{56,88},{64,... | collective-permute-start | bytes 1081352 | tf_op jit(solution)/shard_map/ppermute | solution.py:88
  37.7 20.4 %collective-permute-start.14 = (bf16[128,2048]{1,0:T(8,128)(2,1)S(1)}, bf16[128,2048]{1,0:T(8,128)(2,1)S(1)}, u32[]{:S(2)}, u32[]{:S(2)}) collective-permute-start(bf16[128,2048]{1,0:T(8,128)(2,1)S(1)} %pad_maximum_fusion.2), channel_id=1, source_target_pairs={{0,1},{1,0},{2,3},{3,2},{4,5},{5,4},{6,7},{7,6},{8,9},{9,8},{10,11... | collective-permute-start | bytes 1572872 | tf_op jit(solution)/shard_map/ppermute | solution.py:62
  74.8 34.8 %all-to-all-start.1 = ((bf16[8,128,1024]{2,1,0:T(8,128)(2,1)}), bf16[8,128,1024]{2,1,0:T(8,128)(2,1)S(1)}, u32[]{:S(2)}, u32[]{:S(2)}) async-start(bf16[8,128,1024]{2,1,0:T(8,128)(2,1)} %bitcast.109), calls=%async_computation.1 | async-start | bytes 4194304 | tf_op jit(solution)/shard_map/all_to_all | solution.py:83
  110.9 9.9 %collective-permute-start.17 = (bf16[128,1024]{1,0:T(8,128)(2,1)S(1)}, bf16[128,1024]{1,0:T(8,128)(2,1)S(1)}, u32[]{:S(2)}, u32[]{:S(2)}) collective-permute-start(bf16[128,1024]{1,0:T(8,128)(2,1)S(1)} %get-tuple-element.96.refs_3_), channel_id=1, source_target_pairs={{0,6},{1,7},{2,0},{3,1},{4,2},{5,3},{6,4},{7,5},{8,14},{9,15},{10,... | collective-permute-start | bytes 786440 | tf_op jit(solution)/shard_map/ppermute | solution.py:52
  118.0 9.7 %collective-permute-start.20 = (bf16[128,1024]{1,0:T(8,128)(2,1)S(1)}, bf16[128,1024]{1,0:T(8,128)(2,1)S(1)}, u32[]{:S(2)}, u32[]{:S(2)}) collective-permute-start(bf16[128,1024]{1,0:T(8,128)(2,1)S(1)} %collective-permute-done.15.refs_4_), channel_id=1, source_target_pairs={{0,2},{1,3},{2,4},{3,5},{4,6},{5,7},{6,0},{7,1},{8,10},{9,11},{10,... | collective-permute-start | bytes 786440 | tf_op jit(solution)/shard_map/ppermute | solution.py:52
  118.1 9.6 %collective-permute-start.21 = (bf16[128,1024]{1,0:T(8,128)(2,1)S(1)}, bf16[128,1024]{1,0:T(8,128)(2,1)S(1)}, u32[]{:S(2)}, u32[]{:S(2)}) collective-permute-start(bf16[128,1024]{1,0:T(8,128)(2,1)S(1)} %collective-permute-done.15.refs_4_), channel_id=1, source_target_pairs={{0,6},{1,7},{2,0},{3,1},{4,2},{5,3},{6,4},{7,5},{8,14},{9,15},{10,... | collective-permute-start | bytes 786440 | tf_op jit(solution)/shard_map/ppermute | solution.py:52
  136.2 31.2 %all-to-all-start.2 = ((bf16[8,128,1024]{2,1,0:T(8,128)(2,1)}), bf16[8,128,1024]{2,1,0:T(8,128)(2,1)S(1)}, u32[]{:S(2)}, u32[]{:S(2)}) async-start(bf16[8,128,1024]{2,1,0:T(8,128)(2,1)} %bitcast.108), calls=%async_computation.2 | async-start | bytes 4194304 | tf_op jit(solution)/shard_map/all_to_all | solution.py:83
  169.8 9.1 %collective-permute-start.26 = (bf16[128,1024]{1,0:T(8,128)(2,1)S(1)}, bf16[128,1024]{1,0:T(8,128)(2,1)S(1)}, u32[]{:S(2)}, u32[]{:S(2)}) collective-permute-start(bf16[128,1024]{1,0:T(8,128)(2,1)S(1)} %get-tuple-element.106.refs_3_), channel_id=1, source_target_pairs={{0,2},{1,3},{2,4},{3,5},{4,6},{5,7},{6,0},{7,1},{8,10},{9,11},{10,... | collective-permute-start | bytes 786440 | tf_op jit(solution)/shard_map/ppermute | solution.py:52
  169.8 10.2 %collective-permute-start.25 = (bf16[128,1024]{1,0:T(8,128)(2,1)S(1)}, bf16[128,1024]{1,0:T(8,128)(2,1)S(1)}, u32[]{:S(2)}, u32[]{:S(2)}) collective-permute-start(bf16[128,1024]{1,0:T(8,128)(2,1)S(1)} %get-tuple-element.106.refs_3_), channel_id=1, source_target_pairs={{0,1},{1,0},{2,3},{3,2},{4,5},{5,4},{6,7},{7,6},{8,9},{9,8},{10,11... | collective-permute-start | bytes 786440 | tf_op jit(solution)/shard_map/ppermute | solution.py:52
  169.8 12.9 %collective-permute-start.27 = (bf16[128,1024]{1,0:T(8,128)(2,1)S(1)}, bf16[128,1024]{1,0:T(8,128)(2,1)S(1)}, u32[]{:S(2)}, u32[]{:S(2)}) collective-permute-start(bf16[128,1024]{1,0:T(8,128)(2,1)S(1)} %get-tuple-element.106.refs_3_), channel_id=1, source_target_pairs={{0,6},{1,7},{2,0},{3,1},{4,2},{5,3},{6,4},{7,5},{8,14},{9,15},{10,... | collective-permute-start | bytes 786440 | tf_op jit(solution)/shard_map/ppermute | solution.py:52
  172.5 20.7 %all-to-all-start.3 = ((bf16[64,8,512]{2,1,0:T(8,128)(2,1)}), bf16[64,8,512]{2,1,0:T(8,128)(2,1)S(1)}, u32[]{:S(2)}, u32[]{:S(2)}) async-start(bf16[64,8,512]{2,1,0:T(8,128)(2,1)} %bitcast.110), calls=%async_computation.3 | async-start | bytes 1048576 | tf_op jit(solution)/shard_map/all_to_all | solution.py:707
  180.0 14.0 %collective-permute-start.30 = (bf16[128,1024]{1,0:T(8,128)(2,1)S(1)}, bf16[128,1024]{1,0:T(8,128)(2,1)S(1)}, u32[]{:S(2)}, u32[]{:S(2)}) collective-permute-start(bf16[128,1024]{1,0:T(8,128)(2,1)S(1)} %collective-permute-done.25.refs_4_), channel_id=1, source_target_pairs={{0,2},{1,3},{2,4},{3,5},{4,6},{5,7},{6,0},{7,1},{8,10},{9,11},{10,... | collective-permute-start | bytes 786440 | tf_op jit(solution)/shard_map/ppermute | solution.py:52
  181.2 12.9 %collective-permute-start.31 = (bf16[128,1024]{1,0:T(8,128)(2,1)S(1)}, bf16[128,1024]{1,0:T(8,128)(2,1)S(1)}, u32[]{:S(2)}, u32[]{:S(2)}) collective-permute-start(bf16[128,1024]{1,0:T(8,128)(2,1)S(1)} %collective-permute-done.25.refs_4_), channel_id=1, source_target_pairs={{0,6},{1,7},{2,0},{3,1},{4,2},{5,3},{6,4},{7,5},{8,14},{9,15},{10,... | collective-permute-start | bytes 786440 | tf_op jit(solution)/shard_map/ppermute | solution.py:52
  182.7 8.9 %collective-permute-start.29 = (bf16[64,1024]{1,0:T(8,128)(2,1)S(1)}, bf16[64,1024]{1,0:T(8,128)(2,1)S(1)}, u32[]{:S(2)}, u32[]{:S(2)}) collective-permute-start(bf16[64,1024]{1,0:T(8,128)(2,1)S(1)} %slice.57), channel_id=1, source_target_pairs={{0,6},{1,7},{2,0},{3,1},{4,2},{5,3},{6,4},{7,5},{8,14},{9,15},{10,... | collective-permute-start | bytes 393224 | tf_op jit(solution)/shard_map/ppermute | solution.py:52
  200.0 10.3 %collective-permute-start.34 = (bf16[256,1024]{1,0:T(8,128)(2,1)}, bf16[256,1024]{1,0:T(8,128)(2,1)}, u32[]{:S(2)}, u32[]{:S(2)}) collective-permute-start(bf16[256,1024]{1,0:T(8,128)(2,1)} %broadcast_select_fusion), channel_id=1, source_target_pairs={{0,8},{8,0},{16,24},{24,16},{32,40},{40,32},{48,56},{56,48},{64,72... | collective-permute-start | bytes 1572872 | tf_op jit(solution)/shard_map/ppermute | solution.py:96
  204.8 36.7 %all-to-all-start.4 = ((bf16[8,128,1024]{2,1,0:T(8,128)(2,1)}), bf16[8,128,1024]{2,1,0:T(8,128)(2,1)S(1)}, u32[]{:S(2)}, u32[]{:S(2)}) async-start(bf16[8,128,1024]{2,1,0:T(8,128)(2,1)} %bitcast.104), calls=%async_computation.4 | async-start | bytes 4194304 | tf_op jit(solution)/shard_map/all_to_all | solution.py:83
  211.8 17.6 %collective-permute-start.35 = (bf16[128,1024]{1,0:T(8,128)(2,1)S(1)}, bf16[128,1024]{1,0:T(8,128)(2,1)S(1)}, u32[]{:S(2)}, u32[]{:S(2)}) collective-permute-start(bf16[128,1024]{1,0:T(8,128)(2,1)S(1)} %dynamic-slice_bitcast_fusion.3), channel_id=1, source_target_pairs={{0,64},{8,72},{16,80},{24,88},{32,96},{40,104},{48,112},{56,120},{... | collective-permute-start | bytes 786440 | tf_op jit(solution)/shard_map/ppermute | solution.py:701
  241.5 25.4 %all-to-all-start.5 = ((bf16[64,8,896]{2,1,0:T(8,128)(2,1)}), bf16[64,8,896]{2,1,0:T(8,128)(2,1)S(1)}, u32[]{:S(2)}, u32[]{:S(2)}) async-start(bf16[64,8,896]{2,1,0:T(8,128)(2,1)} %shard_map.219), calls=%async_computation.5 | async-start | bytes 1835008 | tf_op jit(solution)/shard_map/all_to_all | solution.py:707
  249.0 12.2 %collective-permute-start.37 = (bf16[64,1024]{1,0:T(8,128)(2,1)S(1)}, bf16[64,1024]{1,0:T(8,128)(2,1)S(1)}, u32[]{:S(2)}, u32[]{:S(2)}) collective-permute-start(bf16[64,1024]{1,0:T(8,128)(2,1)S(1)} %dynamic-slice_bitcast_fusion.4), channel_id=1, source_target_pairs={{0,32},{8,40},{16,48},{24,56},{32,0},{40,8},{48,16},{56,24},{64,96... | collective-permute-start | bytes 393224 | tf_op jit(solution)/shard_map/ppermute | solution.py:701
  268.1 9.6 %collective-permute-start.39 = (bf16[8,12416]{1,0:T(8,128)(2,1)}, bf16[8,12416]{1,0:T(8,128)(2,1)S(1)}, u32[]{:S(2)}, u32[]{:S(2)}) collective-permute-start(bf16[8,12416]{1,0:T(8,128)(2,1)} %shard_map.221), channel_id=1, source_target_pairs={{0,16},{8,24},{16,0},{24,8},{32,48},{40,56},{48,32},{56,40},{64,80... | collective-permute-start | bytes 595976 | tf_op jit(solution)/shard_map/ppermute | solution.py:769
  270.9 41.1 %all-to-all-start.6 = ((bf16[8,128,1024]{2,1,0:T(8,128)(2,1)}), bf16[8,128,1024]{2,1,0:T(8,128)(2,1)S(1)}, u32[]{:S(2)}, u32[]{:S(2)}) async-start(bf16[8,128,1024]{2,1,0:T(8,128)(2,1)} %bitcast.107), calls=%async_computation.6 | async-start | bytes 4194304 | tf_op jit(solution)/shard_map/all_to_all | solution.py:83
  280.3 18.3 %collective-permute-start.41 = (bf16[16,12416]{1,0:T(8,128)(2,1)}, bf16[16,12416]{1,0:T(8,128)(2,1)S(1)}, u32[]{:S(2)}, u32[]{:S(2)}) collective-permute-start(bf16[16,12416]{1,0:T(8,128)(2,1)} %constant_dynamic-update-slice_fusion.refs_0_), channel_id=1, source_target_pairs={{0,64},{8,72},{16,80},{24,88},{32,96},{40,104},{48,112},{56,120},{... | collective-permute-start | bytes 1191944 | tf_op jit(solution)/shard_map/ppermute | solution.py:88
  281.0 20.7 %collective-permute-start.42 = (bf16[16,12416]{1,0:T(8,128)(2,1)}, bf16[16,12416]{1,0:T(8,128)(2,1)S(1)}, u32[]{:S(2)}, u32[]{:S(2)}) collective-permute-start(bf16[16,12416]{1,0:T(8,128)(2,1)} %constant_dynamic-update-slice_fusion.refs_0_), channel_id=1, source_target_pairs={{0,32},{8,40},{16,48},{24,56},{32,64},{40,72},{48,80},{56,88},{64,... | collective-permute-start | bytes 1191944 | tf_op jit(solution)/shard_map/ppermute | solution.py:88
  281.8 20.3 %collective-permute-start.43 = (bf16[16,12416]{1,0:T(8,128)(2,1)}, bf16[16,12416]{1,0:T(8,128)(2,1)S(1)}, u32[]{:S(2)}, u32[]{:S(2)}) collective-permute-start(bf16[16,12416]{1,0:T(8,128)(2,1)} %constant_dynamic-update-slice_fusion.refs_0_), channel_id=1, source_target_pairs={{0,8},{8,0},{16,24},{24,16},{32,40},{40,32},{48,56},{56,48},{64,72... | collective-permute-start | bytes 1191944 | tf_op jit(solution)/shard_map/ppermute | solution.py:96
  286.8 15.4 %collective-permute-start.44 = (bf16[16,12416]{1,0:T(8,128)(2,1)S(1)}, bf16[16,12416]{1,0:T(8,128)(2,1)S(1)}, u32[]{:S(2)}, u32[]{:S(2)}) collective-permute-start(bf16[16,12416]{1,0:T(8,128)(2,1)S(1)} %collective-permute-done.40.refs_1_), channel_id=1, source_target_pairs={{0,8},{8,0},{16,24},{24,16},{32,40},{40,32},{48,56},{56,48},{64,72... | collective-permute-start | bytes 1191944 | tf_op jit(solution)/shard_map/ppermute | solution.py:96
  (70 other events, 802.2 us)
